TPU v7x, 32 devices: a whole 2x2x4 slice. The times are simulated.
32 devices in a mesh: pair: 8 (over y, x, core), win: 4 (over z).
Axes of the slice: x: 2, y: 2, z: 4, core: 2. Of those that a mesh axis runs over, the one named last changes fastest.
Arguments:
- traces: bfloat16 [2048, 128, 1024], P('pair', 'win'), may hold values from -210 to 210, as said below
- partner: int32 [2, 8], replicated, may hold values from 0 to 7, as said below
- block_ids: int32 [8], replicated, may hold values from 0 to 7, each once
Outputs:
- correlations: float32 [2, 32, 2, 2048, 256], P(None, 'win', None, 'pair')
Inputs may be any that keep to these rules, and one draw needn't show every extreme that they name: traces are noise whose amplitude and spectral colour vary from channel to channel and window to window. Each row of partner pairs every fibre block with one other block: partner[r, partner[r, b]] = b and partner[r, b] != b; the rows are distinct rounds of one round-robin plan. block_ids names each fibre block once.
All inputs are finite; a program needn't handle non-finite values.
Results may differ from a plain program's by a relative error of at most 0.0058.
Values may be sent and summed in bfloat16 or wider, within the bound.
No kernel may reach another device: no remote copies, remote signals or barrier semaphores. Data moves between devices by JAX's collectives and lax.ppermute only.
A program may use at most 128 MiB of HBM per device.

v0:
```python
import math

import jax
import jax.numpy as jnp
from jax import lax
from jax.sharding import PartitionSpec as P

SAMPLES = 1024
BINS = 32
FIRST_BIN = 16
BIN_STEP = 8
ROUNDS = 2


def tapered_table():
    sample = jnp.arange(SAMPLES, dtype=jnp.int32)
    freq = FIRST_BIN + BIN_STEP * jnp.arange(BINS, dtype=jnp.int32)
    phase = sample[:, None] * freq[None, :] % SAMPLES
    angle = 2.0 * math.pi / SAMPLES * phase.astype(jnp.float32)
    taper = 0.5 - 0.5 * jnp.cos(2.0 * math.pi / SAMPLES * sample.astype(jnp.float32))
    real_part = taper[:, None] * jnp.cos(angle)
    imag_part = -taper[:, None] * jnp.sin(angle)
    return jnp.concatenate([real_part, imag_part], axis=1).astype(jnp.bfloat16)


def whitened(trace_rows, dft_table):
    raw = jnp.dot(trace_rows, dft_table, preferred_element_type=jnp.float32)
    power = jnp.mean(raw * raw, axis=-1, keepdims=True)
    return (raw * lax.rsqrt(power + 1e-05)).astype(jnp.bfloat16)


def correlate(local_spec, remote):
    rotated = jnp.concatenate([local_spec[1:2], -local_spec[0:1]], axis=0)
    stacked = jnp.stack([local_spec, rotated], axis=0)
    return jnp.einsum("kcbwi,cbwj->bkij", stacked, remote, preferred_element_type=jnp.float32)


def partner_devices(partner_row, block_ids, slots, holder):
    wanted = jnp.sum(
        jnp.where(block_ids[:, None] == slots[None, :], partner_row[None, :], 0), axis=1
    )
    return jnp.sum(jnp.where(wanted[:, None] == slots[None, :], holder[None, :], 0), axis=1)


def spread_spectra(spectra, pair_count):
    return lax.all_to_all(
        spectra.reshape(pair_count, -1), "pair", split_axis=0, concat_axis=0, tiled=True
    )


def local(traces, partner, block_ids):
    dft_table = tapered_table()
    channels_dev, window_devices, samples = traces.shape
    trace_rows = traces.reshape(channels_dev * window_devices, samples)
    flat_spec = whitened(trace_rows, dft_table)
    pair_count = lax.axis_size("pair")
    win_count = lax.axis_size("win")
    stack_scale = 1.0 / math.sqrt(window_devices * win_count)
    spectra = flat_spec.reshape(channels_dev, window_devices, 2, -1).transpose(2, 3, 1, 0)
    spectra = lax.all_to_all(spectra, "win", split_axis=1, concat_axis=2, tiled=True)
    pieces = spread_spectra(spectra, pair_count)
    spec_shape = spectra.shape
    slots = jnp.arange(pair_count, dtype=jnp.int32)
    holder = jnp.sum(jnp.where(block_ids[None, :] == slots[:, None], slots[None, :], 0), axis=1)
    remotes = []
    outgoing = jnp.stack(
        [
            jnp.take(pieces, partner_devices(partner[round_no], block_ids, slots, holder), axis=0)
            for round_no in range(ROUNDS)
        ],
        axis=0,
    )
    arrived = lax.all_to_all(outgoing, "pair", split_axis=1, concat_axis=1, tiled=True)
    for round_no in range(ROUNDS):
        assemble_arrived = arrived[round_no]
        remotes.append(assemble_arrived.reshape(spec_shape))
    results = []
    for remote in remotes:
        results.append(correlate(spectra, remote) * stack_scale)
    return jnp.stack(results, axis=0)


def solution(mesh):
    placed = (P("pair", "win", None), P(), P())
    return jax.shard_map(
        local,
        mesh=mesh,
        in_specs=placed,
        out_specs=P(None, "win", None, "pair", None),
        check_vma=False,
    )
```

profile of v0, /device:TPU:0, one launch (start us, length us, event | category | flops | bytes accessed | tf_op | source)
XLA Modules:
  0.0 150.1 jit_solution(12708965259652171885)
XLA Ops:
  0.1 0.6 multiply_convert_fusion.2
  0.7 11.0 %multiply_reduce_fusion = (f32[8192]{0:T(1024)S(1)}, f32[64,8192]{1,0:T(8,128)S(1)}) fusion(bf16[8192,1024]{1,0:T(8,128)(2,1)} %bitcast.55, bf16[1024,32]{0,1:T(8,128)(2,1)S(1)} %get-tuple-element.18, bf16[1024,32]{0,1:T(8,128)(2,1)S(1)} %get-tuple-element.17), kind=kOutput, calls=%fused_computation.12 | convolution fusion | flops 1075044352 | bytes 19038208 | tf_op jit(solution)/shard_map/dot_general | solution.py:27
  11.8 4.4 %reshape.63 = bf16[256,32,2,32]{1,0,3,2:T(8,128)(2,1)} reshape(bf16[8192,64]{0,1:T(8,128)(2,1)S(1)} %fusion.2) | data formatting | bytes 2097152 | tf_op jit(solution)/shard_map/reshape | solution.py:59
  16.2 3.5 %copy.58 = bf16[2,32,32,256]{3,2,0,1:T(8,128)(2,1)S(1)} copy(bf16[2,32,32,256]{2,3,1,0:T(8,128)(2,1)} %bitcast.54) | data formatting | bytes 2097152 | tf_op jit(solution)/shard_map/transpose | solution.py:59
  19.7 31.8 %all_to_all.33 = bf16[2,32,32,256]{3,2,0,1:T(8,128)(2,1)S(1)} all-to-all(bf16[2,32,32,256]{3,2,0,1:T(8,128)(2,1)S(1)} %copy.58), channel_id=1, replica_groups=mesh['pair'=8,'win'=4] {'win'}, dimensions={1} | all-to-all | bytes 2097152 | tf_op jit(solution)/shard_map/all_to_all | solution.py:60
  51.5 1.0 copy-done
  52.6 0.5 all_to_all.29
  53.1 0.6 broadcast.119
  53.7 8.1 %reduce.5 = bf16[8,65536]{1,0:T(8,128)(2,1)} reduce(bf16[8,1,65536]{2,1,0:T(2,128)(2,1)S(1)} %all_to_all.29, bf16[]{:T(256)} %broadcast.119), dimensions={1}, to_apply=%all_to_all.29.reduce_sub_computation | reduce | bytes 2097154 | tf_op jit(solution)/shard_map/all_to_all | solution.py:46
  61.7 3.2 %reshape.92 = bf16[8,2,32768]{2,1,0:T(2,128)(2,1)} reshape(bf16[8,65536]{1,0:T(8,128)(2,1)} %reduce.5) | data formatting | bytes 2097152
  64.9 3.8 %all-to-all-start.1 = ((bf16[8,2,32768]{2,1,0:T(2,128)(2,1)}), bf16[8,2,32768]{2,1,0:T(2,128)(2,1)S(1)}, u32[]{:S(2)}, u32[]{:S(2)}) async-start(bf16[8,2,32768]{2,1,0:T(2,128)(2,1)} %reshape.92), calls=%async_computation.1 | async-start | bytes 2097152 | tf_op jit(solution)/shard_map/all_to_all | solution.py:46
  68.9 0.2 select_reduce_fusion.2
  69.2 14.8 %all-to-all-done.1 = bf16[8,2,32768]{2,1,0:T(2,128)(2,1)S(1)} async-done(((bf16[8,2,32768]{2,1,0:T(2,128)(2,1)}), bf16[8,2,32768]{2,1,0:T(2,128)(2,1)S(1)}, u32[]{:S(2)}, u32[]{:S(2)}) %all-to-all-start.1) | async-done | bytes 1048608 | tf_op jit(solution)/shard_map/all_to_all | solution.py:46
  84.1 3.4 %reshape.93 = bf16[8,1,65536]{2,1,0:T(2,128)(2,1)} reshape(bf16[8,2,32768]{2,1,0:T(2,128)(2,1)S(1)} %all-to-all-done.1) | data formatting | bytes 2097152
  87.5 2.7 %copy.87 = bf16[8,1,65536]{2,0,1:T(8,128)(2,1)S(1)} copy(bf16[8,1,65536]{2,1,0:T(2,128)(2,1)} %reshape.93) | data formatting | bytes 2097152
  90.2 1.2 gather_fusion.1
  91.5 2.2 %gather_fusion = bf16[8,65536]{1,0:T(8,128)(2,1)} fusion(bf16[8,65536]{1,0:T(8,128)(2,1)S(1)} %bitcast.53, s32[1024]{0:T(1024)S(1)} %pad_clamp_fusion.1), kind=kCustom, calls=%fused_computation.clone | custom fusion | bytes 2097184 | tf_op jit(solution)/shard_map/jit(_take)/gather | solution.py:68
  93.7 1.4 select_bitcast_fusion.1
  95.4 3.5 %copy.68 = bf16[2,8,65536]{2,0,1:T(2,128)(2,1)} copy(bf16[2,8,65536]{2,1,0:T(8,128)(2,1)S(1)} %pad_maximum_fusion.2) | data formatting | bytes 4194304 | tf_op jit(solution)/shard_map/stack | solution.py:66
  98.9 3.9 %all-to-all-start.2 = ((bf16[2,8,65536]{2,0,1:T(2,128)(2,1)}), bf16[2,8,65536]{2,0,1:T(2,128)(2,1)S(1)}, u32[]{:S(2)}, u32[]{:S(2)}) async-start(bf16[2,8,65536]{2,0,1:T(2,128)(2,1)} %copy.68), calls=%async_computation.2 | async-start | bytes 4194304 | tf_op jit(solution)/shard_map/all_to_all | solution.py:73
  102.8 1.3 copy.65
  104.1 1.3 copy.59
  105.6 1.0 copy.63
  106.6 0.3 copy.64
  106.9 2.1 %maximum_bitcast_fusion = bf16[1,2,8,128,256]{3,4,1,0,2:T(8,128)(2,1)} fusion(bf16[1,8,128,256]{2,3,0,1:T(8,128)(2,1)S(1)} %copy.64, bf16[1,8,128,256]{2,3,0,1:T(8,128)(2,1)} %copy.63), kind=kLoop, calls=%fused_computation.14 | loop fusion | flops 524288 | bytes 2097152 | tf_op jit(solution)/shard_map/stack | solution.py:34
  109.0 20.1 %all-to-all-done.2 = bf16[2,8,65536]{2,0,1:T(2,128)(2,1)S(1)} async-done(((bf16[2,8,65536]{2,0,1:T(2,128)(2,1)}), bf16[2,8,65536]{2,0,1:T(2,128)(2,1)S(1)}, u32[]{:S(2)}, u32[]{:S(2)}) %all-to-all-start.2) | async-done | bytes 2097184 | tf_op jit(solution)/shard_map/all_to_all | solution.py:73
  129.1 10.0 %slice_reduce_fusion.1 = (bf16[8,65536]{1,0:T(8,128)(2,1)}, bf16[8,65536]{1,0:T(8,128)(2,1)S(1)}) fusion(bf16[2,8,65536]{2,0,1:T(2,128)(2,1)S(1)} %all-to-all-done.2), kind=kLoop, calls=%fused_computation.8 | loop fusion | bytes 4194304 | tf_op jit(solution)/shard_map/slice | solution.py:75
  139.1 2.8 %reshape_squeeze.6 = bf16[2,8,128,256]{3,2,1,0:T(8,128)(2,1)} reshape(bf16[8,65536]{1,0:T(8,128)(2,1)} %get-tuple-element.6) | data formatting | bytes 2097152 | tf_op jit(solution)/shard_map/reshape;squeeze | solution.py:76
  142.0 1.4 reshape_squeeze.7
  143.4 2.0 %fusion = f32[1,8,2,256,256]{4,3,2,1,0:T(8,128)S(1)} fusion(bf16[1,2,8,128,256]{3,4,1,0,2:T(8,128)(2,1)S(1)} %copy-done.2, bf16[1,2,8,128,256]{3,4,1,0,2:T(8,128)(2,1)S(1)} %copy-done.1, bf16[2,8,128,256]{3,2,1,0:T(8,128)(2,1)} %reshape_squeeze.7), kind=kOutput, calls=%fused_computation.4 | convolution fusion | flops 538968064 | bytes 7340032 | tf_op jit(solution)/shard_map/kcbwi,cbwj->bkij/dot_general | solution.py:35
  145.5 0.7 fusion.1
  146.2 4.0 %pad_maximum_fusion = f32[2,8,2,256,256]{4,3,2,1,0:T(8,128)} fusion(f32[1,8,2,256,256]{4,3,2,1,0:T(8,128)S(1)} %fusion, f32[1,8,2,256,256]{4,3,2,1,0:T(8,128)S(1)} %fusion.1), kind=kLoop, calls=%fused_computation.2 | loop fusion | flops 2097152 | bytes 16777216 | tf_op jit(solution)/shard_map/stack | solution.py:80
  (27 shorter events, 1.0 us)
Async XLA Ops:
  51.5 1.0 copy-start
  61.7 7.0 %copy-start.5 = (s32[2,8]{1,0:T(2,128)S(1)}, s32[2,8]{1,0:T(2,128)}, u32[]{:S(2)}) copy-start(s32[2,8]{1,0:T(2,128)} %param.6) | copy-start | bytes 196
  61.7 7.0 %copy-start.4 = (s32[8]{0:T(128)S(1)}, s32[8]{0:T(128)}, u32[]{:S(2)}) copy-start(s32[8]{0:T(128)} %param.7) | copy-start | bytes 100
  64.9 19.1 %all-to-all-start.1 = ((bf16[8,2,32768]{2,1,0:T(2,128)(2,1)}), bf16[8,2,32768]{2,1,0:T(2,128)(2,1)S(1)}, u32[]{:S(2)}, u32[]{:S(2)}) async-start(bf16[8,2,32768]{2,1,0:T(2,128)(2,1)} %reshape.92), calls=%async_computation.1 | async-start | bytes 2097152 | tf_op jit(solution)/shard_map/all_to_all | solution.py:46
  98.9 30.2 %all-to-all-start.2 = ((bf16[2,8,65536]{2,0,1:T(2,128)(2,1)}), bf16[2,8,65536]{2,0,1:T(2,128)(2,1)S(1)}, u32[]{:S(2)}, u32[]{:S(2)}) async-start(bf16[2,8,65536]{2,0,1:T(2,128)(2,1)} %copy.68), calls=%async_computation.2 | async-start | bytes 4194304 | tf_op jit(solution)/shard_map/all_to_all | solution.py:73
  139.1 4.3 %copy-start.1 = (bf16[1,2,8,128,256]{3,4,1,0,2:T(8,128)(2,1)S(1)}, bf16[1,2,8,128,256]{3,4,1,0,2:T(8,128)(2,1)}, u32[]{:S(2)}) copy-start(bf16[1,2,8,128,256]{3,4,1,0,2:T(8,128)(2,1)} %copy.65) | copy-start | bytes 3145732
  139.1 4.3 %copy-start.2 = (bf16[1,2,8,128,256]{3,4,1,0,2:T(8,128)(2,1)S(1)}, bf16[1,2,8,128,256]{3,4,1,0,2:T(8,128)(2,1)}, u32[]{:S(2)}) copy-start(bf16[1,2,8,128,256]{3,4,1,0,2:T(8,128)(2,1)} %maximum_bitcast_fusion) | copy-start | bytes 3145732
  143.4 2.0 %copy-start.3 = (bf16[2,8,128,256]{3,2,1,0:T(8,128)(2,1)S(1)}, bf16[2,8,128,256]{3,2,1,0:T(8,128)(2,1)}, u32[]{:S(2)}) copy-start(bf16[2,8,128,256]{3,2,1,0:T(8,128)(2,1)} %reshape_squeeze.6) | copy-start | bytes 3145732
where the time goes:
time: 151 us; the launch traced here: 150 us
  local copies, waits for them, and re-layouts  44.6 us (30%)
  waiting for transfers between devices  34.9 us (23%)
  blocking collectives  31.8 us (21%)
  other arithmetic  17.2 us (11%)
  matrix products  13.7 us (9%)
  starting transfers between devices  7.64 us (5%)
    all_to_all x1, blocking collectives, local(): lax.all_to_all(spectra, 'win', split_axis=1, concat_axis=2, tiled=True)  31.8 us
    all_to_all x1, waiting for transfers between devices, local(): lax.all_to_all(outgoing, 'pair', split_axis=1, concat_axis=1, tiled=True)  20.1 us
    all_to_all x1, waiting for transfers between devices, spread_spectra(): lax.all_to_all(spectra.reshape(pair_count, -1), 'pair', split_axis=0, con...  14.8 us
    dot_general x1, matrix products, whitened(): raw = jnp.dot(trace_rows, dft_table, preferred_element_type=jnp.float32)  11 us
    unnamed x15, local copies, waits for them, and re-layouts  10.3 us
    slice x1, local copies, waits for them, and re-layouts, local(): assemble_arrived = arrived[round_no]  10 us
    all_to_all x1, other arithmetic, spread_spectra(): lax.all_to_all(spectra.reshape(pair_count, -1), 'pair', split_axis=0, con...  8.05 us
    reshape x1, local copies, waits for them, and re-layouts, local(): flat_spec.reshape(channels_dev, window_devices, 2, -1).transpose(2, 3, 1, 0)  4.37 us
  transfers between devices with their start and end apart: 2, of which 2 were waited for; matrix products, arithmetic and copies ran while one was open for 4% of the time, Pallas kernels for 0%

commit v1 on v0

v1 whole, which is shorter than its diff:
```python
import functools
import math

import jax
import jax.numpy as jnp
from jax import lax
from jax.experimental import pallas as pl
from jax.experimental.pallas import tpu as pltpu
from jax.sharding import PartitionSpec as P

SAMPLES = 1024
BINS = 32
FIRST_BIN = 16
BIN_STEP = 8
ROUNDS = 2
LANES = 128
WIN_ROWS = 16
VMEM_BYTES = 40 * 1024 * 1024


def tapered_table(win_count):
    sample = jnp.arange(SAMPLES, dtype=jnp.int32)
    bins_dev = BINS // win_count
    me = lax.axis_index("win")
    owner = me ^ jnp.arange(win_count, dtype=jnp.int32)
    bins = (owner[:, None] * bins_dev + jnp.arange(bins_dev, dtype=jnp.int32)[None, :]).reshape(-1)
    freq = FIRST_BIN + BIN_STEP * bins
    phase = sample[:, None] * freq[None, :] % SAMPLES
    angle = 2.0 * math.pi / SAMPLES * phase.astype(jnp.float32)
    taper = 0.5 - 0.5 * jnp.cos(2.0 * math.pi / SAMPLES * sample.astype(jnp.float32))
    real_part = taper[:, None] * jnp.cos(angle)
    imag_part = -taper[:, None] * jnp.sin(angle)
    both = jnp.stack([real_part, imag_part], axis=2).reshape(SAMPLES, 2 * BINS)
    return both.astype(jnp.bfloat16)


def spectra_kernel(steps, n_out, low_ref, high_ref, table_ref, *rest):
    outs, raw_ref, turned_ref = rest[:n_out], rest[n_out], rest[n_out + 1]
    step = pl.program_id(1)
    rows = low_ref.shape[0] * WIN_ROWS
    low = low_ref[...].reshape(rows, SAMPLES)
    high = high_ref[...].reshape(rows, SAMPLES)
    raw = jnp.dot(low, table_ref[0], preferred_element_type=jnp.float32)
    raw += jnp.dot(high, table_ref[1], preferred_element_type=jnp.float32)
    raw_ref[pl.ds(pl.multiple_of(step * rows, rows), rows), :] = raw

    @pl.when(step == steps - 1)
    def _():
        columns = 2 * BINS
        for w in range(WIN_ROWS):
            turned = raw_ref[pl.ds(w, LANES, stride=WIN_ROWS), :].T
            for half in range(2):
                part = turned[half * columns : (half + 1) * columns]
                power = jnp.mean(part * part, axis=0, keepdims=True)
                first = half * columns * WIN_ROWS + w
                turned_ref[pl.ds(first, columns, stride=WIN_ROWS), :] = part * lax.rsqrt(power + 1e-05)
        per = columns // n_out
        for s in range(n_out):
            for half in range(2):
                first = (half * columns + s * per) * WIN_ROWS
                piece = turned_ref[first : first + per * WIN_ROWS, :].astype(jnp.bfloat16)
                outs[s][:, :, half * LANES : (half + 1) * LANES] = piece.reshape(per, WIN_ROWS, LANES)


def local_spectra(traces, win_count):
    channels, windows, samples = traces.shape
    table = tapered_table(win_count)
    columns = table.shape[1]
    zero = jnp.zeros_like(table)
    tables = jnp.stack([jnp.concatenate([table, zero], 1), jnp.concatenate([zero, table], 1)], 0)
    chan_rows = 16
    steps = channels // 2 // chan_rows
    per = columns // win_count
    block = (chan_rows, WIN_ROWS, samples)
    return pl.pallas_call(
        functools.partial(spectra_kernel, steps, win_count),
        grid=(windows // WIN_ROWS, steps),
        in_specs=[
            pl.BlockSpec(block, lambda w, i: (i, w, 0)),
            pl.BlockSpec(block, lambda w, i: (i + steps, w, 0)),
            pl.BlockSpec((2, samples, 2 * columns), lambda w, i: (0, 0, 0)),
        ],
        out_specs=[pl.BlockSpec((per, WIN_ROWS, channels), lambda w, i: (0, w, 0))] * win_count,
        out_shape=[jax.ShapeDtypeStruct((per, windows, channels), jnp.bfloat16)] * win_count,
        scratch_shapes=[
            pltpu.VMEM((LANES * WIN_ROWS, 2 * columns), jnp.float32),
            pltpu.VMEM((2 * columns * WIN_ROWS, LANES), jnp.float32),
        ],
        compiler_params=pltpu.CompilerParams(vmem_limit_bytes=VMEM_BYTES),
        name="spectra",
    )(traces, traces, tables)


def correlate_kernel(scale, n_chunks, *refs):
    locals_, remotes, out_ref = refs[:n_chunks], refs[n_chunks : 2 * n_chunks], refs[2 * n_chunks]
    bin_no, round_no = pl.program_id(0), pl.program_id(1)
    windows, channels = locals_[0].shape[1:]
    left, right, turned = [], [], []
    for s in range(n_chunks):
        left += [locals_[s][2 * bin_no], locals_[s][2 * bin_no + 1]]
        real, imag = remotes[s][round_no, 2 * bin_no], remotes[s][round_no, 2 * bin_no + 1]
        right += [real, imag]
        turned += [-imag, real]
    left = jnp.concatenate(left, axis=0)
    contract = (((0,), (0,)), ((), ()))
    for part, rows in enumerate((right, turned)):
        product = lax.dot_general(
            left, jnp.concatenate(rows, axis=0), contract, preferred_element_type=jnp.float32
        )
        out_ref[0, 0, part] = product * scale


def correlate(own, remotes, windows):
    n_chunks = len(own)
    channels = own[0].shape[-1]
    bins_dev = own[0].shape[0] // 2
    whole = pl.BlockSpec(memory_space=pltpu.VMEM)
    return pl.pallas_call(
        functools.partial(correlate_kernel, 1.0 / math.sqrt(windows), n_chunks),
        grid=(bins_dev, ROUNDS),
        in_specs=[whole] * (2 * n_chunks),
        out_specs=pl.BlockSpec((1, 1, 2, channels, channels), lambda b, r: (r, b, 0, 0, 0)),
        out_shape=jax.ShapeDtypeStruct((ROUNDS, bins_dev, 2, channels, channels), jnp.float32),
        compiler_params=pltpu.CompilerParams(vmem_limit_bytes=VMEM_BYTES),
        name="cross_spectra",
    )(*own, *remotes)


def partner_positions(partner, block_ids, count):
    slots = jnp.arange(count, dtype=jnp.int32)
    holder = jnp.sum(jnp.where(block_ids[None, :] == slots[:, None], slots[None, :], 0), axis=1)
    at_block = block_ids[:, None] == slots[None, :]
    wanted = jnp.sum(jnp.where(at_block[None], partner[:, None, :], 0), axis=2)
    return jnp.sum(jnp.where(wanted[:, :, None] == slots, holder, 0), axis=2)


def swap(value, axis, distance):
    count = lax.axis_size(axis)
    return lax.ppermute(value, axis, [(i, i ^ distance) for i in range(count)])


def gather_even(piece, pair_count):
    half = piece.shape[0] // 2
    found = {0: (piece[:half], piece[half:])}
    for distance in range(2, pair_count, 2):
        if distance != 6:
            whole = swap(piece, "pair", distance)
            found[distance] = (whole[:half], whole[half:])
    if 6 < pair_count:
        found[6] = (swap(found[4][0], "pair", 2), swap(found[2][1], "pair", 4))
    return found


def pick(found, distance):
    halves = []
    for part in range(2):
        items = sorted(found.items())
        value = items[-1][1][part]
        for at, pieces in items[:-1]:
            value = jnp.where(distance == at, pieces[part], value)
        halves.append(value)
    return jnp.concatenate(halves, axis=0)


def local(traces, partner, block_ids):
    pair_count = lax.axis_size("pair")
    win_count = lax.axis_size("win")
    windows_dev = traces.shape[1]
    me = lax.axis_index("pair")
    slots = jnp.arange(pair_count, dtype=jnp.int32)
    paired = partner_positions(partner, block_ids, pair_count)
    mine = jnp.sum(jnp.where(slots == me, paired, 0), axis=1) ^ me
    beside = jnp.sum(jnp.where(slots == (me ^ 1), paired, 0), axis=1) ^ me
    sent = local_spectra(traces, win_count)
    own = [sent[0]] + [swap(sent[s], "win", s) for s in range(1, win_count)]
    remotes = []
    for piece in own:
        found = gather_even(piece, pair_count)
        outgoing = jnp.stack([pick(found, beside[r]) for r in range(ROUNDS)], axis=0)
        arrived = swap(outgoing, "pair", 1)
        remotes.append(
            jnp.stack(
                [
                    jnp.where(mine[r] % 2 == 1, arrived[r], pick(found, mine[r]))
                    for r in range(ROUNDS)
                ],
                axis=0,
            )
        )
    return correlate(own, remotes, windows_dev * win_count)


def solution(mesh):
    placed = (P("pair", "win", None), P(), P())
    return jax.shard_map(
        local,
        mesh=mesh,
        in_specs=placed,
        out_specs=P(None, "win", None, "pair", None),
        check_vma=False,
    )
```

time: 151 us -> 84.9 us (0.56)
  local copies, waits for them, and re-layouts: 44.6 us -> 1.92 us
  blocking collectives: 31.8 us -> 0 us
  Pallas kernels: 0 us -> 24.7 us
  starting transfers between devices: 7.64 us -> 22.2 us
  waiting for transfers between devices: 34.9 us -> 20.6 us
  other arithmetic: 17.2 us -> 3.04 us
  matrix products: 13.7 us -> 0 us
  between operations: 0.22 us -> 11.9 us
    all_to_all x2 -> x0, waiting for transfers between devices: 34.9 us -> none  [the longest x1 20.1 us: local(): lax.all_to_all(outgoing, 'pair', split_axis=1, concat_axis=1, tiled=True)]
    all_to_all x1 -> x0, blocking collectives: 31.8 us -> none  [local(): lax.all_to_all(spectra, 'win', split_axis=1, concat_axis=2, tiled=True)]
    pallas_call x0 -> x2, Pallas kernels: none -> 24.7 us  [the longest x1 16 us: local_spectra(): pl.pallas_call(functools.partial(spectra_kernel, steps, win_count), grid=...]
    ppermute x0 -> x23, starting transfers between devices: none -> 22.2 us  [swap(): return lax.ppermute(value, axis, [(i, i ^ distance) for i in range(count)])]
    ppermute x0 -> x23, waiting for transfers between devices: none -> 20.6 us  [swap(): return lax.ppermute(value, axis, [(i, i ^ distance) for i in range(count)])]
    dot_general x3 -> x0, matrix products: 13.7 us -> none  [the longest x1 11 us: whitened(): raw = jnp.dot(trace_rows, dft_table, preferred_element_type=jnp.float32)]
    unnamed x15 -> x4, local copies, waits for them, and re-layouts: 10.3 us -> 0.01 us
    slice x3 -> x10, local copies, waits for them, and re-layouts: 11.1 us -> 1.31 us  [the longest x1 0.64 us: local(): mine[r] % 2 == 1]
  transfers between devices with their start and end apart: 2 -> 23, of which waited for: 2 -> 9; matrix products, arithmetic and copies ran while one was open for 4% -> 4% of each run, Pallas kernels for 0% -> 0%
where the time goes in v1:
time: 84.9 us; the launch traced here: 84.4 us
  Pallas kernels  24.7 us (29%)
  starting transfers between devices  22.2 us (26%)
  waiting for transfers between devices  20.6 us (24%)
  between operations  11.9 us (14%)
  other arithmetic  3.04 us (4%)
  local copies, waits for them, and re-layouts  1.92 us (2%)
    ppermute x23, starting transfers between devices, swap(): return lax.ppermute(value, axis, [(i, i ^ distance) for i in range(count)])  22.2 us
    ppermute x23, waiting for transfers between devices, swap(): return lax.ppermute(value, axis, [(i, i ^ distance) for i in range(count)])  20.6 us
    pallas_call x1, Pallas kernels, local_spectra(): pl.pallas_call(functools.partial(spectra_kernel, steps, win_count), grid=...  16 us
    pallas_call x1, Pallas kernels, correlate(): pl.pallas_call(functools.partial(correlate_kernel, 1.0 / math.sqrt(window...  8.66 us
  transfers between devices with their start and end apart: 23, of which 9 were waited for; matrix products, arithmetic and copies ran while one was open for 4% of the time, Pallas kernels for 0%

profile of v1, /device:TPU:0, one launch (start us, length us, event | category | flops | bytes accessed | tf_op | source)
XLA Modules:
  0.0 84.4 jit_solution(4849139009672262614)
XLA Ops:
  0.2 0.6 multiply_convert_fusion.1
  1.5 16.0 %spectra.1 = (bf16[16,32,256]{2,1,0:T(8,128)(2,1)S(1)}, bf16[16,32,256]{2,1,0:T(8,128)(2,1)S(1)}, bf16[16,32,256]{2,1,0:T(8,128)(2,1)S(1)}, bf16[16,32,256]{2,1,0:T(8,128)(2,1)S(1)}) custom-call(bf16[256,32,1024]{2,1,0:T(8,128)(2,1)} %high_ref.1, bf16[256,32,1024]{2,1,0:T(8,128)(2,1)} %high_ref.1, bf16[2,1024,128]{2,1,0:T(8,128)(2,1)S(1)} %pad_maximum_fusion.table_ref), custom_call_target="tpu_custom_call" | custom-call | tf_op jit(solution)/shard_map/spectra/pallas_call | solution.py:75
  17.5 3.0 %collective-permute-start.4 = (bf16[16,32,256]{2,1,0:T(8,128)(2,1)S(1)}, bf16[16,32,256]{2,1,0:T(8,128)(2,1)S(1)}, u32[]{:S(2)}, u32[]{:S(2)}) collective-permute-start(bf16[16,32,256]{2,1,0:T(8,128)(2,1)S(1)} %get-tuple-element.9.refs_0_), channel_id=1, source_target_pairs={{0,8},{4,12},{8,0},{12,4},{16,24},{20,28},{24,16},{28,20},{1,9},{5... | collective-permute-start | bytes 786440 | tf_op jit(solution)/shard_map/ppermute | solution.py:139
  20.5 1.5 %collective-permute-start.3 = (bf16[16,32,256]{2,1,0:T(8,128)(2,1)S(1)}, bf16[16,32,256]{2,1,0:T(8,128)(2,1)S(1)}, u32[]{:S(2)}, u32[]{:S(2)}) collective-permute-start(bf16[16,32,256]{2,1,0:T(8,128)(2,1)S(1)} %get-tuple-element.9.refs_0_), channel_id=1, source_target_pairs={{0,16},{4,20},{8,24},{12,28},{16,0},{20,4},{24,8},{28,12},{1,17},{... | collective-permute-start | bytes 786440 | tf_op jit(solution)/shard_map/ppermute | solution.py:139
  22.0 1.6 %collective-permute-start = (bf16[16,32,256]{2,1,0:T(8,128)(2,1)S(1)}, bf16[16,32,256]{2,1,0:T(8,128)(2,1)S(1)}, u32[]{:S(2)}, u32[]{:S(2)}) collective-permute-start(bf16[16,32,256]{2,1,0:T(8,128)(2,1)S(1)} %get-tuple-element.10), channel_id=1, source_target_pairs={{0,1},{1,0},{2,3},{3,2},{4,5},{5,4},{6,7},{7,6},{8,9},{9,8},{10,11... | collective-permute-start | bytes 786440 | tf_op jit(solution)/shard_map/ppermute | solution.py:139
  23.6 2.6 %collective-permute-start.1 = (bf16[16,32,256]{2,1,0:T(8,128)(2,1)S(1)}, bf16[16,32,256]{2,1,0:T(8,128)(2,1)S(1)}, u32[]{:S(2)}, u32[]{:S(2)}) collective-permute-start(bf16[16,32,256]{2,1,0:T(8,128)(2,1)S(1)} %get-tuple-element.11), channel_id=1, source_target_pairs={{0,2},{1,3},{2,0},{3,1},{4,6},{5,7},{6,4},{7,5},{8,10},{9,11},{10,... | collective-permute-start | bytes 786440 | tf_op jit(solution)/shard_map/ppermute | solution.py:139
  27.2 1.5 %collective-permute-start.6 = (bf16[8,32,256]{2,1,0:T(8,128)(2,1)S(1)}, bf16[8,32,256]{2,1,0:T(8,128)(2,1)S(1)}, u32[]{:S(2)}, u32[]{:S(2)}) collective-permute-start(bf16[8,32,256]{2,1,0:T(8,128)(2,1)S(1)} %slice.167), channel_id=1, source_target_pairs={{0,16},{4,20},{8,24},{12,28},{16,0},{20,4},{24,8},{28,12},{1,17},{... | collective-permute-start | bytes 393224 | tf_op jit(solution)/shard_map/ppermute | solution.py:139
  28.7 1.6 %collective-permute-start.5 = (bf16[8,32,256]{2,1,0:T(8,128)(2,1)S(1)}, bf16[8,32,256]{2,1,0:T(8,128)(2,1)S(1)}, u32[]{:S(2)}, u32[]{:S(2)}) collective-permute-start(bf16[8,32,256]{2,1,0:T(8,128)(2,1)S(1)} %slice.164), channel_id=1, source_target_pairs={{0,8},{4,12},{8,0},{12,4},{16,24},{20,28},{24,16},{28,20},{1,9},{5... | collective-permute-start | bytes 393224 | tf_op jit(solution)/shard_map/ppermute | solution.py:139
  30.2 0.6 fusion.8
  34.6 0.6 fusion.7
  42.9 0.6 collective-permute-start.9
  43.5 1.5 %collective-permute-done.1.refs_2_ = bf16[16,32,256]{2,1,0:T(8,128)(2,1)S(1)} collective-permute-done((bf16[16,32,256]{2,1,0:T(8,128)(2,1)S(1)}, bf16[16,32,256]{2,1,0:T(8,128)(2,1)S(1)}, u32[]{:S(2)}, u32[]{:S(2)}) %collective-permute-start.1) | collective-permute-done | bytes 262176 | tf_op jit(solution)/shard_map/ppermute | solution.py:139
  45.0 0.5 collective-permute-start.8
  45.5 0.5 collective-permute-start.19
  46.0 1.5 %collective-permute-start.18 = (bf16[16,32,256]{2,1,0:T(8,128)(2,1)S(1)}, bf16[16,32,256]{2,1,0:T(8,128)(2,1)S(1)}, u32[]{:S(2)}, u32[]{:S(2)}) collective-permute-start(bf16[16,32,256]{2,1,0:T(8,128)(2,1)S(1)} %collective-permute-done.2.refs_3_), channel_id=1, source_target_pairs={{0,16},{4,20},{8,24},{12,28},{16,0},{20,4},{24,8},{28,12},{1,17},{... | collective-permute-start | bytes 786440 | tf_op jit(solution)/shard_map/ppermute | solution.py:139
  47.6 1.5 %collective-permute-start.14 = (bf16[16,32,256]{2,1,0:T(8,128)(2,1)S(1)}, bf16[16,32,256]{2,1,0:T(8,128)(2,1)S(1)}, u32[]{:S(2)}, u32[]{:S(2)}) collective-permute-start(bf16[16,32,256]{2,1,0:T(8,128)(2,1)S(1)} %collective-permute-done.1.refs_2_), channel_id=1, source_target_pairs={{0,8},{4,12},{8,0},{12,4},{16,24},{20,28},{24,16},{28,20},{1,9},{5... | collective-permute-start | bytes 786440 | tf_op jit(solution)/shard_map/ppermute | solution.py:139
  49.2 8.6 %collective-permute-done.19 = bf16[16,32,256]{2,1,0:T(8,128)(2,1)S(1)} collective-permute-done((bf16[16,32,256]{2,1,0:T(8,128)(2,1)S(1)}, bf16[16,32,256]{2,1,0:T(8,128)(2,1)S(1)}, u32[]{:S(2)}, u32[]{:S(2)}) %collective-permute-start.19) | collective-permute-done | bytes 262176 | tf_op jit(solution)/shard_map/ppermute | solution.py:139
  57.9 0.5 collective-permute-start.13
  58.4 1.6 %collective-permute-start.21 = (bf16[8,32,256]{2,1,0:T(8,128)(2,1)S(1)}, bf16[8,32,256]{2,1,0:T(8,128)(2,1)S(1)}, u32[]{:S(2)}, u32[]{:S(2)}) collective-permute-start(bf16[8,32,256]{2,1,0:T(8,128)(2,1)S(1)} %slice.190), channel_id=1, source_target_pairs={{0,16},{4,20},{8,24},{12,28},{16,0},{20,4},{24,8},{28,12},{1,17},{... | collective-permute-start | bytes 393224 | tf_op jit(solution)/shard_map/ppermute | solution.py:139
  60.0 0.6 collective-permute-start.20
  60.8 1.4 %collective-permute-done.14 = bf16[16,32,256]{2,1,0:T(8,128)(2,1)S(1)} collective-permute-done((bf16[16,32,256]{2,1,0:T(8,128)(2,1)S(1)}, bf16[16,32,256]{2,1,0:T(8,128)(2,1)S(1)}, u32[]{:S(2)}, u32[]{:S(2)}) %collective-permute-start.14) | collective-permute-done | bytes 262176 | tf_op jit(solution)/shard_map/ppermute | solution.py:139
  62.2 0.5 collective-permute-start.11
  62.8 1.6 %collective-permute-done.13 = bf16[16,32,256]{2,1,0:T(8,128)(2,1)S(1)} collective-permute-done((bf16[16,32,256]{2,1,0:T(8,128)(2,1)S(1)}, bf16[16,32,256]{2,1,0:T(8,128)(2,1)S(1)}, u32[]{:S(2)}, u32[]{:S(2)}) %collective-permute-start.13) | collective-permute-done | bytes 262176 | tf_op jit(solution)/shard_map/ppermute | solution.py:139
  64.4 0.4 collective-permute-start.10
  64.8 2.4 %collective-permute-done.21 = bf16[8,32,256]{2,1,0:T(8,128)(2,1)S(1)} collective-permute-done((bf16[8,32,256]{2,1,0:T(8,128)(2,1)S(1)}, bf16[8,32,256]{2,1,0:T(8,128)(2,1)S(1)}, u32[]{:S(2)}, u32[]{:S(2)}) %collective-permute-start.21) | collective-permute-done | bytes 131104 | tf_op jit(solution)/shard_map/ppermute | solution.py:139
  67.2 1.3 %collective-permute-start.15 = (bf16[8,32,256]{2,1,0:T(8,128)(2,1)S(1)}, bf16[8,32,256]{2,1,0:T(8,128)(2,1)S(1)}, u32[]{:S(2)}, u32[]{:S(2)}) collective-permute-start(bf16[8,32,256]{2,1,0:T(8,128)(2,1)S(1)} %slice.178), channel_id=1, source_target_pairs={{0,8},{4,12},{8,0},{12,4},{16,24},{20,28},{24,16},{28,20},{1,9},{5... | collective-permute-start | bytes 393224 | tf_op jit(solution)/shard_map/ppermute | solution.py:139
  68.8 3.3 %collective-permute-done.16 = bf16[8,32,256]{2,1,0:T(8,128)(2,1)S(1)} collective-permute-done((bf16[8,32,256]{2,1,0:T(8,128)(2,1)S(1)}, bf16[8,32,256]{2,1,0:T(8,128)(2,1)S(1)}, u32[]{:S(2)}, u32[]{:S(2)}) %collective-permute-start.16) | collective-permute-done | bytes 131104 | tf_op jit(solution)/shard_map/ppermute | solution.py:139
  72.5 0.6 collective-permute-start.17
  73.6 0.5 collective-permute-done.22
  74.2 0.6 collective-permute-done.17
  74.9 0.6 collective-permute-done.12
  75.7 8.7 %cross_spectra.1 = f32[2,8,2,256,256]{4,3,2,1,0:T(8,128)} custom-call(bf16[16,32,256]{2,1,0:T(8,128)(2,1)S(1)} %get-tuple-element.9.refs_0_, bf16[16,32,256]{2,1,0:T(8,128)(2,1)S(1)} %collective-permute-done.refs_1_, bf16[16,32,256]{2,1,0:T(8,128)(2,1)S(1)} %collective-permute-done.1.refs_2_, bf16[16,32,256]{2,1,0:T(8,128)(2,1)S(1)} %collective-permute-done.2.refs_3_, ...), custom_call_target="tpu_custom_call" | custom-call | tf_op jit(solution)/shard_map/cross_spectra/pallas_call | solution.py:118
  (81 shorter events, 3.6 us)
Async XLA Ops:
  1.5 25.0 %copy-start.1 = (s32[8]{0:T(128)S(1)}, s32[8]{0:T(128)}, u32[]{:S(2)}) copy-start(s32[8]{0:T(128)} %param.5) | copy-start | bytes 100
  1.5 25.2 %copy-start = (s32[2,8]{1,0:T(2,128)S(1)}, s32[2,8]{1,0:T(2,128)}, u32[]{:S(2)}) copy-start(s32[2,8]{1,0:T(2,128)} %param.4) | copy-start | bytes 196
  17.5 9.7 %collective-permute-start.4 = (bf16[16,32,256]{2,1,0:T(8,128)(2,1)S(1)}, bf16[16,32,256]{2,1,0:T(8,128)(2,1)S(1)}, u32[]{:S(2)}, u32[]{:S(2)}) collective-permute-start(bf16[16,32,256]{2,1,0:T(8,128)(2,1)S(1)} %get-tuple-element.9.refs_0_), channel_id=1, source_target_pairs={{0,8},{4,12},{8,0},{12,4},{16,24},{20,28},{24,16},{28,20},{1,9},{5... | collective-permute-start | bytes 786440 | tf_op jit(solution)/shard_map/ppermute | solution.py:139
  20.5 8.2 %collective-permute-start.3 = (bf16[16,32,256]{2,1,0:T(8,128)(2,1)S(1)}, bf16[16,32,256]{2,1,0:T(8,128)(2,1)S(1)}, u32[]{:S(2)}, u32[]{:S(2)}) collective-permute-start(bf16[16,32,256]{2,1,0:T(8,128)(2,1)S(1)} %get-tuple-element.9.refs_0_), channel_id=1, source_target_pairs={{0,16},{4,20},{8,24},{12,28},{16,0},{20,4},{24,8},{28,12},{1,17},{... | collective-permute-start | bytes 786440 | tf_op jit(solution)/shard_map/ppermute | solution.py:139
  22.0 20.9 %collective-permute-start = (bf16[16,32,256]{2,1,0:T(8,128)(2,1)S(1)}, bf16[16,32,256]{2,1,0:T(8,128)(2,1)S(1)}, u32[]{:S(2)}, u32[]{:S(2)}) collective-permute-start(bf16[16,32,256]{2,1,0:T(8,128)(2,1)S(1)} %get-tuple-element.10), channel_id=1, source_target_pairs={{0,1},{1,0},{2,3},{3,2},{4,5},{5,4},{6,7},{7,6},{8,9},{9,8},{10,11... | collective-permute-start | bytes 786440 | tf_op jit(solution)/shard_map/ppermute | solution.py:139
  23.6 21.4 %collective-permute-start.1 = (bf16[16,32,256]{2,1,0:T(8,128)(2,1)S(1)}, bf16[16,32,256]{2,1,0:T(8,128)(2,1)S(1)}, u32[]{:S(2)}, u32[]{:S(2)}) collective-permute-start(bf16[16,32,256]{2,1,0:T(8,128)(2,1)S(1)} %get-tuple-element.11), channel_id=1, source_target_pairs={{0,2},{1,3},{2,0},{3,1},{4,6},{5,7},{6,4},{7,5},{8,10},{9,11},{10,... | collective-permute-start | bytes 786440 | tf_op jit(solution)/shard_map/ppermute | solution.py:139
  26.2 19.3 %collective-permute-start.2 = (bf16[16,32,256]{2,1,0:T(8,128)(2,1)S(1)}, bf16[16,32,256]{2,1,0:T(8,128)(2,1)S(1)}, u32[]{:S(2)}, u32[]{:S(2)}) collective-permute-start(bf16[16,32,256]{2,1,0:T(8,128)(2,1)S(1)} %get-tuple-element.12), channel_id=1, source_target_pairs={{0,3},{1,2},{2,1},{3,0},{4,7},{5,6},{6,5},{7,4},{8,11},{9,10},{10,... | collective-permute-start | bytes 786440 | tf_op jit(solution)/shard_map/ppermute | solution.py:139
  27.2 18.8 %collective-permute-start.6 = (bf16[8,32,256]{2,1,0:T(8,128)(2,1)S(1)}, bf16[8,32,256]{2,1,0:T(8,128)(2,1)S(1)}, u32[]{:S(2)}, u32[]{:S(2)}) collective-permute-start(bf16[8,32,256]{2,1,0:T(8,128)(2,1)S(1)} %slice.167), channel_id=1, source_target_pairs={{0,16},{4,20},{8,24},{12,28},{16,0},{20,4},{24,8},{28,12},{1,17},{... | collective-permute-start | bytes 393224 | tf_op jit(solution)/shard_map/ppermute | solution.py:139
  28.7 18.9 %collective-permute-start.5 = (bf16[8,32,256]{2,1,0:T(8,128)(2,1)S(1)}, bf16[8,32,256]{2,1,0:T(8,128)(2,1)S(1)}, u32[]{:S(2)}, u32[]{:S(2)}) collective-permute-start(bf16[8,32,256]{2,1,0:T(8,128)(2,1)S(1)} %slice.164), channel_id=1, source_target_pairs={{0,8},{4,12},{8,0},{12,4},{16,24},{20,28},{24,16},{28,20},{1,9},{5... | collective-permute-start | bytes 393224 | tf_op jit(solution)/shard_map/ppermute | solution.py:139
  42.9 17.1 %collective-permute-start.9 = (bf16[16,32,256]{2,1,0:T(8,128)(2,1)S(1)}, bf16[16,32,256]{2,1,0:T(8,128)(2,1)S(1)}, u32[]{:S(2)}, u32[]{:S(2)}) collective-permute-start(bf16[16,32,256]{2,1,0:T(8,128)(2,1)S(1)} %collective-permute-done.refs_1_), channel_id=1, source_target_pairs={{0,8},{4,12},{8,0},{12,4},{16,24},{20,28},{24,16},{28,20},{1,9},{5... | collective-permute-start | bytes 786440 | tf_op jit(solution)/shard_map/ppermute | solution.py:139
  45.0 15.7 %collective-permute-start.8 = (bf16[16,32,256]{2,1,0:T(8,128)(2,1)S(1)}, bf16[16,32,256]{2,1,0:T(8,128)(2,1)S(1)}, u32[]{:S(2)}, u32[]{:S(2)}) collective-permute-start(bf16[16,32,256]{2,1,0:T(8,128)(2,1)S(1)} %collective-permute-done.refs_1_), channel_id=1, source_target_pairs={{0,16},{4,20},{8,24},{12,28},{16,0},{20,4},{24,8},{28,12},{1,17},{... | collective-permute-start | bytes 786440 | tf_op jit(solution)/shard_map/ppermute | solution.py:139
  45.5 12.4 %collective-permute-start.19 = (bf16[16,32,256]{2,1,0:T(8,128)(2,1)S(1)}, bf16[16,32,256]{2,1,0:T(8,128)(2,1)S(1)}, u32[]{:S(2)}, u32[]{:S(2)}) collective-permute-start(bf16[16,32,256]{2,1,0:T(8,128)(2,1)S(1)} %collective-permute-done.2.refs_3_), channel_id=1, source_target_pairs={{0,8},{4,12},{8,0},{12,4},{16,24},{20,28},{24,16},{28,20},{1,9},{5... | collective-permute-start | bytes 786440 | tf_op jit(solution)/shard_map/ppermute | solution.py:139
  46.0 12.4 %collective-permute-start.18 = (bf16[16,32,256]{2,1,0:T(8,128)(2,1)S(1)}, bf16[16,32,256]{2,1,0:T(8,128)(2,1)S(1)}, u32[]{:S(2)}, u32[]{:S(2)}) collective-permute-start(bf16[16,32,256]{2,1,0:T(8,128)(2,1)S(1)} %collective-permute-done.2.refs_3_), channel_id=1, source_target_pairs={{0,16},{4,20},{8,24},{12,28},{16,0},{20,4},{24,8},{28,12},{1,17},{... | collective-permute-start | bytes 786440 | tf_op jit(solution)/shard_map/ppermute | solution.py:139
  47.6 14.7 %collective-permute-start.14 = (bf16[16,32,256]{2,1,0:T(8,128)(2,1)S(1)}, bf16[16,32,256]{2,1,0:T(8,128)(2,1)S(1)}, u32[]{:S(2)}, u32[]{:S(2)}) collective-permute-start(bf16[16,32,256]{2,1,0:T(8,128)(2,1)S(1)} %collective-permute-done.1.refs_2_), channel_id=1, source_target_pairs={{0,8},{4,12},{8,0},{12,4},{16,24},{20,28},{24,16},{28,20},{1,9},{5... | collective-permute-start | bytes 786440 | tf_op jit(solution)/shard_map/ppermute | solution.py:139
  57.9 6.5 %collective-permute-start.13 = (bf16[16,32,256]{2,1,0:T(8,128)(2,1)S(1)}, bf16[16,32,256]{2,1,0:T(8,128)(2,1)S(1)}, u32[]{:S(2)}, u32[]{:S(2)}) collective-permute-start(bf16[16,32,256]{2,1,0:T(8,128)(2,1)S(1)} %collective-permute-done.1.refs_2_), channel_id=1, source_target_pairs={{0,16},{4,20},{8,24},{12,28},{16,0},{20,4},{24,8},{28,12},{1,17},{... | collective-permute-start | bytes 786440 | tf_op jit(solution)/shard_map/ppermute | solution.py:139
  58.4 8.8 %collective-permute-start.21 = (bf16[8,32,256]{2,1,0:T(8,128)(2,1)S(1)}, bf16[8,32,256]{2,1,0:T(8,128)(2,1)S(1)}, u32[]{:S(2)}, u32[]{:S(2)}) collective-permute-start(bf16[8,32,256]{2,1,0:T(8,128)(2,1)S(1)} %slice.190), channel_id=1, source_target_pairs={{0,16},{4,20},{8,24},{12,28},{16,0},{20,4},{24,8},{28,12},{1,17},{... | collective-permute-start | bytes 393224 | tf_op jit(solution)/shard_map/ppermute | solution.py:139
  60.0 7.2 %collective-permute-start.20 = (bf16[8,32,256]{2,1,0:T(8,128)(2,1)S(1)}, bf16[8,32,256]{2,1,0:T(8,128)(2,1)S(1)}, u32[]{:S(2)}, u32[]{:S(2)}) collective-permute-start(bf16[8,32,256]{2,1,0:T(8,128)(2,1)S(1)} %slice.186), channel_id=1, source_target_pairs={{0,8},{4,12},{8,0},{12,4},{16,24},{20,28},{24,16},{28,20},{1,9},{5... | collective-permute-start | bytes 393224 | tf_op jit(solution)/shard_map/ppermute | solution.py:139
  60.7 12.7 %collective-permute-start.7 = (bf16[2,16,32,256]{3,2,1,0:T(8,128)(2,1)S(1)}, bf16[2,16,32,256]{3,2,1,0:T(8,128)(2,1)S(1)}, u32[]{:S(2)}, u32[]{:S(2)}) collective-permute-start(bf16[2,16,32,256]{3,2,1,0:T(8,128)(2,1)S(1)} %pad_maximum_fusion.1), channel_id=1, source_target_pairs={{0,4},{4,0},{8,12},{12,8},{16,20},{20,16},{24,28},{28,24},{1,5},{5... | collective-permute-start | bytes 1572872 | tf_op jit(solution)/shard_map/ppermute | solution.py:139
  62.2 10.8 %collective-permute-start.11 = (bf16[8,32,256]{2,1,0:T(8,128)(2,1)S(1)}, bf16[8,32,256]{2,1,0:T(8,128)(2,1)S(1)}, u32[]{:S(2)}, u32[]{:S(2)}) collective-permute-start(bf16[8,32,256]{2,1,0:T(8,128)(2,1)S(1)} %slice.174), channel_id=1, source_target_pairs={{0,16},{4,20},{8,24},{12,28},{16,0},{20,4},{24,8},{28,12},{1,17},{... | collective-permute-start | bytes 393224 | tf_op jit(solution)/shard_map/ppermute | solution.py:139
  64.4 8.7 %collective-permute-start.10 = (bf16[8,32,256]{2,1,0:T(8,128)(2,1)S(1)}, bf16[8,32,256]{2,1,0:T(8,128)(2,1)S(1)}, u32[]{:S(2)}, u32[]{:S(2)}) collective-permute-start(bf16[8,32,256]{2,1,0:T(8,128)(2,1)S(1)} %slice.170), channel_id=1, source_target_pairs={{0,8},{4,12},{8,0},{12,4},{16,24},{20,28},{24,16},{28,20},{1,9},{5... | collective-permute-start | bytes 393224 | tf_op jit(solution)/shard_map/ppermute | solution.py:139
  67.2 5.0 %collective-permute-start.16 = (bf16[8,32,256]{2,1,0:T(8,128)(2,1)S(1)}, bf16[8,32,256]{2,1,0:T(8,128)(2,1)S(1)}, u32[]{:S(2)}, u32[]{:S(2)}) collective-permute-start(bf16[8,32,256]{2,1,0:T(8,128)(2,1)S(1)} %slice.182), channel_id=1, source_target_pairs={{0,16},{4,20},{8,24},{12,28},{16,0},{20,4},{24,8},{28,12},{1,17},{... | collective-permute-start | bytes 393224 | tf_op jit(solution)/shard_map/ppermute | solution.py:139
  67.2 5.0 %collective-permute-start.15 = (bf16[8,32,256]{2,1,0:T(8,128)(2,1)S(1)}, bf16[8,32,256]{2,1,0:T(8,128)(2,1)S(1)}, u32[]{:S(2)}, u32[]{:S(2)}) collective-permute-start(bf16[8,32,256]{2,1,0:T(8,128)(2,1)S(1)} %slice.178), channel_id=1, source_target_pairs={{0,8},{4,12},{8,0},{12,4},{16,24},{20,28},{24,16},{28,20},{1,9},{5... | collective-permute-start | bytes 393224 | tf_op jit(solution)/shard_map/ppermute | solution.py:139
  72.2 1.9 %collective-permute-start.22 = (bf16[2,16,32,256]{3,2,1,0:T(8,128)(2,1)S(1)}, bf16[2,16,32,256]{3,2,1,0:T(8,128)(2,1)S(1)}, u32[]{:S(2)}, u32[]{:S(2)}) collective-permute-start(bf16[2,16,32,256]{3,2,1,0:T(8,128)(2,1)S(1)} %pad_maximum_fusion.7), channel_id=1, source_target_pairs={{0,4},{4,0},{8,12},{12,8},{16,20},{20,16},{24,28},{28,24},{1,5},{5... | collective-permute-start | bytes 1572872 | tf_op jit(solution)/shard_map/ppermute | solution.py:139
  72.5 2.3 %collective-permute-start.17 = (bf16[2,16,32,256]{3,2,1,0:T(8,128)(2,1)S(1)}, bf16[2,16,32,256]{3,2,1,0:T(8,128)(2,1)S(1)}, u32[]{:S(2)}, u32[]{:S(2)}) collective-permute-start(bf16[2,16,32,256]{3,2,1,0:T(8,128)(2,1)S(1)} %pad_maximum_fusion.5), channel_id=1, source_target_pairs={{0,4},{4,0},{8,12},{12,8},{16,20},{20,16},{24,28},{28,24},{1,5},{5... | collective-permute-start | bytes 1572872 | tf_op jit(solution)/shard_map/ppermute | solution.py:139
  73.4 2.2 %collective-permute-start.12 = (bf16[2,16,32,256]{3,2,1,0:T(8,128)(2,1)S(1)}, bf16[2,16,32,256]{3,2,1,0:T(8,128)(2,1)S(1)}, u32[]{:S(2)}, u32[]{:S(2)}) collective-permute-start(bf16[2,16,32,256]{3,2,1,0:T(8,128)(2,1)S(1)} %pad_maximum_fusion.3), channel_id=1, source_target_pairs={{0,4},{4,0},{8,12},{12,8},{16,20},{20,16},{24,28},{28,24},{1,5},{5... | collective-permute-start | bytes 1572872 | tf_op jit(solution)/shard_map/ppermute | solution.py:139

commit v2 on v0

v2 whole, which is shorter than its diff:
```python
import functools
import math

import jax
import jax.numpy as jnp
import numpy as np
from jax import lax
from jax.experimental import pallas as pl
from jax.experimental.pallas import tpu as pltpu
from jax.sharding import PartitionSpec as P

BINS = 32
FIRST_BIN = 16
BIN_STEP = 8
ROUNDS = 2
LANES = 128
WIN_ROWS = 16
PITCH = 20
VMEM_BYTES = 44 * 1024 * 1024


def tapered_table(samples):
    sample = np.arange(samples, dtype=np.int32)
    freq = FIRST_BIN + BIN_STEP * np.arange(BINS, dtype=np.int32)
    phase = sample[:, None] * freq[None, :] % samples
    step = np.float32(2.0 * math.pi / samples)
    angle = step * phase.astype(np.float32)
    taper = np.float32(0.5) - np.float32(0.5) * np.cos(step * sample.astype(np.float32))
    both = np.stack([taper[:, None] * np.cos(angle), -taper[:, None] * np.sin(angle)], axis=2)
    both = both.reshape(samples, 2 * BINS)
    zero = np.zeros_like(both)
    tables = np.stack([np.concatenate([both, zero], 1), np.concatenate([zero, both], 1)], 0)
    return jnp.asarray(tables, dtype=jnp.bfloat16)


def spectra_kernel(chan_rows, n_out, win_ref, traces_ref, table_hbm, *rest):
    outs = rest[:n_out]
    raw_ref, turned_ref, traces_buf, table_ref, sems, table_sem = rest[n_out:]
    columns = 2 * BINS
    per = columns // n_out
    samples = traces_ref.shape[2]
    steps = LANES // chan_rows
    halves = traces_ref.shape[1] // WIN_ROWS
    rows = chan_rows * WIN_ROWS

    def copy(h, i, g):
        first = g * LANES + i * chan_rows
        return pltpu.make_async_copy(
            traces_ref.at[pl.ds(first, chan_rows), pl.ds(h * WIN_ROWS, WIN_ROWS), :],
            traces_buf.at[h, pl.ds(first, chan_rows)],
            sems.at[h, i, g],
        )

    table_copy = pltpu.make_async_copy(table_hbm, table_ref, table_sem)
    table_copy.start()
    for h in range(halves):

        @pl.loop(0, steps)
        def _(i):
            copy(h, i, 0).start()
            copy(h, i, 1).start()

    table_copy.wait()
    for h in range(halves):

        @pl.loop(0, steps)
        def _(i):
            copy(h, i, 0).wait()
            copy(h, i, 1).wait()
            low = traces_buf[h, pl.ds(i * chan_rows, chan_rows)].reshape(rows, samples)
            high = traces_buf[h, pl.ds(LANES + i * chan_rows, chan_rows)].reshape(rows, samples)
            raw = jnp.dot(low, table_ref[0], preferred_element_type=jnp.float32)
            raw += jnp.dot(high, table_ref[1], preferred_element_type=jnp.float32)
            base = pl.multiple_of(i * (chan_rows * PITCH), 8)
            for c in range(chan_rows):
                raw_ref[pl.ds(base + c * PITCH, WIN_ROWS), :] = raw[c * WIN_ROWS : (c + 1) * WIN_ROWS]

        for w in range(WIN_ROWS):
            turned = raw_ref[pl.ds(w, LANES, stride=PITCH), :].T
            for g in range(2):
                part = turned[g * columns : (g + 1) * columns]
                power = jnp.mean(part * part, axis=0, keepdims=True)
                first = g * columns * PITCH + w
                turned_ref[pl.ds(first, columns, stride=PITCH), :] = part * lax.rsqrt(power + 1e-05)
        for s in range(n_out):
            base = pl.multiple_of((win_ref[0] ^ s) * (per * PITCH), 8)
            for g in range(2):
                for k in range(per):
                    piece = turned_ref[pl.ds(base + (g * columns + k) * PITCH, WIN_ROWS), :]
                    outs[s][k, h * WIN_ROWS : (h + 1) * WIN_ROWS, g * LANES : (g + 1) * LANES] = (
                        piece.astype(jnp.bfloat16)
                    )


def local_spectra(traces, win_count):
    channels, windows, samples = traces.shape
    columns = 2 * BINS
    chan_rows = 32
    per = columns // win_count
    steps, halves = LANES // chan_rows, windows // WIN_ROWS
    flops = 2 * channels * windows * samples * columns
    return pl.pallas_call(
        functools.partial(spectra_kernel, chan_rows, win_count),
        in_specs=[
            pl.BlockSpec(memory_space=pltpu.SMEM),
            pl.BlockSpec(memory_space=pl.ANY),
            pl.BlockSpec(memory_space=pl.ANY),
        ],
        out_specs=[pl.BlockSpec(memory_space=pltpu.VMEM)] * win_count,
        out_shape=[jax.ShapeDtypeStruct((per, windows, channels), jnp.bfloat16)] * win_count,
        scratch_shapes=[
            pltpu.VMEM((LANES * PITCH, 2 * columns), jnp.float32),
            pltpu.VMEM((2 * columns * PITCH, LANES), jnp.float32),
            pltpu.VMEM((halves, channels, WIN_ROWS, samples), jnp.bfloat16),
            pltpu.VMEM((2, samples, 2 * columns), jnp.bfloat16),
            pltpu.SemaphoreType.DMA((halves, steps, 2)),
            pltpu.SemaphoreType.DMA,
        ],
        compiler_params=pltpu.CompilerParams(vmem_limit_bytes=VMEM_BYTES),
        cost_estimate=pl.CostEstimate(flops=flops, bytes_accessed=traces.size * 2, transcendentals=0),
        name="spectra",
    )(lax.axis_index("win").reshape(1), traces, tapered_table(samples))


def pick_kernel(keys, far_ref, *refs):
    halves, out_ref = refs[:-1], refs[-1]
    half = halves[0].shape[0] // 2
    for r in range(ROUNDS):
        for n, at in enumerate(keys):

            @pl.when(far_ref[r] == at)
            def _():
                low, high = halves[2 * n], halves[2 * n + 1]
                out_ref[r, :half] = low[:half]
                out_ref[r, half:] = high[high.shape[0] - half :]


def pick(found, far):
    keys = sorted(found)
    halves = [h for at in keys for h in found[at]]
    rows, windows, channels = found[0][0].shape
    whole = pl.BlockSpec(memory_space=pltpu.VMEM)
    return pl.pallas_call(
        functools.partial(pick_kernel, keys),
        in_specs=[pl.BlockSpec(memory_space=pltpu.SMEM)] + [whole] * len(halves),
        out_specs=whole,
        out_shape=jax.ShapeDtypeStruct((ROUNDS, rows, windows, channels), jnp.bfloat16),
        compiler_params=pltpu.CompilerParams(vmem_limit_bytes=VMEM_BYTES),
        name="pick",
    )(far, *halves)


def left_kernel(n_chunks, *refs):
    own, out_ref = refs[:n_chunks], refs[n_chunks]
    channels = out_ref.shape[1] // 2

    @pl.loop(0, out_ref.shape[0])
    def _(bin_no):
        straight, turned = [], []
        for s in range(n_chunks):
            real, imag = own[s][2 * bin_no], own[s][2 * bin_no + 1]
            straight += [real, imag]
            turned += [imag, -real]
        out_ref[bin_no, :channels] = jnp.concatenate(straight, axis=0).T
        out_ref[bin_no, channels:] = jnp.concatenate(turned, axis=0).T


def left_side(own, windows):
    rows, _, channels = own[0].shape
    whole = pl.BlockSpec(memory_space=pltpu.VMEM)
    return pl.pallas_call(
        functools.partial(left_kernel, len(own)),
        in_specs=[whole] * len(own),
        out_specs=whole,
        out_shape=jax.ShapeDtypeStruct((rows // 2, 2 * channels, 2 * windows), jnp.bfloat16),
        compiler_params=pltpu.CompilerParams(vmem_limit_bytes=VMEM_BYTES),
        name="left_side",
    )(*own)


def correlate_kernel(scale, n_chunks, keys, far_ref, left_ref, *refs):
    beside, refs = refs[:n_chunks], refs[n_chunks:]
    found, (out_hbm, right_ref, result_ref, sems) = refs[:-4], refs[-4:]
    bins_dev, both, depth = left_ref.shape
    rows, windows, channels = beside[0].shape[1:]
    half = rows // 2
    for r in range(ROUNDS):
        far = far_ref[r]

        @pl.when(far % 2 == 1)
        def _():
            for s in range(n_chunks):
                right_ref[r, s] = beside[s][r]

        for n, at in enumerate(keys):

            @pl.when(far == at)
            def _():
                for s in range(n_chunks):
                    low, high = found[(s * len(keys) + n) * 2 : (s * len(keys) + n) * 2 + 2]
                    right_ref[r, s, :half] = low[:half]
                    right_ref[r, s, half:] = high[high.shape[0] - half :]

    def send(bin_no, r):
        slot = bin_no % 2
        return pltpu.make_async_copy(result_ref.at[slot, r], out_hbm.at[r, bin_no], sems.at[slot, r])

    @pl.loop(0, bins_dev)
    def _(bin_no):
        for r in range(ROUNDS):
            right = jnp.concatenate(
                [right_ref[r, s, 2 * bin_no + part] for s in range(n_chunks) for part in range(2)], axis=0
            )

            @pl.when(bin_no >= 2)
            def _():
                send(bin_no - 2, r).wait()

            for part in range(2):
                left = left_ref[bin_no, part * channels : (part + 1) * channels]
                product = jnp.dot(left, right, preferred_element_type=jnp.float32)
                result_ref[bin_no % 2, r, part] = product * scale
            send(bin_no, r).start()

    for bin_no in range(max(bins_dev - 2, 0), bins_dev):
        for r in range(ROUNDS):
            send(bin_no, r).wait()


def correlate(far, left, beside, found, windows):
    n_chunks = len(beside)
    _, rows, windows_dev, channels = beside[0].shape
    bins_dev = rows // 2
    keys = [at for at in sorted(found[0]) if at]
    halves = [h for pieces in found for at in keys for h in pieces[at]]
    whole = pl.BlockSpec(memory_space=pltpu.VMEM)
    result = (ROUNDS, bins_dev, 2, channels, channels)
    flops = 8 * ROUNDS * bins_dev * windows * channels * channels
    return pl.pallas_call(
        functools.partial(correlate_kernel, 1.0 / math.sqrt(windows), n_chunks, keys),
        in_specs=[pl.BlockSpec(memory_space=pltpu.SMEM)] + [whole] * (1 + n_chunks + len(halves)),
        out_specs=pl.BlockSpec(memory_space=pl.ANY),
        out_shape=jax.ShapeDtypeStruct(result, jnp.float32),
        scratch_shapes=[
            pltpu.VMEM((ROUNDS, n_chunks, rows, windows_dev, channels), jnp.bfloat16),
            pltpu.VMEM((2, ROUNDS, 2, channels, channels), jnp.float32),
            pltpu.SemaphoreType.DMA((2, ROUNDS)),
        ],
        compiler_params=pltpu.CompilerParams(vmem_limit_bytes=VMEM_BYTES),
        cost_estimate=pl.CostEstimate(flops=flops, bytes_accessed=4 * math.prod(result), transcendentals=0),
        name="cross_spectra",
    )(far, left, *beside, *halves)


def partner_positions(partner, block_ids, count):
    slots = jnp.arange(count, dtype=jnp.int32)
    holder = jnp.sum(jnp.where(block_ids[None, :] == slots[:, None], slots[None, :], 0), axis=1)
    at_block = block_ids[:, None] == slots[None, :]
    wanted = jnp.sum(jnp.where(at_block[None], partner[:, None, :], 0), axis=2)
    return jnp.sum(jnp.where(wanted[:, :, None] == slots, holder, 0), axis=2)


def swap(value, axis, distance):
    count = lax.axis_size(axis)
    return lax.ppermute(value, axis, [(i, i ^ distance) for i in range(count)])


def after(value, *others):
    return lax.optimization_barrier((value, *others))[0]


def gather_even(piece, pair_count):
    half = piece.shape[0] // 2
    found = {0: (piece, piece)}
    for distance in range(2, pair_count, 2):
        if distance != 6:
            whole = swap(piece, "pair", distance)
            found[distance] = (whole, whole)
    if 6 < pair_count:
        found[6] = (swap(found[4][0][:half], "pair", 2), swap(found[2][1][half:], "pair", 4))
    return found


def local(traces, partner, block_ids):
    pair_count = lax.axis_size("pair")
    win_count = lax.axis_size("win")
    windows_dev = traces.shape[1]
    me = lax.axis_index("pair")
    slots = jnp.arange(pair_count, dtype=jnp.int32)
    paired = partner_positions(partner, block_ids, pair_count)
    mine = jnp.sum(jnp.where(slots == me, paired, 0), axis=1) ^ me
    beside = jnp.sum(jnp.where(slots == (me ^ 1), paired, 0), axis=1) ^ me
    sent = local_spectra(traces, win_count)
    own = [sent[0]]
    for s in range(1, win_count):
        own.append(swap(after(sent[s], own[2]) if s == 3 else sent[s], "win", s))
    found = []
    for s, piece in enumerate(own):
        direct = [at for at in (2, 4) if at < pair_count]
        if s >= 2:
            piece = after(piece, *[found[s - 1][at][0] for at in direct], *found[s - 2].get(6, ()))
        found.append(gather_even(piece, pair_count))
    arrived = [swap(pick(pieces, beside), "pair", 1) for pieces in found]
    windows = windows_dev * win_count
    return correlate(mine, left_side(own, windows), arrived, found, windows)


def solution(mesh):
    placed = (P("pair", "win", None), P(), P())
    return jax.shard_map(
        local,
        mesh=mesh,
        in_specs=placed,
        out_specs=P(None, "win", None, "pair", None),
        check_vma=False,
    )
```

time: 151 us -> 67 us (0.44)
  local copies, waits for them, and re-layouts: 44.6 us -> 1.78 us
  blocking collectives: 31.8 us -> 0 us
  starting transfers between devices: 7.64 us -> 30.3 us
  waiting for transfers between devices: 34.9 us -> 16.5 us
  Pallas kernels: 0 us -> 17.3 us
  other arithmetic: 17.2 us -> 0.7 us
  matrix products: 13.7 us -> 0 us
    all_to_all x2 -> x0, waiting for transfers between devices: 34.9 us -> none  [the longest x1 20.1 us: local(): lax.all_to_all(outgoing, 'pair', split_axis=1, concat_axis=1, tiled=True)]
    all_to_all x1 -> x0, blocking collectives: 31.8 us -> none  [local(): lax.all_to_all(spectra, 'win', split_axis=1, concat_axis=2, tiled=True)]
    ppermute x0 -> x23, starting transfers between devices: none -> 30.3 us  [swap(): return lax.ppermute(value, axis, [(i, i ^ distance) for i in range(count)])]
    pallas_call x0 -> x7, Pallas kernels: none -> 17.3 us  [the longest x1 8.28 us: local_spectra(): pl.pallas_call(functools.partial(spectra_kernel, chan_rows, win_count), i...]
    ppermute x0 -> x23, waiting for transfers between devices: none -> 16.5 us  [swap(): return lax.ppermute(value, axis, [(i, i ^ distance) for i in range(count)])]
    dot_general x3 -> x0, matrix products: 13.7 us -> none  [the longest x1 11 us: whitened(): raw = jnp.dot(trace_rows, dft_table, preferred_element_type=jnp.float32)]
    slice x3 -> x8, local copies, waits for them, and re-layouts: 11.1 us -> 0.74 us  [the longest x4 0.69 us: gather_even(): found[2][1][half:]]
    unnamed x15 -> x6, local copies, waits for them, and re-layouts: 10.3 us -> 1.05 us
  transfers between devices with their start and end apart: 2 -> 23, of which waited for: 2 -> 7; matrix products, arithmetic and copies ran while one was open for 4% -> 2% of each run, Pallas kernels for 0% -> 5%
where the time goes in v2:
time: 67 us; the launch traced here: 66.8 us
  starting transfers between devices  30.3 us (45%)
  Pallas kernels  17.3 us (26%)
  waiting for transfers between devices  16.5 us (25%)
  local copies, waits for them, and re-layouts  1.78 us (3%)
  other arithmetic  0.7 us (1%)
    ppermute x23, starting transfers between devices, swap(): return lax.ppermute(value, axis, [(i, i ^ distance) for i in range(count)])  30.3 us
    ppermute x23, waiting for transfers between devices, swap(): return lax.ppermute(value, axis, [(i, i ^ distance) for i in range(count)])  16.5 us
    pallas_call x1, Pallas kernels, local_spectra(): pl.pallas_call(functools.partial(spectra_kernel, chan_rows, win_count), i...  8.28 us
    pallas_call x1, Pallas kernels, correlate(): pl.pallas_call(functools.partial(correlate_kernel, 1.0 / math.sqrt(window...  5.54 us
    pallas_call x4, Pallas kernels, pick(): pl.pallas_call(functools.partial(pick_kernel, keys), in_specs=[pl.BlockSp...  2.52 us
  transfers between devices with their start and end apart: 23, of which 7 were waited for; matrix products, arithmetic and copies ran while one was open for 2% of the time, Pallas kernels for 5%

profile of v2, /device:TPU:0, one launch (start us, length us, event | category | flops | bytes accessed | tf_op | source)
XLA Modules:
  0.0 66.8 jit_solution(8277021904032248762)
XLA Ops:
  0.0 1.0 %copy-done = bf16[2,1024,128]{2,1,0:T(8,128)(2,1)S(1)} copy-done((bf16[2,1024,128]{2,1,0:T(8,128)(2,1)S(1)}, bf16[2,1024,128]{2,1,0:T(8,128)(2,1)}, u32[]{:S(2)}) %copy-start) | copy-done | bytes 524312
  1.0 8.3 %spectra.1 = (bf16[16,32,256]{2,1,0:T(8,128)(2,1)S(1)}, bf16[16,32,256]{2,1,0:T(8,128)(2,1)S(1)}, bf16[16,32,256]{2,1,0:T(8,128)(2,1)S(1)}, bf16[16,32,256]{2,1,0:T(8,128)(2,1)S(1)}) custom-call(s32[1]{0:T(128)} %bitcast.win_ref, bf16[256,32,1024]{2,1,0:T(8,128)(2,1)} %traces_ref.1, bf16[2,1024,128]{2,1,0:T(8,128)(2,1)S(1)} %copy-done), custom_call_target="tpu_custom_call" | custom-call | flops 1073741824 | bytes 16777216 | tf_op jit(solution)/shard_map/spectra/pallas_call | solution.py:102
  9.3 3.1 %collective-permute-start = (bf16[16,32,256]{2,1,0:T(8,128)(2,1)S(1)}, bf16[16,32,256]{2,1,0:T(8,128)(2,1)S(1)}, u32[]{:S(2)}, u32[]{:S(2)}) collective-permute-start(bf16[16,32,256]{2,1,0:T(8,128)(2,1)S(1)} %get-tuple-element.13), channel_id=1, source_target_pairs={{0,1},{1,0},{2,3},{3,2},{4,5},{5,4},{6,7},{7,6},{8,9},{9,8},{10,11... | collective-permute-start | bytes 786440 | tf_op jit(solution)/shard_map/ppermute | solution.py:265
  12.4 1.5 %collective-permute-start.4 = (bf16[16,32,256]{2,1,0:T(8,128)(2,1)S(1)}, bf16[16,32,256]{2,1,0:T(8,128)(2,1)S(1)}, u32[]{:S(2)}, u32[]{:S(2)}) collective-permute-start(bf16[16,32,256]{2,1,0:T(8,128)(2,1)S(1)} %get-tuple-element.12.refs_0_.refs_1_), channel_id=1, source_target_pairs={{0,16},{4,20},{8,24},{12,28},{16,0},{20,4},{24,8},{28,12},{1,17},{... | collective-permute-start | bytes 786440 | tf_op jit(solution)/shard_map/ppermute | solution.py:265
  13.9 1.5 %collective-permute-start.3 = (bf16[16,32,256]{2,1,0:T(8,128)(2,1)S(1)}, bf16[16,32,256]{2,1,0:T(8,128)(2,1)S(1)}, u32[]{:S(2)}, u32[]{:S(2)}) collective-permute-start(bf16[16,32,256]{2,1,0:T(8,128)(2,1)S(1)} %get-tuple-element.12.refs_0_.refs_1_), channel_id=1, source_target_pairs={{0,8},{4,12},{8,0},{12,4},{16,24},{20,28},{24,16},{28,20},{1,9},{5... | collective-permute-start | bytes 786440 | tf_op jit(solution)/shard_map/ppermute | solution.py:265
  15.4 2.6 %collective-permute-start.1 = (bf16[16,32,256]{2,1,0:T(8,128)(2,1)S(1)}, bf16[16,32,256]{2,1,0:T(8,128)(2,1)S(1)}, u32[]{:S(2)}, u32[]{:S(2)}) collective-permute-start(bf16[16,32,256]{2,1,0:T(8,128)(2,1)S(1)} %get-tuple-element.14), channel_id=1, source_target_pairs={{0,2},{1,3},{2,0},{3,1},{4,6},{5,7},{6,4},{7,5},{8,10},{9,11},{10,... | collective-permute-start | bytes 786440 | tf_op jit(solution)/shard_map/ppermute | solution.py:265
  18.0 3.3 %collective-permute-done.refs_1_.refs_0_ = bf16[16,32,256]{2,1,0:T(8,128)(2,1)S(1)} collective-permute-done((bf16[16,32,256]{2,1,0:T(8,128)(2,1)S(1)}, bf16[16,32,256]{2,1,0:T(8,128)(2,1)S(1)}, u32[]{:S(2)}, u32[]{:S(2)}) %collective-permute-start) | collective-permute-done | bytes 262176 | tf_op jit(solution)/shard_map/ppermute | solution.py:265
  21.3 3.2 %collective-permute-start.9 = (bf16[16,32,256]{2,1,0:T(8,128)(2,1)S(1)}, bf16[16,32,256]{2,1,0:T(8,128)(2,1)S(1)}, u32[]{:S(2)}, u32[]{:S(2)}) collective-permute-start(bf16[16,32,256]{2,1,0:T(8,128)(2,1)S(1)} %collective-permute-done.refs_1_.refs_0_), channel_id=1, source_target_pairs={{0,16},{4,20},{8,24},{12,28},{16,0},{20,4},{24,8},{28,12},{1,17},{... | collective-permute-start | bytes 786440 | tf_op jit(solution)/shard_map/ppermute | solution.py:265
  24.5 2.4 %collective-permute-start.8 = (bf16[16,32,256]{2,1,0:T(8,128)(2,1)S(1)}, bf16[16,32,256]{2,1,0:T(8,128)(2,1)S(1)}, u32[]{:S(2)}, u32[]{:S(2)}) collective-permute-start(bf16[16,32,256]{2,1,0:T(8,128)(2,1)S(1)} %collective-permute-done.refs_1_.refs_0_), channel_id=1, source_target_pairs={{0,8},{4,12},{8,0},{12,4},{16,24},{20,28},{24,16},{28,20},{1,9},{5... | collective-permute-start | bytes 786440 | tf_op jit(solution)/shard_map/ppermute | solution.py:265
  27.1 2.1 %collective-permute-done.1.refs_2_.refs_0_.refs_1_ = bf16[16,32,256]{2,1,0:T(8,128)(2,1)S(1)} collective-permute-done((bf16[16,32,256]{2,1,0:T(8,128)(2,1)S(1)}, bf16[16,32,256]{2,1,0:T(8,128)(2,1)S(1)}, u32[]{:S(2)}, u32[]{:S(2)}) %collective-permute-start.1) | collective-permute-done | bytes 262176 | tf_op jit(solution)/shard_map/ppermute | solution.py:265
  29.2 3.4 %collective-permute-start.2 = (bf16[16,32,256]{2,1,0:T(8,128)(2,1)S(1)}, bf16[16,32,256]{2,1,0:T(8,128)(2,1)S(1)}, u32[]{:S(2)}, u32[]{:S(2)}) collective-permute-start(bf16[16,32,256]{2,1,0:T(8,128)(2,1)S(1)} %get-tuple-element.16), channel_id=1, source_target_pairs={{0,3},{1,2},{2,1},{3,0},{4,7},{5,6},{6,5},{7,4},{8,11},{9,10},{10,... | collective-permute-start | bytes 786440 | tf_op jit(solution)/shard_map/ppermute | solution.py:265
  32.6 2.2 %collective-permute-done.5.refs_6_.refs_8_ = bf16[8,32,256]{2,1,0:T(8,128)(2,1)S(1)} collective-permute-done((bf16[8,32,256]{2,1,0:T(8,128)(2,1)S(1)}, bf16[8,32,256]{2,1,0:T(8,128)(2,1)S(1)}, u32[]{:S(2)}, u32[]{:S(2)}) %collective-permute-start.5) | collective-permute-done | bytes 131104 | tf_op jit(solution)/shard_map/ppermute | solution.py:265
  35.2 1.7 %collective-permute-start.13 = (bf16[16,32,256]{2,1,0:T(8,128)(2,1)S(1)}, bf16[16,32,256]{2,1,0:T(8,128)(2,1)S(1)}, u32[]{:S(2)}, u32[]{:S(2)}) collective-permute-start(bf16[16,32,256]{2,1,0:T(8,128)(2,1)S(1)} %collective-permute-done.1.refs_2_.refs_0_.refs_1_), channel_id=1, source_target_pairs={{0,8},{4,12},{8,0},{12,4},{16,24},{20,28},{24,16},{28,20},{1,9},{5... | collective-permute-start | bytes 786440 | tf_op jit(solution)/shard_map/ppermute | solution.py:265
  37.4 0.7 slice.35
  38.1 1.7 %collective-permute-start.11 = (bf16[8,32,256]{2,1,0:T(8,128)(2,1)}, bf16[8,32,256]{2,1,0:T(8,128)(2,1)S(1)}, u32[]{:S(2)}, u32[]{:S(2)}) collective-permute-start(bf16[8,32,256]{2,1,0:T(8,128)(2,1)} %slice.35), channel_id=1, source_target_pairs={{0,16},{4,20},{8,24},{12,28},{16,0},{20,4},{24,8},{28,12},{1,17},{... | collective-permute-start | bytes 393224 | tf_op jit(solution)/shard_map/ppermute | solution.py:265
  40.1 4.2 %collective-permute-done.10.refs_6_.refs_14_ = bf16[8,32,256]{2,1,0:T(8,128)(2,1)S(1)} collective-permute-done((bf16[8,32,256]{2,1,0:T(8,128)(2,1)S(1)}, bf16[8,32,256]{2,1,0:T(8,128)(2,1)S(1)}, u32[]{:S(2)}, u32[]{:S(2)}) %collective-permute-start.10) | collective-permute-done | bytes 131104 | tf_op jit(solution)/shard_map/ppermute | solution.py:265
  44.3 1.5 %collective-permute-start.19 = (bf16[16,32,256]{2,1,0:T(8,128)(2,1)S(1)}, bf16[16,32,256]{2,1,0:T(8,128)(2,1)S(1)}, u32[]{:S(2)}, u32[]{:S(2)}) collective-permute-start(bf16[16,32,256]{2,1,0:T(8,128)(2,1)S(1)} %collective-permute-done.2.refs_3_.refs_0_.refs_1_), channel_id=1, source_target_pairs={{0,16},{4,20},{8,24},{12,28},{16,0},{20,4},{24,8},{28,12},{1,17},{... | collective-permute-start | bytes 786440 | tf_op jit(solution)/shard_map/ppermute | solution.py:265
  45.8 1.6 %collective-permute-start.18 = (bf16[16,32,256]{2,1,0:T(8,128)(2,1)S(1)}, bf16[16,32,256]{2,1,0:T(8,128)(2,1)S(1)}, u32[]{:S(2)}, u32[]{:S(2)}) collective-permute-start(bf16[16,32,256]{2,1,0:T(8,128)(2,1)S(1)} %collective-permute-done.2.refs_3_.refs_0_.refs_1_), channel_id=1, source_target_pairs={{0,8},{4,12},{8,0},{12,4},{16,24},{20,28},{24,16},{28,20},{1,9},{5... | collective-permute-start | bytes 786440 | tf_op jit(solution)/shard_map/ppermute | solution.py:265
  47.8 0.5 collective-permute-start.15
  48.3 0.6 collective-permute-start.16
  49.0 3.0 %collective-permute-done.19.refs_4_.refs_5_.refs_24_.refs_25_ = bf16[16,32,256]{2,1,0:T(8,128)(2,1)S(1)} collective-permute-done((bf16[16,32,256]{2,1,0:T(8,128)(2,1)S(1)}, bf16[16,32,256]{2,1,0:T(8,128)(2,1)S(1)}, u32[]{:S(2)}, u32[]{:S(2)}) %collective-permute-start.19) | collective-permute-done | bytes 262176 | tf_op jit(solution)/shard_map/ppermute | solution.py:265
  51.9 1.7 %collective-permute-start.20 = (bf16[8,32,256]{2,1,0:T(8,128)(2,1)S(1)}, bf16[8,32,256]{2,1,0:T(8,128)(2,1)S(1)}, u32[]{:S(2)}, u32[]{:S(2)}) collective-permute-start(bf16[8,32,256]{2,1,0:T(8,128)(2,1)S(1)} %slice.38), channel_id=1, source_target_pairs={{0,8},{4,12},{8,0},{12,4},{16,24},{20,28},{24,16},{28,20},{1,9},{5... | collective-permute-start | bytes 393224 | tf_op jit(solution)/shard_map/ppermute | solution.py:265
  53.6 1.5 %collective-permute-start.21 = (bf16[8,32,256]{2,1,0:T(8,128)(2,1)S(1)}, bf16[8,32,256]{2,1,0:T(8,128)(2,1)S(1)}, u32[]{:S(2)}, u32[]{:S(2)}) collective-permute-start(bf16[8,32,256]{2,1,0:T(8,128)(2,1)S(1)} %slice.39), channel_id=1, source_target_pairs={{0,16},{4,20},{8,24},{12,28},{16,0},{20,4},{24,8},{28,12},{1,17},{... | collective-permute-start | bytes 393224 | tf_op jit(solution)/shard_map/ppermute | solution.py:265
  55.2 0.6 pick.4
  55.9 0.6 pick.5
  56.6 0.5 collective-permute-start.12
  57.1 0.6 pick.6
  57.8 0.8 %collective-permute-done.21.refs_7_.refs_27_ = bf16[8,32,256]{2,1,0:T(8,128)(2,1)S(1)} collective-permute-done((bf16[8,32,256]{2,1,0:T(8,128)(2,1)S(1)}, bf16[8,32,256]{2,1,0:T(8,128)(2,1)S(1)}, u32[]{:S(2)}, u32[]{:S(2)}) %collective-permute-start.21) | collective-permute-done | bytes 131104 | tf_op jit(solution)/shard_map/ppermute | solution.py:265
  58.7 0.6 pick.7
  59.4 1.0 %left_side.1.left_ref = bf16[8,512,256]{2,1,0:T(8,128)(2,1)S(1)} custom-call(bf16[16,32,256]{2,1,0:T(8,128)(2,1)S(1)} %get-tuple-element.12.refs_0_.refs_1_, bf16[16,32,256]{2,1,0:T(8,128)(2,1)S(1)} %collective-permute-done.refs_1_.refs_0_, bf16[16,32,256]{2,1,0:T(8,128)(2,1)S(1)} %collective-permute-done.1.refs_2_.refs_0_.refs_1_, ...), custom_call_target="tpu_custom_call" | custom-call | tf_op jit(solution)/shard_map/left_side/pallas_call | solution.py:171
  60.4 0.9 %collective-permute-done.22.refs_3_ = bf16[2,16,32,256]{3,2,1,0:T(8,128)(2,1)S(1)} collective-permute-done((bf16[2,16,32,256]{3,2,1,0:T(8,128)(2,1)S(1)}, bf16[2,16,32,256]{3,2,1,0:T(8,128)(2,1)S(1)}, u32[]{:S(2)}, u32[]{:S(2)}) %collective-permute-start.22) | collective-permute-done | bytes 524320 | tf_op jit(solution)/shard_map/ppermute | solution.py:265
  61.3 5.5 %cross_spectra.1 = f32[2,8,2,256,256]{4,3,2,1,0:T(8,128)} custom-call(s32[2]{0:T(128)S(1)} %broadcast_xor_fusion.1.far_ref, bf16[8,512,256]{2,1,0:T(8,128)(2,1)S(1)} %left_side.1.left_ref, bf16[2,16,32,256]{3,2,1,0:T(8,128)(2,1)S(1)} %collective-permute-done.7.refs_0_, bf16[2,16,32,256]{3,2,1,0:T(8,128)(2,1)S(1)} %collective-permute-done.12.refs_1_, ...), custom_call_target="tpu_custom_call" | custom-call | flops 1073741824 | bytes 8388608 | tf_op jit(solution)/shard_map/cross_spectra/pallas_call | solution.py:239
  (43 shorter events, 1.9 us)
Async XLA Ops:
  0.0 1.0 %copy-start = (bf16[2,1024,128]{2,1,0:T(8,128)(2,1)S(1)}, bf16[2,1024,128]{2,1,0:T(8,128)(2,1)}, u32[]{:S(2)}) copy-start(bf16[2,1024,128]{2,1,0:T(8,128)(2,1)} %constant.15.clone.table_hbm) | copy-start | bytes 1572868
  1.0 35.9 %copy-start.2 = (s32[8]{0:T(128)S(1)}, s32[8]{0:T(128)}, u32[]{:S(2)}) copy-start(s32[8]{0:T(128)} %param.6) | copy-start | bytes 100
  1.0 38.9 %copy-start.1 = (s32[2,8]{1,0:T(2,128)S(1)}, s32[2,8]{1,0:T(2,128)}, u32[]{:S(2)}) copy-start(s32[2,8]{1,0:T(2,128)} %param.5) | copy-start | bytes 196
  9.3 12.0 %collective-permute-start = (bf16[16,32,256]{2,1,0:T(8,128)(2,1)S(1)}, bf16[16,32,256]{2,1,0:T(8,128)(2,1)S(1)}, u32[]{:S(2)}, u32[]{:S(2)}) collective-permute-start(bf16[16,32,256]{2,1,0:T(8,128)(2,1)S(1)} %get-tuple-element.13), channel_id=1, source_target_pairs={{0,1},{1,0},{2,3},{3,2},{4,5},{5,4},{6,7},{7,6},{8,9},{9,8},{10,11... | collective-permute-start | bytes 786440 | tf_op jit(solution)/shard_map/ppermute | solution.py:265
  12.4 14.5 %collective-permute-start.4 = (bf16[16,32,256]{2,1,0:T(8,128)(2,1)S(1)}, bf16[16,32,256]{2,1,0:T(8,128)(2,1)S(1)}, u32[]{:S(2)}, u32[]{:S(2)}) collective-permute-start(bf16[16,32,256]{2,1,0:T(8,128)(2,1)S(1)} %get-tuple-element.12.refs_0_.refs_1_), channel_id=1, source_target_pairs={{0,16},{4,20},{8,24},{12,28},{16,0},{20,4},{24,8},{28,12},{1,17},{... | collective-permute-start | bytes 786440 | tf_op jit(solution)/shard_map/ppermute | solution.py:265
  13.9 13.1 %collective-permute-start.3 = (bf16[16,32,256]{2,1,0:T(8,128)(2,1)S(1)}, bf16[16,32,256]{2,1,0:T(8,128)(2,1)S(1)}, u32[]{:S(2)}, u32[]{:S(2)}) collective-permute-start(bf16[16,32,256]{2,1,0:T(8,128)(2,1)S(1)} %get-tuple-element.12.refs_0_.refs_1_), channel_id=1, source_target_pairs={{0,8},{4,12},{8,0},{12,4},{16,24},{20,28},{24,16},{28,20},{1,9},{5... | collective-permute-start | bytes 786440 | tf_op jit(solution)/shard_map/ppermute | solution.py:265
  15.4 13.8 %collective-permute-start.1 = (bf16[16,32,256]{2,1,0:T(8,128)(2,1)S(1)}, bf16[16,32,256]{2,1,0:T(8,128)(2,1)S(1)}, u32[]{:S(2)}, u32[]{:S(2)}) collective-permute-start(bf16[16,32,256]{2,1,0:T(8,128)(2,1)S(1)} %get-tuple-element.14), channel_id=1, source_target_pairs={{0,2},{1,3},{2,0},{3,1},{4,6},{5,7},{6,4},{7,5},{8,10},{9,11},{10,... | collective-permute-start | bytes 786440 | tf_op jit(solution)/shard_map/ppermute | solution.py:265
  21.3 13.6 %collective-permute-start.9 = (bf16[16,32,256]{2,1,0:T(8,128)(2,1)S(1)}, bf16[16,32,256]{2,1,0:T(8,128)(2,1)S(1)}, u32[]{:S(2)}, u32[]{:S(2)}) collective-permute-start(bf16[16,32,256]{2,1,0:T(8,128)(2,1)S(1)} %collective-permute-done.refs_1_.refs_0_), channel_id=1, source_target_pairs={{0,16},{4,20},{8,24},{12,28},{16,0},{20,4},{24,8},{28,12},{1,17},{... | collective-permute-start | bytes 786440 | tf_op jit(solution)/shard_map/ppermute | solution.py:265
  24.5 10.4 %collective-permute-start.8 = (bf16[16,32,256]{2,1,0:T(8,128)(2,1)S(1)}, bf16[16,32,256]{2,1,0:T(8,128)(2,1)S(1)}, u32[]{:S(2)}, u32[]{:S(2)}) collective-permute-start(bf16[16,32,256]{2,1,0:T(8,128)(2,1)S(1)} %collective-permute-done.refs_1_.refs_0_), channel_id=1, source_target_pairs={{0,8},{4,12},{8,0},{12,4},{16,24},{20,28},{24,16},{28,20},{1,9},{5... | collective-permute-start | bytes 786440 | tf_op jit(solution)/shard_map/ppermute | solution.py:265
  26.9 7.9 %collective-permute-start.5 = (bf16[8,32,256]{2,1,0:T(8,128)(2,1)S(1)}, bf16[8,32,256]{2,1,0:T(8,128)(2,1)S(1)}, u32[]{:S(2)}, u32[]{:S(2)}) collective-permute-start(bf16[8,32,256]{2,1,0:T(8,128)(2,1)S(1)} %slice.32), channel_id=1, source_target_pairs={{0,8},{4,12},{8,0},{12,4},{16,24},{20,28},{24,16},{28,20},{1,9},{5... | collective-permute-start | bytes 393224 | tf_op jit(solution)/shard_map/ppermute | solution.py:265
  27.0 7.8 %collective-permute-start.6 = (bf16[8,32,256]{2,1,0:T(8,128)(2,1)S(1)}, bf16[8,32,256]{2,1,0:T(8,128)(2,1)S(1)}, u32[]{:S(2)}, u32[]{:S(2)}) collective-permute-start(bf16[8,32,256]{2,1,0:T(8,128)(2,1)S(1)} %slice.33), channel_id=1, source_target_pairs={{0,16},{4,20},{8,24},{12,28},{16,0},{20,4},{24,8},{28,12},{1,17},{... | collective-permute-start | bytes 393224 | tf_op jit(solution)/shard_map/ppermute | solution.py:265
  29.2 10.9 %collective-permute-start.2 = (bf16[16,32,256]{2,1,0:T(8,128)(2,1)S(1)}, bf16[16,32,256]{2,1,0:T(8,128)(2,1)S(1)}, u32[]{:S(2)}, u32[]{:S(2)}) collective-permute-start(bf16[16,32,256]{2,1,0:T(8,128)(2,1)S(1)} %get-tuple-element.16), channel_id=1, source_target_pairs={{0,3},{1,2},{2,1},{3,0},{4,7},{5,6},{6,5},{7,4},{8,11},{9,10},{10,... | collective-permute-start | bytes 786440 | tf_op jit(solution)/shard_map/ppermute | solution.py:265
  34.9 9.4 %collective-permute-start.14 = (bf16[16,32,256]{2,1,0:T(8,128)(2,1)S(1)}, bf16[16,32,256]{2,1,0:T(8,128)(2,1)S(1)}, u32[]{:S(2)}, u32[]{:S(2)}) collective-permute-start(bf16[16,32,256]{2,1,0:T(8,128)(2,1)S(1)} %collective-permute-done.1.refs_2_.refs_0_.refs_1_), channel_id=1, source_target_pairs={{0,16},{4,20},{8,24},{12,28},{16,0},{20,4},{24,8},{28,12},{1,17},{... | collective-permute-start | bytes 786440 | tf_op jit(solution)/shard_map/ppermute | solution.py:265
  35.2 9.1 %collective-permute-start.13 = (bf16[16,32,256]{2,1,0:T(8,128)(2,1)S(1)}, bf16[16,32,256]{2,1,0:T(8,128)(2,1)S(1)}, u32[]{:S(2)}, u32[]{:S(2)}) collective-permute-start(bf16[16,32,256]{2,1,0:T(8,128)(2,1)S(1)} %collective-permute-done.1.refs_2_.refs_0_.refs_1_), channel_id=1, source_target_pairs={{0,8},{4,12},{8,0},{12,4},{16,24},{20,28},{24,16},{28,20},{1,9},{5... | collective-permute-start | bytes 786440 | tf_op jit(solution)/shard_map/ppermute | solution.py:265
  37.1 7.2 %collective-permute-start.10 = (bf16[8,32,256]{2,1,0:T(8,128)(2,1)S(1)}, bf16[8,32,256]{2,1,0:T(8,128)(2,1)S(1)}, u32[]{:S(2)}, u32[]{:S(2)}) collective-permute-start(bf16[8,32,256]{2,1,0:T(8,128)(2,1)S(1)} %slice.34), channel_id=1, source_target_pairs={{0,8},{4,12},{8,0},{12,4},{16,24},{20,28},{24,16},{28,20},{1,9},{5... | collective-permute-start | bytes 393224 | tf_op jit(solution)/shard_map/ppermute | solution.py:265
  38.1 6.2 %collective-permute-start.11 = (bf16[8,32,256]{2,1,0:T(8,128)(2,1)}, bf16[8,32,256]{2,1,0:T(8,128)(2,1)S(1)}, u32[]{:S(2)}, u32[]{:S(2)}) collective-permute-start(bf16[8,32,256]{2,1,0:T(8,128)(2,1)} %slice.35), channel_id=1, source_target_pairs={{0,16},{4,20},{8,24},{12,28},{16,0},{20,4},{24,8},{28,12},{1,17},{... | collective-permute-start | bytes 393224 | tf_op jit(solution)/shard_map/ppermute | solution.py:265
  44.3 7.6 %collective-permute-start.19 = (bf16[16,32,256]{2,1,0:T(8,128)(2,1)S(1)}, bf16[16,32,256]{2,1,0:T(8,128)(2,1)S(1)}, u32[]{:S(2)}, u32[]{:S(2)}) collective-permute-start(bf16[16,32,256]{2,1,0:T(8,128)(2,1)S(1)} %collective-permute-done.2.refs_3_.refs_0_.refs_1_), channel_id=1, source_target_pairs={{0,16},{4,20},{8,24},{12,28},{16,0},{20,4},{24,8},{28,12},{1,17},{... | collective-permute-start | bytes 786440 | tf_op jit(solution)/shard_map/ppermute | solution.py:265
  45.8 7.8 %collective-permute-start.18 = (bf16[16,32,256]{2,1,0:T(8,128)(2,1)S(1)}, bf16[16,32,256]{2,1,0:T(8,128)(2,1)S(1)}, u32[]{:S(2)}, u32[]{:S(2)}) collective-permute-start(bf16[16,32,256]{2,1,0:T(8,128)(2,1)S(1)} %collective-permute-done.2.refs_3_.refs_0_.refs_1_), channel_id=1, source_target_pairs={{0,8},{4,12},{8,0},{12,4},{16,24},{20,28},{24,16},{28,20},{1,9},{5... | collective-permute-start | bytes 786440 | tf_op jit(solution)/shard_map/ppermute | solution.py:265
  47.8 8.7 %collective-permute-start.15 = (bf16[8,32,256]{2,1,0:T(8,128)(2,1)S(1)}, bf16[8,32,256]{2,1,0:T(8,128)(2,1)S(1)}, u32[]{:S(2)}, u32[]{:S(2)}) collective-permute-start(bf16[8,32,256]{2,1,0:T(8,128)(2,1)S(1)} %slice.36), channel_id=1, source_target_pairs={{0,8},{4,12},{8,0},{12,4},{16,24},{20,28},{24,16},{28,20},{1,9},{5... | collective-permute-start | bytes 393224 | tf_op jit(solution)/shard_map/ppermute | solution.py:265
  48.3 8.8 %collective-permute-start.16 = (bf16[8,32,256]{2,1,0:T(8,128)(2,1)S(1)}, bf16[8,32,256]{2,1,0:T(8,128)(2,1)S(1)}, u32[]{:S(2)}, u32[]{:S(2)}) collective-permute-start(bf16[8,32,256]{2,1,0:T(8,128)(2,1)S(1)} %slice.37), channel_id=1, source_target_pairs={{0,16},{4,20},{8,24},{12,28},{16,0},{20,4},{24,8},{28,12},{1,17},{... | collective-permute-start | bytes 393224 | tf_op jit(solution)/shard_map/ppermute | solution.py:265
  51.9 5.9 %collective-permute-start.20 = (bf16[8,32,256]{2,1,0:T(8,128)(2,1)S(1)}, bf16[8,32,256]{2,1,0:T(8,128)(2,1)S(1)}, u32[]{:S(2)}, u32[]{:S(2)}) collective-permute-start(bf16[8,32,256]{2,1,0:T(8,128)(2,1)S(1)} %slice.38), channel_id=1, source_target_pairs={{0,8},{4,12},{8,0},{12,4},{16,24},{20,28},{24,16},{28,20},{1,9},{5... | collective-permute-start | bytes 393224 | tf_op jit(solution)/shard_map/ppermute | solution.py:265
  53.6 5.0 %collective-permute-start.21 = (bf16[8,32,256]{2,1,0:T(8,128)(2,1)S(1)}, bf16[8,32,256]{2,1,0:T(8,128)(2,1)S(1)}, u32[]{:S(2)}, u32[]{:S(2)}) collective-permute-start(bf16[8,32,256]{2,1,0:T(8,128)(2,1)S(1)} %slice.39), channel_id=1, source_target_pairs={{0,16},{4,20},{8,24},{12,28},{16,0},{20,4},{24,8},{28,12},{1,17},{... | collective-permute-start | bytes 393224 | tf_op jit(solution)/shard_map/ppermute | solution.py:265
  55.8 4.6 %collective-permute-start.7 = (bf16[2,16,32,256]{3,2,1,0:T(8,128)(2,1)S(1)}, bf16[2,16,32,256]{3,2,1,0:T(8,128)(2,1)S(1)}, u32[]{:S(2)}, u32[]{:S(2)}) collective-permute-start(bf16[2,16,32,256]{3,2,1,0:T(8,128)(2,1)S(1)} %pick.4), channel_id=1, source_target_pairs={{0,4},{4,0},{8,12},{12,8},{16,20},{20,16},{24,28},{28,24},{1,5},{5... | collective-permute-start | bytes 1572872 | tf_op jit(solution)/shard_map/ppermute | solution.py:265
  56.6 3.8 %collective-permute-start.12 = (bf16[2,16,32,256]{3,2,1,0:T(8,128)(2,1)S(1)}, bf16[2,16,32,256]{3,2,1,0:T(8,128)(2,1)S(1)}, u32[]{:S(2)}, u32[]{:S(2)}) collective-permute-start(bf16[2,16,32,256]{3,2,1,0:T(8,128)(2,1)S(1)} %pick.5), channel_id=1, source_target_pairs={{0,4},{4,0},{8,12},{12,8},{16,20},{20,16},{24,28},{28,24},{1,5},{5... | collective-permute-start | bytes 1572872 | tf_op jit(solution)/shard_map/ppermute | solution.py:265
  57.7 2.7 %collective-permute-start.17 = (bf16[2,16,32,256]{3,2,1,0:T(8,128)(2,1)S(1)}, bf16[2,16,32,256]{3,2,1,0:T(8,128)(2,1)S(1)}, u32[]{:S(2)}, u32[]{:S(2)}) collective-permute-start(bf16[2,16,32,256]{3,2,1,0:T(8,128)(2,1)S(1)} %pick.6), channel_id=1, source_target_pairs={{0,4},{4,0},{8,12},{12,8},{16,20},{20,16},{24,28},{28,24},{1,5},{5... | collective-permute-start | bytes 1572872 | tf_op jit(solution)/shard_map/ppermute | solution.py:265
  59.3 2.0 %collective-permute-start.22 = (bf16[2,16,32,256]{3,2,1,0:T(8,128)(2,1)S(1)}, bf16[2,16,32,256]{3,2,1,0:T(8,128)(2,1)S(1)}, u32[]{:S(2)}, u32[]{:S(2)}) collective-permute-start(bf16[2,16,32,256]{3,2,1,0:T(8,128)(2,1)S(1)} %pick.7), channel_id=1, source_target_pairs={{0,4},{4,0},{8,12},{12,8},{16,20},{20,16},{24,28},{28,24},{1,5},{5... | collective-permute-start | bytes 1572872 | tf_op jit(solution)/shard_map/ppermute | solution.py:265

commit v3 on v2

v3 whole, which is shorter than its diff:
```python
import functools
import math

import jax
import jax.numpy as jnp
from jax import lax
from jax.experimental import pallas as pl
from jax.experimental.pallas import tpu as pltpu
from jax.sharding import PartitionSpec as P

BINS = 32
FIRST_BIN = 16
BIN_STEP = 8
ROUNDS = 2
LANES = 128
WIN_ROWS = 16
PITCH = 20
VMEM_BYTES = 44 * 1024 * 1024


def fill_table(table_ref):
    samples, columns = table_ref.shape[1], 2 * BINS
    period = samples // math.gcd(FIRST_BIN, BIN_STEP, samples)
    step = 2.0 * math.pi / samples
    sample = lax.broadcasted_iota(jnp.int32, (period, LANES), 0)
    column = lax.broadcasted_iota(jnp.int32, (period, LANES), 1) & (columns - 1)
    freq = FIRST_BIN + BIN_STEP * (column >> 1)
    angle = step * ((sample * freq) & (samples - 1)).astype(jnp.float32)
    waves = jnp.where((column & 1) == 0, jnp.cos(angle), -jnp.sin(angle))
    around = step * sample.astype(jnp.float32)
    cosine, sine = jnp.cos(around), jnp.sin(around)
    low = lax.broadcasted_iota(jnp.int32, (period, LANES), 1) < columns
    for n in range(samples // period):
        turn = 2.0 * math.pi * n * period / samples
        taper = 0.5 - 0.5 * (math.cos(turn) * cosine - math.sin(turn) * sine)
        tapered = taper * waves
        rows = slice(n * period, (n + 1) * period)
        table_ref[0, rows] = jnp.where(low, tapered, 0.0).astype(jnp.bfloat16)
        table_ref[1, rows] = jnp.where(low, 0.0, tapered).astype(jnp.bfloat16)


def spectra_kernel(chan_rows, win_count, pieces, win_ref, traces_ref, *rest):
    outs = rest[: len(pieces)]
    raw_ref, turned_ref, traces_buf, table_ref, sems = rest[len(pieces) :]
    columns = 2 * BINS
    per = columns // win_count
    samples = traces_ref.shape[2]
    steps = LANES // chan_rows
    halves = traces_ref.shape[1] // WIN_ROWS
    rows = chan_rows * WIN_ROWS

    def copy(h, i, g):
        first = g * LANES + i * chan_rows
        return pltpu.make_async_copy(
            traces_ref.at[pl.ds(first, chan_rows), pl.ds(h * WIN_ROWS, WIN_ROWS), :],
            traces_buf.at[h, pl.ds(first, chan_rows)],
            sems.at[h, i, g],
        )

    for h in range(halves):

        @pl.loop(0, steps)
        def _(i):
            copy(h, i, 0).start()
            copy(h, i, 1).start()

    fill_table(table_ref)
    for h in range(halves):

        @pl.loop(0, steps)
        def _(i):
            copy(h, i, 0).wait()
            copy(h, i, 1).wait()
            low = traces_buf[h, pl.ds(i * chan_rows, chan_rows)].reshape(rows, samples)
            high = traces_buf[h, pl.ds(LANES + i * chan_rows, chan_rows)].reshape(rows, samples)
            raw = jnp.dot(low, table_ref[0], preferred_element_type=jnp.float32)
            raw += jnp.dot(high, table_ref[1], preferred_element_type=jnp.float32)
            base = pl.multiple_of(i * (chan_rows * PITCH), 8)
            for c in range(chan_rows):
                raw_ref[pl.ds(base + c * PITCH, WIN_ROWS), :] = raw[c * WIN_ROWS : (c + 1) * WIN_ROWS]

        for w in range(WIN_ROWS):
            turned = raw_ref[pl.ds(w, LANES, stride=PITCH), :].T
            for g in range(2):
                part = turned[g * columns : (g + 1) * columns]
                power = jnp.mean(part * part, axis=0, keepdims=True)
                first = g * columns * PITCH + w
                turned_ref[pl.ds(first, columns, stride=PITCH), :] = part * lax.rsqrt(power + 1e-05)
        for out_ref, (s, low, high) in zip(outs, pieces):
            base = pl.multiple_of((win_ref[0] ^ s) * (per * PITCH), 8)
            for g in range(2):
                for k in range(low, high):
                    taken = turned_ref[pl.ds(base + (g * columns + k) * PITCH, WIN_ROWS), :]
                    out_ref[k - low, h * WIN_ROWS : (h + 1) * WIN_ROWS, g * LANES : (g + 1) * LANES] = (
                        taken.astype(jnp.bfloat16)
                    )


def local_spectra(traces, win_count, pieces):
    channels, windows, samples = traces.shape
    columns = 2 * BINS
    chan_rows = 32
    steps, halves = LANES // chan_rows, windows // WIN_ROWS
    flops = 2 * channels * windows * samples * columns
    return pl.pallas_call(
        functools.partial(spectra_kernel, chan_rows, win_count, pieces),
        in_specs=[
            pl.BlockSpec(memory_space=pltpu.SMEM),
            pl.BlockSpec(memory_space=pl.ANY),
        ],
        out_specs=[pl.BlockSpec(memory_space=pltpu.VMEM)] * len(pieces),
        out_shape=[
            jax.ShapeDtypeStruct((high - low, windows, channels), jnp.bfloat16) for _, low, high in pieces
        ],
        scratch_shapes=[
            pltpu.VMEM((LANES * PITCH, 2 * columns), jnp.float32),
            pltpu.VMEM((2 * columns * PITCH, LANES), jnp.float32),
            pltpu.VMEM((halves, channels, WIN_ROWS, samples), jnp.bfloat16),
            pltpu.VMEM((2, samples, 2 * columns), jnp.bfloat16),
            pltpu.SemaphoreType.DMA((halves, steps, 2)),
        ],
        compiler_params=pltpu.CompilerParams(vmem_limit_bytes=VMEM_BYTES),
        cost_estimate=pl.CostEstimate(flops=flops, bytes_accessed=traces.size * 2, transcendentals=0),
        name="spectra",
    )(lax.axis_index("win").reshape(1), traces)


def cut(found, low, high):
    cuts = {}
    for at, parts in found.items():
        cuts[at], start = [], 0
        for part in parts:
            first, last = max(low, start), min(high, start + part.shape[0])
            if first < last:
                cuts[at].append((part, first - start, last - first))
            start += part.shape[0]
    return cuts


def pick_kernel(places, far_ref, *refs):
    out_ref = refs[-1]
    for r in range(ROUNDS):
        for at in places:

            @pl.when(far_ref[r] == at)
            def _():
                row = 0
                for n, first, count in places[at]:
                    out_ref[r, row : row + count] = refs[n][first : first + count]
                    row += count


def pick(cuts, far):
    arrays, places = [], {at: [] for at in sorted(cuts[0])}
    for chunk in cuts:
        for at in places:
            for part, first, count in chunk[at]:
                places[at].append((len(arrays), first, count))
                arrays.append(part)
    rows = sum(count for _, _, count in places[0])
    whole = pl.BlockSpec(memory_space=pltpu.VMEM)
    return pl.pallas_call(
        functools.partial(pick_kernel, places),
        in_specs=[pl.BlockSpec(memory_space=pltpu.SMEM)] + [whole] * len(arrays),
        out_specs=whole,
        out_shape=jax.ShapeDtypeStruct((ROUNDS, rows, *arrays[0].shape[1:]), jnp.bfloat16),
        compiler_params=pltpu.CompilerParams(vmem_limit_bytes=VMEM_BYTES),
        name="pick",
    )(far, *arrays)


def left_kernel(*refs):
    own, out_ref = refs[:-1], refs[-1]
    channels = out_ref.shape[1] // 2

    @pl.loop(0, out_ref.shape[0])
    def _(bin_no):
        straight, turned = [], []
        for source in own:
            real, imag = source[2 * bin_no], source[2 * bin_no + 1]
            straight += [real, imag]
            turned += [imag, -real]
        out_ref[bin_no, :channels] = jnp.concatenate(straight, axis=0).T
        out_ref[bin_no, channels:] = jnp.concatenate(turned, axis=0).T


def left_side(own, windows):
    rows, _, channels = own[0].shape
    whole = pl.BlockSpec(memory_space=pltpu.VMEM)
    return pl.pallas_call(
        left_kernel,
        in_specs=[whole] * len(own),
        out_specs=whole,
        out_shape=jax.ShapeDtypeStruct((rows // 2, 2 * channels, 2 * windows), jnp.bfloat16),
        compiler_params=pltpu.CompilerParams(vmem_limit_bytes=VMEM_BYTES),
        name="left_side",
    )(*own)


def correlate_kernel(scale, first_bin, layout, far_ref, left_ref, *refs):
    out_hbm, right_ref, result_ref, sems = refs[-4:]
    bins, _, _, channels, _ = result_ref.shape
    rows = right_ref.shape[2]
    for r in range(ROUNDS):
        far = far_ref[r]

        @pl.when(far % 2 == 1)
        def _():
            for c, ((n, first), _) in enumerate(layout):
                right_ref[r, c] = refs[n][r, first : first + rows]

        for at in layout[0][1]:

            @pl.when(far == at)
            def _():
                for c, (_, by_key) in enumerate(layout):
                    row = 0
                    for n, first, count in by_key[at]:
                        right_ref[r, c, row : row + count] = refs[n][first : first + count]
                        row += count

    def send(bin_no, r):
        target = out_hbm.at[r, first_bin + bin_no]
        return pltpu.make_async_copy(result_ref.at[bin_no, r], target, sems.at[bin_no, r])

    @pl.loop(0, bins)
    def _(bin_no):
        for r in range(ROUNDS):
            right = jnp.concatenate(
                [right_ref[r, c, 2 * bin_no + part] for c in range(len(layout)) for part in range(2)], axis=0
            )
            product = jnp.dot(left_ref[first_bin + bin_no], right, preferred_element_type=jnp.float32)
            result_ref[bin_no, r] = (product * scale).reshape(2, channels, channels)
            send(bin_no, r).start()

    @pl.loop(0, bins)
    def _(bin_no):
        for r in range(ROUNDS):
            send(bin_no, r).wait()


def correlate(far, left, other, found, first_bin, bins, result):
    bins_dev, both, depth = left.shape
    channels = both // 2
    low, high = 2 * first_bin, 2 * (first_bin + bins)
    arrays, layout = [], []

    def cover(parts):
        taken, start = [], 0
        for part in parts:
            stop = start + part.shape[0]
            first, last = max(low, start), min(high, stop)
            if first < last:
                taken.append((len(arrays), first - start, last - first))
                arrays.append(part)
            start = stop
        return taken

    across = [array for array, _ in other]
    kept = [n for n, array in enumerate(across) if not any(array is seen for seen in across[:n])]
    arrays += [across[n] for n in kept]
    for chunk, (array, first) in zip(found, other):
        n = [array is across[m] for m in kept].index(True)
        layout.append(((n, first), {at: cover(chunk[at]) for at in sorted(chunk) if at}))
    windows_dev = found[0][0][0].shape[1]
    before = [] if result is None else [result]
    whole = pl.BlockSpec(memory_space=pltpu.VMEM)
    shape = (ROUNDS, bins_dev, 2, channels, channels)
    flops = 4 * ROUNDS * bins * depth * channels * channels
    bytes_out = 4 * ROUNDS * bins * 2 * channels * channels
    scale = 1.0 / math.sqrt(depth // 2)

    return pl.pallas_call(
        functools.partial(correlate_kernel, scale, first_bin, layout),
        in_specs=[pl.BlockSpec(memory_space=pltpu.SMEM)]
        + [whole] * (1 + len(arrays))
        + [pl.BlockSpec(memory_space=pl.ANY)] * len(before),
        out_specs=pl.BlockSpec(memory_space=pl.ANY),
        out_shape=jax.ShapeDtypeStruct(shape, jnp.float32),
        scratch_shapes=[
            pltpu.VMEM((ROUNDS, len(layout), 2 * bins, windows_dev, channels), jnp.bfloat16),
            pltpu.VMEM((bins, ROUNDS, 2, channels, channels), jnp.float32),
            pltpu.SemaphoreType.DMA((bins, ROUNDS)),
        ],
        input_output_aliases={2 + len(arrays): 0} if before else {},
        compiler_params=pltpu.CompilerParams(vmem_limit_bytes=VMEM_BYTES),
        cost_estimate=pl.CostEstimate(flops=flops, bytes_accessed=bytes_out, transcendentals=0),
        name="cross_spectra",
    )(far, left, *arrays, *before)


def partner_positions(partner, block_ids, count):
    slots = jnp.arange(count, dtype=jnp.int32)
    holder = jnp.sum(jnp.where(block_ids[None, :] == slots[:, None], slots[None, :], 0), axis=1)
    at_block = block_ids[:, None] == slots[None, :]
    wanted = jnp.sum(jnp.where(at_block[None], partner[:, None, :], 0), axis=2)
    return jnp.sum(jnp.where(wanted[:, :, None] == slots, holder, 0), axis=2)


def swap(value, axis, distance):
    count = lax.axis_size(axis)
    return lax.ppermute(value, axis, [(i, i ^ distance) for i in range(count)])


def after(value, *others):
    return lax.optimization_barrier((value, *others))[0] if others else value


def gather_even(piece):
    pair_count = lax.axis_size("pair")
    half = piece.shape[0] // 2
    found = {0: [piece]}
    for distance in range(2, pair_count, 2):
        if distance != 6:
            found[distance] = [swap(piece, "pair", distance)]
    if 6 < pair_count:
        found[6] = [swap(found[4][0][:half], "pair", 2), swap(found[2][0][half:], "pair", 4)]
    return found


def local(traces, partner, block_ids):
    pair_count = lax.axis_size("pair")
    win_count = lax.axis_size("win")
    rows = 2 * BINS // win_count
    windows = traces.shape[1] * win_count
    me = lax.axis_index("pair")
    slots = jnp.arange(pair_count, dtype=jnp.int32)
    paired = partner_positions(partner, block_ids, pair_count)
    mine = jnp.sum(jnp.where(slots == me, paired, 0), axis=1) ^ me
    beside = jnp.sum(jnp.where(slots == (me ^ 1), paired, 0), axis=1) ^ me

    sent = local_spectra(traces, win_count, [(s, 0, rows) for s in range(win_count)])
    own, found = [], []
    for s, piece in enumerate(sent):
        if s:
            piece = swap(after(piece, own[2]) if s == 3 else piece, "win", s)
        own.append(piece)
    for s, piece in enumerate(own):
        if s >= 2:
            near = [part for at in (2, 4) for part in found[s - 1].get(at, [])]
            piece = after(piece, *near, *found[s - 2].get(6, []))
        found.append(gather_even(piece))
    left = left_side(own, windows)
    half, bins = rows // 2, rows // 2
    waited = after(beside, left)
    early = [swap(pick([cut(chunk, 0, rows)], waited), "pair", 1) for chunk in found[:-2]]
    late = [
        swap(pick([cut(chunk, at, at + half) for chunk in found[-2:]], beside), "pair", 1)
        for at in (0, half)
    ]
    result = None
    for part, (low, count) in enumerate(((0, bins // 2), (bins // 2, bins - bins // 2))):
        other = [(array, 2 * low) for array in early] + [(late[part], 0), (late[part], half)]
        result = correlate(mine, left, other, found, low, count, result)
    return result


def solution(mesh):
    placed = (P("pair", "win", None), P(), P())
    return jax.shard_map(
        local,
        mesh=mesh,
        in_specs=placed,
        out_specs=P(None, "win", None, "pair", None),
        check_vma=False,
    )
```

time: 67 us -> 65.9 us (0.984)
  local copies, waits for them, and re-layouts: 1.78 us -> 0.74 us
  waiting for transfers between devices: 16.5 us -> 15.5 us
    unnamed x6 -> x4, local copies, waits for them, and re-layouts: 1.05 us -> 0.01 us
    ppermute x23, waiting for transfers between devices: 16.5 us -> 15.5 us  [swap(): return lax.ppermute(value, axis, [(i, i ^ distance) for i in range(count)])]
    pallas_call x7 -> x8, Pallas kernels: 17.3 us -> 17.8 us  [the longest x1 8.27 us: local_spectra(): pl.pallas_call(functools.partial(spectra_kernel, chan_rows, win_count, pi...]
  transfers between devices with their start and end apart: 23 -> 23, of which waited for: 7 -> 6; matrix products, arithmetic and copies ran while one was open for 2% -> 2% of each run, Pallas kernels for 5% -> 10%
where the time goes in v3:
time: 65.9 us; the launch traced here: 65.7 us
  starting transfers between devices  30.8 us (47%)
  Pallas kernels  17.8 us (27%)
  waiting for transfers between devices  15.5 us (24%)
  local copies, waits for them, and re-layouts  0.74 us (1%)
  other arithmetic  0.7 us (1%)
    ppermute x23, starting transfers between devices, swap(): return lax.ppermute(value, axis, [(i, i ^ distance) for i in range(count)])  30.8 us
    ppermute x23, waiting for transfers between devices, swap(): return lax.ppermute(value, axis, [(i, i ^ distance) for i in range(count)])  15.5 us
    pallas_call x1, Pallas kernels, local_spectra(): pl.pallas_call(functools.partial(spectra_kernel, chan_rows, win_count, pi...  8.27 us
    pallas_call x2, Pallas kernels, correlate(): pl.pallas_call(functools.partial(correlate_kernel, scale, first_bin, layo...  6.06 us
    pallas_call x4, Pallas kernels, pick(): pl.pallas_call(functools.partial(pick_kernel, places), in_specs=[pl.Block...  2.53 us
  transfers between devices with their start and end apart: 23, of which 6 were waited for; matrix products, arithmetic and copies ran while one was open for 2% of the time, Pallas kernels for 10%

profile of v3, /device:TPU:0, one launch (start us, length us, event | category | flops | bytes accessed | tf_op | source)
XLA Modules:
  0.0 65.7 jit_solution(11016699131967020807)
XLA Ops:
  0.0 8.3 %spectra.1 = (bf16[16,32,256]{2,1,0:T(8,128)(2,1)S(1)}, bf16[16,32,256]{2,1,0:T(8,128)(2,1)S(1)}, bf16[16,32,256]{2,1,0:T(8,128)(2,1)S(1)}, bf16[16,32,256]{2,1,0:T(8,128)(2,1)S(1)}) custom-call(s32[1]{0:T(128)} %bitcast.win_ref, bf16[256,32,1024]{2,1,0:T(8,128)(2,1)} %traces_ref.1), custom_call_target="tpu_custom_call" | custom-call | flops 1073741824 | bytes 16777216 | tf_op jit(solution)/shard_map/spectra/pallas_call | solution.py:105
  8.3 3.1 %collective-permute-start = (bf16[16,32,256]{2,1,0:T(8,128)(2,1)S(1)}, bf16[16,32,256]{2,1,0:T(8,128)(2,1)S(1)}, u32[]{:S(2)}, u32[]{:S(2)}) collective-permute-start(bf16[16,32,256]{2,1,0:T(8,128)(2,1)S(1)} %get-tuple-element.14), channel_id=1, source_target_pairs={{0,1},{1,0},{2,3},{3,2},{4,5},{5,4},{6,7},{7,6},{8,9},{9,8},{10,11... | collective-permute-start | bytes 786440 | tf_op jit(solution)/shard_map/ppermute | solution.py:302
  11.4 1.5 %collective-permute-start.4 = (bf16[16,32,256]{2,1,0:T(8,128)(2,1)S(1)}, bf16[16,32,256]{2,1,0:T(8,128)(2,1)S(1)}, u32[]{:S(2)}, u32[]{:S(2)}) collective-permute-start(bf16[16,32,256]{2,1,0:T(8,128)(2,1)S(1)} %get-tuple-element.13.refs_0_), channel_id=1, source_target_pairs={{0,16},{4,20},{8,24},{12,28},{16,0},{20,4},{24,8},{28,12},{1,17},{... | collective-permute-start | bytes 786440 | tf_op jit(solution)/shard_map/ppermute | solution.py:302
  12.9 1.5 %collective-permute-start.3 = (bf16[16,32,256]{2,1,0:T(8,128)(2,1)S(1)}, bf16[16,32,256]{2,1,0:T(8,128)(2,1)S(1)}, u32[]{:S(2)}, u32[]{:S(2)}) collective-permute-start(bf16[16,32,256]{2,1,0:T(8,128)(2,1)S(1)} %get-tuple-element.13.refs_0_), channel_id=1, source_target_pairs={{0,8},{4,12},{8,0},{12,4},{16,24},{20,28},{24,16},{28,20},{1,9},{5... | collective-permute-start | bytes 786440 | tf_op jit(solution)/shard_map/ppermute | solution.py:302
  14.4 2.6 %collective-permute-start.1 = (bf16[16,32,256]{2,1,0:T(8,128)(2,1)S(1)}, bf16[16,32,256]{2,1,0:T(8,128)(2,1)S(1)}, u32[]{:S(2)}, u32[]{:S(2)}) collective-permute-start(bf16[16,32,256]{2,1,0:T(8,128)(2,1)S(1)} %get-tuple-element.15), channel_id=1, source_target_pairs={{0,2},{1,3},{2,0},{3,1},{4,6},{5,7},{6,4},{7,5},{8,10},{9,11},{10,... | collective-permute-start | bytes 786440 | tf_op jit(solution)/shard_map/ppermute | solution.py:302
  17.0 3.3 %collective-permute-done.refs_1_.refs_0_ = bf16[16,32,256]{2,1,0:T(8,128)(2,1)S(1)} collective-permute-done((bf16[16,32,256]{2,1,0:T(8,128)(2,1)S(1)}, bf16[16,32,256]{2,1,0:T(8,128)(2,1)S(1)}, u32[]{:S(2)}, u32[]{:S(2)}) %collective-permute-start) | collective-permute-done | bytes 262176 | tf_op jit(solution)/shard_map/ppermute | solution.py:302
  20.2 3.2 %collective-permute-start.9 = (bf16[16,32,256]{2,1,0:T(8,128)(2,1)S(1)}, bf16[16,32,256]{2,1,0:T(8,128)(2,1)S(1)}, u32[]{:S(2)}, u32[]{:S(2)}) collective-permute-start(bf16[16,32,256]{2,1,0:T(8,128)(2,1)S(1)} %collective-permute-done.refs_1_.refs_0_), channel_id=1, source_target_pairs={{0,16},{4,20},{8,24},{12,28},{16,0},{20,4},{24,8},{28,12},{1,17},{... | collective-permute-start | bytes 786440 | tf_op jit(solution)/shard_map/ppermute | solution.py:302
  23.4 2.4 %collective-permute-start.8 = (bf16[16,32,256]{2,1,0:T(8,128)(2,1)S(1)}, bf16[16,32,256]{2,1,0:T(8,128)(2,1)S(1)}, u32[]{:S(2)}, u32[]{:S(2)}) collective-permute-start(bf16[16,32,256]{2,1,0:T(8,128)(2,1)S(1)} %collective-permute-done.refs_1_.refs_0_), channel_id=1, source_target_pairs={{0,8},{4,12},{8,0},{12,4},{16,24},{20,28},{24,16},{28,20},{1,9},{5... | collective-permute-start | bytes 786440 | tf_op jit(solution)/shard_map/ppermute | solution.py:302
  26.1 2.1 %collective-permute-done.1.refs_2_.refs_0_ = bf16[16,32,256]{2,1,0:T(8,128)(2,1)S(1)} collective-permute-done((bf16[16,32,256]{2,1,0:T(8,128)(2,1)S(1)}, bf16[16,32,256]{2,1,0:T(8,128)(2,1)S(1)}, u32[]{:S(2)}, u32[]{:S(2)}) %collective-permute-start.1) | collective-permute-done | bytes 262176 | tf_op jit(solution)/shard_map/ppermute | solution.py:302
  28.1 3.4 %collective-permute-start.2 = (bf16[16,32,256]{2,1,0:T(8,128)(2,1)S(1)}, bf16[16,32,256]{2,1,0:T(8,128)(2,1)S(1)}, u32[]{:S(2)}, u32[]{:S(2)}) collective-permute-start(bf16[16,32,256]{2,1,0:T(8,128)(2,1)S(1)} %get-tuple-element.17), channel_id=1, source_target_pairs={{0,3},{1,2},{2,1},{3,0},{4,7},{5,6},{6,5},{7,4},{8,11},{9,10},{10,... | collective-permute-start | bytes 786440 | tf_op jit(solution)/shard_map/ppermute | solution.py:302
  31.6 2.2 %collective-permute-done.5.refs_3_.refs_5_ = bf16[8,32,256]{2,1,0:T(8,128)(2,1)S(1)} collective-permute-done((bf16[8,32,256]{2,1,0:T(8,128)(2,1)S(1)}, bf16[8,32,256]{2,1,0:T(8,128)(2,1)S(1)}, u32[]{:S(2)}, u32[]{:S(2)}) %collective-permute-start.5) | collective-permute-done | bytes 131104 | tf_op jit(solution)/shard_map/ppermute | solution.py:302
  34.2 1.7 %collective-permute-start.13 = (bf16[16,32,256]{2,1,0:T(8,128)(2,1)S(1)}, bf16[16,32,256]{2,1,0:T(8,128)(2,1)S(1)}, u32[]{:S(2)}, u32[]{:S(2)}) collective-permute-start(bf16[16,32,256]{2,1,0:T(8,128)(2,1)S(1)} %collective-permute-done.1.refs_2_.refs_0_), channel_id=1, source_target_pairs={{0,8},{4,12},{8,0},{12,4},{16,24},{20,28},{24,16},{28,20},{1,9},{5... | collective-permute-start | bytes 786440 | tf_op jit(solution)/shard_map/ppermute | solution.py:302
  36.4 0.7 %slice.35 = bf16[8,32,256]{2,1,0:T(8,128)(2,1)} slice(bf16[16,32,256]{2,1,0:T(8,128)(2,1)S(1)} %collective-permute-done.8.refs_1_.refs_6_), slice={[8:16], [0:32], [0:256]} | slice | bytes 262144 | tf_op jit(solution)/shard_map/slice | solution.py:317
  37.0 1.7 %collective-permute-start.11 = (bf16[8,32,256]{2,1,0:T(8,128)(2,1)}, bf16[8,32,256]{2,1,0:T(8,128)(2,1)S(1)}, u32[]{:S(2)}, u32[]{:S(2)}) collective-permute-start(bf16[8,32,256]{2,1,0:T(8,128)(2,1)} %slice.35), channel_id=1, source_target_pairs={{0,16},{4,20},{8,24},{12,28},{16,0},{20,4},{24,8},{28,12},{1,17},{... | collective-permute-start | bytes 393224 | tf_op jit(solution)/shard_map/ppermute | solution.py:302
  39.1 4.2 %collective-permute-done.10.refs_3_.refs_8_ = bf16[8,32,256]{2,1,0:T(8,128)(2,1)S(1)} collective-permute-done((bf16[8,32,256]{2,1,0:T(8,128)(2,1)S(1)}, bf16[8,32,256]{2,1,0:T(8,128)(2,1)S(1)}, u32[]{:S(2)}, u32[]{:S(2)}) %collective-permute-start.10) | collective-permute-done | bytes 131104 | tf_op jit(solution)/shard_map/ppermute | solution.py:302
  43.3 1.5 %collective-permute-start.17 = (bf16[16,32,256]{2,1,0:T(8,128)(2,1)S(1)}, bf16[16,32,256]{2,1,0:T(8,128)(2,1)S(1)}, u32[]{:S(2)}, u32[]{:S(2)}) collective-permute-start(bf16[16,32,256]{2,1,0:T(8,128)(2,1)S(1)} %collective-permute-done.2.refs_3_.refs_4_), channel_id=1, source_target_pairs={{0,16},{4,20},{8,24},{12,28},{16,0},{20,4},{24,8},{28,12},{1,17},{... | collective-permute-start | bytes 786440 | tf_op jit(solution)/shard_map/ppermute | solution.py:302
  44.8 1.6 %collective-permute-start.16 = (bf16[16,32,256]{2,1,0:T(8,128)(2,1)S(1)}, bf16[16,32,256]{2,1,0:T(8,128)(2,1)S(1)}, u32[]{:S(2)}, u32[]{:S(2)}) collective-permute-start(bf16[16,32,256]{2,1,0:T(8,128)(2,1)S(1)} %collective-permute-done.2.refs_3_.refs_4_), channel_id=1, source_target_pairs={{0,8},{4,12},{8,0},{12,4},{16,24},{20,28},{24,16},{28,20},{1,9},{5... | collective-permute-start | bytes 786440 | tf_op jit(solution)/shard_map/ppermute | solution.py:302
  46.8 0.5 collective-permute-start.20
  47.3 0.6 collective-permute-start.15
  47.9 3.0 %collective-permute-done.17.refs_6_.refs_13_ = bf16[16,32,256]{2,1,0:T(8,128)(2,1)S(1)} collective-permute-done((bf16[16,32,256]{2,1,0:T(8,128)(2,1)S(1)}, bf16[16,32,256]{2,1,0:T(8,128)(2,1)S(1)}, u32[]{:S(2)}, u32[]{:S(2)}) %collective-permute-start.17) | collective-permute-done | bytes 262176 | tf_op jit(solution)/shard_map/ppermute | solution.py:302
  50.9 1.7 %collective-permute-start.21 = (bf16[8,32,256]{2,1,0:T(8,128)(2,1)S(1)}, bf16[8,32,256]{2,1,0:T(8,128)(2,1)S(1)}, u32[]{:S(2)}, u32[]{:S(2)}) collective-permute-start(bf16[8,32,256]{2,1,0:T(8,128)(2,1)S(1)} %slice.39), channel_id=1, source_target_pairs={{0,8},{4,12},{8,0},{12,4},{16,24},{20,28},{24,16},{28,20},{1,9},{5... | collective-permute-start | bytes 393224 | tf_op jit(solution)/shard_map/ppermute | solution.py:302
  52.6 1.5 %collective-permute-start.18 = (bf16[8,32,256]{2,1,0:T(8,128)(2,1)S(1)}, bf16[8,32,256]{2,1,0:T(8,128)(2,1)S(1)}, u32[]{:S(2)}, u32[]{:S(2)}) collective-permute-start(bf16[8,32,256]{2,1,0:T(8,128)(2,1)S(1)} %slice.37), channel_id=1, source_target_pairs={{0,16},{4,20},{8,24},{12,28},{16,0},{20,4},{24,8},{28,12},{1,17},{... | collective-permute-start | bytes 393224 | tf_op jit(solution)/shard_map/ppermute | solution.py:302
  54.2 1.0 %left_side.1.left_ref = bf16[8,512,256]{2,1,0:T(8,128)(2,1)S(1)} custom-call(bf16[16,32,256]{2,1,0:T(8,128)(2,1)S(1)} %get-tuple-element.13.refs_0_, bf16[16,32,256]{2,1,0:T(8,128)(2,1)S(1)} %collective-permute-done.refs_1_.refs_0_, bf16[16,32,256]{2,1,0:T(8,128)(2,1)S(1)} %collective-permute-done.1.refs_2_.refs_0_, ...), custom_call_target="tpu_custom_call" | custom-call | tf_op jit(solution)/shard_map/left_side/pallas_call | solution.py:190
  55.1 0.6 pick.4
  55.9 0.6 pick.5
  56.5 0.5 collective-permute-start.12
  57.1 0.6 pick.7
  57.8 0.6 pick.6
  58.4 0.5 collective-permute-start.19
  59.0 0.7 %collective-permute-done.22.refs_2_ = bf16[2,16,32,256]{3,2,1,0:T(8,128)(2,1)S(1)} collective-permute-done((bf16[2,16,32,256]{3,2,1,0:T(8,128)(2,1)S(1)}, bf16[2,16,32,256]{3,2,1,0:T(8,128)(2,1)S(1)}, u32[]{:S(2)}, u32[]{:S(2)}) %collective-permute-start.22) | collective-permute-done | bytes 524320 | tf_op jit(solution)/shard_map/ppermute | solution.py:302
  59.7 3.0 %cross_spectra.2.refs_15_ = f32[2,8,2,256,256]{4,3,2,1,0:T(8,128)} custom-call(s32[2]{0:T(128)S(1)} %broadcast_xor_fusion.1.far_ref, bf16[8,512,256]{2,1,0:T(8,128)(2,1)S(1)} %left_side.1.left_ref, bf16[2,16,32,256]{3,2,1,0:T(8,128)(2,1)S(1)} %collective-permute-done.7.refs_0_, bf16[2,16,32,256]{3,2,1,0:T(8,128)(2,1)S(1)} %collective-permute-done.12.refs_1_, ...), custom_call_target="tpu_custom_call" | custom-call | flops 536870912 | bytes 4194304 | tf_op jit(solution)/shard_map/cross_spectra/pallas_call | solution.py:273
  62.7 3.0 %cross_spectra.3 = f32[2,8,2,256,256]{4,3,2,1,0:T(8,128)} custom-call(s32[2]{0:T(128)S(1)} %broadcast_xor_fusion.1.far_ref, bf16[8,512,256]{2,1,0:T(8,128)(2,1)S(1)} %left_side.1.left_ref, bf16[2,16,32,256]{3,2,1,0:T(8,128)(2,1)S(1)} %collective-permute-done.7.refs_0_, ...), custom_call_target="tpu_custom_call", output_to_operand_aliasing={{}: (17, {})} | custom-call | flops 536870912 | bytes 4194304 | tf_op jit(solution)/shard_map/cross_spectra/pallas_call | solution.py:273
  (42 shorter events, 1.8 us)
Async XLA Ops:
  0.0 35.9 %copy-start.1 = (s32[8]{0:T(128)S(1)}, s32[8]{0:T(128)}, u32[]{:S(2)}) copy-start(s32[8]{0:T(128)} %param.5) | copy-start | bytes 100
  0.0 38.9 %copy-start = (s32[2,8]{1,0:T(2,128)S(1)}, s32[2,8]{1,0:T(2,128)}, u32[]{:S(2)}) copy-start(s32[2,8]{1,0:T(2,128)} %param.4) | copy-start | bytes 196
  8.3 12.0 %collective-permute-start = (bf16[16,32,256]{2,1,0:T(8,128)(2,1)S(1)}, bf16[16,32,256]{2,1,0:T(8,128)(2,1)S(1)}, u32[]{:S(2)}, u32[]{:S(2)}) collective-permute-start(bf16[16,32,256]{2,1,0:T(8,128)(2,1)S(1)} %get-tuple-element.14), channel_id=1, source_target_pairs={{0,1},{1,0},{2,3},{3,2},{4,5},{5,4},{6,7},{7,6},{8,9},{9,8},{10,11... | collective-permute-start | bytes 786440 | tf_op jit(solution)/shard_map/ppermute | solution.py:302
  11.4 14.5 %collective-permute-start.4 = (bf16[16,32,256]{2,1,0:T(8,128)(2,1)S(1)}, bf16[16,32,256]{2,1,0:T(8,128)(2,1)S(1)}, u32[]{:S(2)}, u32[]{:S(2)}) collective-permute-start(bf16[16,32,256]{2,1,0:T(8,128)(2,1)S(1)} %get-tuple-element.13.refs_0_), channel_id=1, source_target_pairs={{0,16},{4,20},{8,24},{12,28},{16,0},{20,4},{24,8},{28,12},{1,17},{... | collective-permute-start | bytes 786440 | tf_op jit(solution)/shard_map/ppermute | solution.py:302
  12.9 13.1 %collective-permute-start.3 = (bf16[16,32,256]{2,1,0:T(8,128)(2,1)S(1)}, bf16[16,32,256]{2,1,0:T(8,128)(2,1)S(1)}, u32[]{:S(2)}, u32[]{:S(2)}) collective-permute-start(bf16[16,32,256]{2,1,0:T(8,128)(2,1)S(1)} %get-tuple-element.13.refs_0_), channel_id=1, source_target_pairs={{0,8},{4,12},{8,0},{12,4},{16,24},{20,28},{24,16},{28,20},{1,9},{5... | collective-permute-start | bytes 786440 | tf_op jit(solution)/shard_map/ppermute | solution.py:302
  14.4 13.8 %collective-permute-start.1 = (bf16[16,32,256]{2,1,0:T(8,128)(2,1)S(1)}, bf16[16,32,256]{2,1,0:T(8,128)(2,1)S(1)}, u32[]{:S(2)}, u32[]{:S(2)}) collective-permute-start(bf16[16,32,256]{2,1,0:T(8,128)(2,1)S(1)} %get-tuple-element.15), channel_id=1, source_target_pairs={{0,2},{1,3},{2,0},{3,1},{4,6},{5,7},{6,4},{7,5},{8,10},{9,11},{10,... | collective-permute-start | bytes 786440 | tf_op jit(solution)/shard_map/ppermute | solution.py:302
  20.2 13.6 %collective-permute-start.9 = (bf16[16,32,256]{2,1,0:T(8,128)(2,1)S(1)}, bf16[16,32,256]{2,1,0:T(8,128)(2,1)S(1)}, u32[]{:S(2)}, u32[]{:S(2)}) collective-permute-start(bf16[16,32,256]{2,1,0:T(8,128)(2,1)S(1)} %collective-permute-done.refs_1_.refs_0_), channel_id=1, source_target_pairs={{0,16},{4,20},{8,24},{12,28},{16,0},{20,4},{24,8},{28,12},{1,17},{... | collective-permute-start | bytes 786440 | tf_op jit(solution)/shard_map/ppermute | solution.py:302
  23.4 10.4 %collective-permute-start.8 = (bf16[16,32,256]{2,1,0:T(8,128)(2,1)S(1)}, bf16[16,32,256]{2,1,0:T(8,128)(2,1)S(1)}, u32[]{:S(2)}, u32[]{:S(2)}) collective-permute-start(bf16[16,32,256]{2,1,0:T(8,128)(2,1)S(1)} %collective-permute-done.refs_1_.refs_0_), channel_id=1, source_target_pairs={{0,8},{4,12},{8,0},{12,4},{16,24},{20,28},{24,16},{28,20},{1,9},{5... | collective-permute-start | bytes 786440 | tf_op jit(solution)/shard_map/ppermute | solution.py:302
  25.9 7.9 %collective-permute-start.5 = (bf16[8,32,256]{2,1,0:T(8,128)(2,1)S(1)}, bf16[8,32,256]{2,1,0:T(8,128)(2,1)S(1)}, u32[]{:S(2)}, u32[]{:S(2)}) collective-permute-start(bf16[8,32,256]{2,1,0:T(8,128)(2,1)S(1)} %slice.32), channel_id=1, source_target_pairs={{0,8},{4,12},{8,0},{12,4},{16,24},{20,28},{24,16},{28,20},{1,9},{5... | collective-permute-start | bytes 393224 | tf_op jit(solution)/shard_map/ppermute | solution.py:302
  26.0 7.8 %collective-permute-start.6 = (bf16[8,32,256]{2,1,0:T(8,128)(2,1)S(1)}, bf16[8,32,256]{2,1,0:T(8,128)(2,1)S(1)}, u32[]{:S(2)}, u32[]{:S(2)}) collective-permute-start(bf16[8,32,256]{2,1,0:T(8,128)(2,1)S(1)} %slice.33), channel_id=1, source_target_pairs={{0,16},{4,20},{8,24},{12,28},{16,0},{20,4},{24,8},{28,12},{1,17},{... | collective-permute-start | bytes 393224 | tf_op jit(solution)/shard_map/ppermute | solution.py:302
  28.1 10.9 %collective-permute-start.2 = (bf16[16,32,256]{2,1,0:T(8,128)(2,1)S(1)}, bf16[16,32,256]{2,1,0:T(8,128)(2,1)S(1)}, u32[]{:S(2)}, u32[]{:S(2)}) collective-permute-start(bf16[16,32,256]{2,1,0:T(8,128)(2,1)S(1)} %get-tuple-element.17), channel_id=1, source_target_pairs={{0,3},{1,2},{2,1},{3,0},{4,7},{5,6},{6,5},{7,4},{8,11},{9,10},{10,... | collective-permute-start | bytes 786440 | tf_op jit(solution)/shard_map/ppermute | solution.py:302
  33.8 9.4 %collective-permute-start.14 = (bf16[16,32,256]{2,1,0:T(8,128)(2,1)S(1)}, bf16[16,32,256]{2,1,0:T(8,128)(2,1)S(1)}, u32[]{:S(2)}, u32[]{:S(2)}) collective-permute-start(bf16[16,32,256]{2,1,0:T(8,128)(2,1)S(1)} %collective-permute-done.1.refs_2_.refs_0_), channel_id=1, source_target_pairs={{0,16},{4,20},{8,24},{12,28},{16,0},{20,4},{24,8},{28,12},{1,17},{... | collective-permute-start | bytes 786440 | tf_op jit(solution)/shard_map/ppermute | solution.py:302
  34.2 9.1 %collective-permute-start.13 = (bf16[16,32,256]{2,1,0:T(8,128)(2,1)S(1)}, bf16[16,32,256]{2,1,0:T(8,128)(2,1)S(1)}, u32[]{:S(2)}, u32[]{:S(2)}) collective-permute-start(bf16[16,32,256]{2,1,0:T(8,128)(2,1)S(1)} %collective-permute-done.1.refs_2_.refs_0_), channel_id=1, source_target_pairs={{0,8},{4,12},{8,0},{12,4},{16,24},{20,28},{24,16},{28,20},{1,9},{5... | collective-permute-start | bytes 786440 | tf_op jit(solution)/shard_map/ppermute | solution.py:302
  36.0 7.2 %collective-permute-start.10 = (bf16[8,32,256]{2,1,0:T(8,128)(2,1)S(1)}, bf16[8,32,256]{2,1,0:T(8,128)(2,1)S(1)}, u32[]{:S(2)}, u32[]{:S(2)}) collective-permute-start(bf16[8,32,256]{2,1,0:T(8,128)(2,1)S(1)} %slice.34), channel_id=1, source_target_pairs={{0,8},{4,12},{8,0},{12,4},{16,24},{20,28},{24,16},{28,20},{1,9},{5... | collective-permute-start | bytes 393224 | tf_op jit(solution)/shard_map/ppermute | solution.py:302
  37.0 6.2 %collective-permute-start.11 = (bf16[8,32,256]{2,1,0:T(8,128)(2,1)}, bf16[8,32,256]{2,1,0:T(8,128)(2,1)S(1)}, u32[]{:S(2)}, u32[]{:S(2)}) collective-permute-start(bf16[8,32,256]{2,1,0:T(8,128)(2,1)} %slice.35), channel_id=1, source_target_pairs={{0,16},{4,20},{8,24},{12,28},{16,0},{20,4},{24,8},{28,12},{1,17},{... | collective-permute-start | bytes 393224 | tf_op jit(solution)/shard_map/ppermute | solution.py:302
  43.3 7.6 %collective-permute-start.17 = (bf16[16,32,256]{2,1,0:T(8,128)(2,1)S(1)}, bf16[16,32,256]{2,1,0:T(8,128)(2,1)S(1)}, u32[]{:S(2)}, u32[]{:S(2)}) collective-permute-start(bf16[16,32,256]{2,1,0:T(8,128)(2,1)S(1)} %collective-permute-done.2.refs_3_.refs_4_), channel_id=1, source_target_pairs={{0,16},{4,20},{8,24},{12,28},{16,0},{20,4},{24,8},{28,12},{1,17},{... | collective-permute-start | bytes 786440 | tf_op jit(solution)/shard_map/ppermute | solution.py:302
  44.8 7.8 %collective-permute-start.16 = (bf16[16,32,256]{2,1,0:T(8,128)(2,1)S(1)}, bf16[16,32,256]{2,1,0:T(8,128)(2,1)S(1)}, u32[]{:S(2)}, u32[]{:S(2)}) collective-permute-start(bf16[16,32,256]{2,1,0:T(8,128)(2,1)S(1)} %collective-permute-done.2.refs_3_.refs_4_), channel_id=1, source_target_pairs={{0,8},{4,12},{8,0},{12,4},{16,24},{20,28},{24,16},{28,20},{1,9},{5... | collective-permute-start | bytes 786440 | tf_op jit(solution)/shard_map/ppermute | solution.py:302
  46.8 9.7 %collective-permute-start.20 = (bf16[8,32,256]{2,1,0:T(8,128)(2,1)S(1)}, bf16[8,32,256]{2,1,0:T(8,128)(2,1)S(1)}, u32[]{:S(2)}, u32[]{:S(2)}) collective-permute-start(bf16[8,32,256]{2,1,0:T(8,128)(2,1)S(1)} %slice.38), channel_id=1, source_target_pairs={{0,8},{4,12},{8,0},{12,4},{16,24},{20,28},{24,16},{28,20},{1,9},{5... | collective-permute-start | bytes 393224 | tf_op jit(solution)/shard_map/ppermute | solution.py:302
  47.3 10.5 %collective-permute-start.15 = (bf16[8,32,256]{2,1,0:T(8,128)(2,1)S(1)}, bf16[8,32,256]{2,1,0:T(8,128)(2,1)S(1)}, u32[]{:S(2)}, u32[]{:S(2)}) collective-permute-start(bf16[8,32,256]{2,1,0:T(8,128)(2,1)S(1)} %slice.36), channel_id=1, source_target_pairs={{0,16},{4,20},{8,24},{12,28},{16,0},{20,4},{24,8},{28,12},{1,17},{... | collective-permute-start | bytes 393224 | tf_op jit(solution)/shard_map/ppermute | solution.py:302
  50.9 6.1 %collective-permute-start.21 = (bf16[8,32,256]{2,1,0:T(8,128)(2,1)S(1)}, bf16[8,32,256]{2,1,0:T(8,128)(2,1)S(1)}, u32[]{:S(2)}, u32[]{:S(2)}) collective-permute-start(bf16[8,32,256]{2,1,0:T(8,128)(2,1)S(1)} %slice.39), channel_id=1, source_target_pairs={{0,8},{4,12},{8,0},{12,4},{16,24},{20,28},{24,16},{28,20},{1,9},{5... | collective-permute-start | bytes 393224 | tf_op jit(solution)/shard_map/ppermute | solution.py:302
  52.6 5.2 %collective-permute-start.18 = (bf16[8,32,256]{2,1,0:T(8,128)(2,1)S(1)}, bf16[8,32,256]{2,1,0:T(8,128)(2,1)S(1)}, u32[]{:S(2)}, u32[]{:S(2)}) collective-permute-start(bf16[8,32,256]{2,1,0:T(8,128)(2,1)S(1)} %slice.37), channel_id=1, source_target_pairs={{0,16},{4,20},{8,24},{12,28},{16,0},{20,4},{24,8},{28,12},{1,17},{... | collective-permute-start | bytes 393224 | tf_op jit(solution)/shard_map/ppermute | solution.py:302
  55.8 3.2 %collective-permute-start.7 = (bf16[2,16,32,256]{3,2,1,0:T(8,128)(2,1)S(1)}, bf16[2,16,32,256]{3,2,1,0:T(8,128)(2,1)S(1)}, u32[]{:S(2)}, u32[]{:S(2)}) collective-permute-start(bf16[2,16,32,256]{3,2,1,0:T(8,128)(2,1)S(1)} %pick.4), channel_id=1, source_target_pairs={{0,4},{4,0},{8,12},{12,8},{16,20},{20,16},{24,28},{28,24},{1,5},{5... | collective-permute-start | bytes 1572872 | tf_op jit(solution)/shard_map/ppermute | solution.py:302
  56.5 2.5 %collective-permute-start.12 = (bf16[2,16,32,256]{3,2,1,0:T(8,128)(2,1)S(1)}, bf16[2,16,32,256]{3,2,1,0:T(8,128)(2,1)S(1)}, u32[]{:S(2)}, u32[]{:S(2)}) collective-permute-start(bf16[2,16,32,256]{3,2,1,0:T(8,128)(2,1)S(1)} %pick.5), channel_id=1, source_target_pairs={{0,4},{4,0},{8,12},{12,8},{16,20},{20,16},{24,28},{28,24},{1,5},{5... | collective-permute-start | bytes 1572872 | tf_op jit(solution)/shard_map/ppermute | solution.py:302
  57.7 2.0 %collective-permute-start.22 = (bf16[2,16,32,256]{3,2,1,0:T(8,128)(2,1)S(1)}, bf16[2,16,32,256]{3,2,1,0:T(8,128)(2,1)S(1)}, u32[]{:S(2)}, u32[]{:S(2)}) collective-permute-start(bf16[2,16,32,256]{3,2,1,0:T(8,128)(2,1)S(1)} %pick.7), channel_id=1, source_target_pairs={{0,4},{4,0},{8,12},{12,8},{16,20},{20,16},{24,28},{28,24},{1,5},{5... | collective-permute-start | bytes 1572872 | tf_op jit(solution)/shard_map/ppermute | solution.py:302
  58.4 4.3 %collective-permute-start.19 = (bf16[2,16,32,256]{3,2,1,0:T(8,128)(2,1)S(1)}, bf16[2,16,32,256]{3,2,1,0:T(8,128)(2,1)S(1)}, u32[]{:S(2)}, u32[]{:S(2)}) collective-permute-start(bf16[2,16,32,256]{3,2,1,0:T(8,128)(2,1)S(1)} %pick.6), channel_id=1, source_target_pairs={{0,4},{4,0},{8,12},{12,8},{16,20},{20,16},{24,28},{28,24},{1,5},{5... | collective-permute-start | bytes 1572872 | tf_op jit(solution)/shard_map/ppermute | solution.py:302

commit v4 on v3

--- a/solution.py
+++ b/solution.py
@@ -197,17 +197,20 @@
     )(*own)
 
 
-def correlate_kernel(scale, first_bin, layout, far_ref, left_ref, *refs):
+def correlate_kernel(scale, layout, far_ref, left_ref, *refs):
     out_hbm, right_ref, result_ref, sems = refs[-4:]
     bins, _, _, channels, _ = result_ref.shape
-    rows = right_ref.shape[2]
+
     for r in range(ROUNDS):
         far = far_ref[r]
 
         @pl.when(far % 2 == 1)
         def _():
-            for c, ((n, first), _) in enumerate(layout):
-                right_ref[r, c] = refs[n][r, first : first + rows]
+            for c, (across, _) in enumerate(layout):
+                row = 0
+                for n, first, count in across:
+                    right_ref[r, c, row : row + count] = refs[n][r, first : first + count]
+                    row += count
 
         for at in layout[0][1]:
 
@@ -215,13 +218,13 @@
             def _():
                 for c, (_, by_key) in enumerate(layout):
                     row = 0
-                    for n, first, count in by_key[at]:
-                        right_ref[r, c, row : row + count] = refs[n][first : first + count]
+                    for n in by_key[at]:
+                        count = refs[n].shape[0]
+                        right_ref[r, c, row : row + count] = refs[n][...]
                         row += count
 
     def send(bin_no, r):
-        target = out_hbm.at[r, first_bin + bin_no]
-        return pltpu.make_async_copy(result_ref.at[bin_no, r], target, sems.at[bin_no, r])
+        return pltpu.make_async_copy(result_ref.at[bin_no, r], out_hbm.at[r, bin_no], sems.at[bin_no, r])
 
     @pl.loop(0, bins)
     def _(bin_no):
@@ -229,7 +232,7 @@
             right = jnp.concatenate(
                 [right_ref[r, c, 2 * bin_no + part] for c in range(len(layout)) for part in range(2)], axis=0
             )
-            product = jnp.dot(left_ref[first_bin + bin_no], right, preferred_element_type=jnp.float32)
+            product = jnp.dot(left_ref[bin_no], right, preferred_element_type=jnp.float32)
             result_ref[bin_no, r] = (product * scale).reshape(2, channels, channels)
             send(bin_no, r).start()
 
@@ -239,54 +242,36 @@
             send(bin_no, r).wait()
 
 
-def correlate(far, left, other, found, first_bin, bins, result):
-    bins_dev, both, depth = left.shape
+def correlate(far, left, found, across, other):
+    bins, both, depth = left.shape
     channels = both // 2
-    low, high = 2 * first_bin, 2 * (first_bin + bins)
-    arrays, layout = [], []
-
-    def cover(parts):
-        taken, start = [], 0
-        for part in parts:
-            stop = start + part.shape[0]
-            first, last = max(low, start), min(high, stop)
-            if first < last:
-                taken.append((len(arrays), first - start, last - first))
-                arrays.append(part)
-            start = stop
-        return taken
-
-    across = [array for array, _ in other]
-    kept = [n for n, array in enumerate(across) if not any(array is seen for seen in across[:n])]
-    arrays += [across[n] for n in kept]
-    for chunk, (array, first) in zip(found, other):
-        n = [array is across[m] for m in kept].index(True)
-        layout.append(((n, first), {at: cover(chunk[at]) for at in sorted(chunk) if at}))
-    windows_dev = found[0][0][0].shape[1]
-    before = [] if result is None else [result]
+    arrays, layout = list(across), []
+
+    def numbered(parts):
+        arrays.extend(parts)
+        return list(range(len(arrays) - len(parts), len(arrays)))
+
+    for chunk, parts in zip(found, other):
+        layout.append((parts, {at: numbered(chunk[at]) for at in sorted(chunk) if at}))
+    rows, windows_dev, _ = found[0][0][0].shape
     whole = pl.BlockSpec(memory_space=pltpu.VMEM)
-    shape = (ROUNDS, bins_dev, 2, channels, channels)
+    shape = (ROUNDS, bins, 2, channels, channels)
     flops = 4 * ROUNDS * bins * depth * channels * channels
-    bytes_out = 4 * ROUNDS * bins * 2 * channels * channels
     scale = 1.0 / math.sqrt(depth // 2)
-
     return pl.pallas_call(
-        functools.partial(correlate_kernel, scale, first_bin, layout),
-        in_specs=[pl.BlockSpec(memory_space=pltpu.SMEM)]
-        + [whole] * (1 + len(arrays))
-        + [pl.BlockSpec(memory_space=pl.ANY)] * len(before),
+        functools.partial(correlate_kernel, scale, layout),
+        in_specs=[pl.BlockSpec(memory_space=pltpu.SMEM)] + [whole] * (1 + len(arrays)),
         out_specs=pl.BlockSpec(memory_space=pl.ANY),
         out_shape=jax.ShapeDtypeStruct(shape, jnp.float32),
         scratch_shapes=[
-            pltpu.VMEM((ROUNDS, len(layout), 2 * bins, windows_dev, channels), jnp.bfloat16),
+            pltpu.VMEM((ROUNDS, len(layout), rows, windows_dev, channels), jnp.bfloat16),
             pltpu.VMEM((bins, ROUNDS, 2, channels, channels), jnp.float32),
             pltpu.SemaphoreType.DMA((bins, ROUNDS)),
         ],
-        input_output_aliases={2 + len(arrays): 0} if before else {},
         compiler_params=pltpu.CompilerParams(vmem_limit_bytes=VMEM_BYTES),
-        cost_estimate=pl.CostEstimate(flops=flops, bytes_accessed=bytes_out, transcendentals=0),
+        cost_estimate=pl.CostEstimate(flops=flops, bytes_accessed=4 * math.prod(shape), transcendentals=0),
         name="cross_spectra",
-    )(far, left, *arrays, *before)
+    )(far, left, *arrays)
 
 
 def partner_positions(partner, block_ids, count):
@@ -306,14 +291,14 @@
     return lax.optimization_barrier((value, *others))[0] if others else value
 
 
-def gather_even(piece):
+def gather_even(piece, relay):
     pair_count = lax.axis_size("pair")
     half = piece.shape[0] // 2
     found = {0: [piece]}
     for distance in range(2, pair_count, 2):
-        if distance != 6:
+        if distance != 6 or not relay:
             found[distance] = [swap(piece, "pair", distance)]
-    if 6 < pair_count:
+    if relay and 6 < pair_count:
         found[6] = [swap(found[4][0][:half], "pair", 2), swap(found[2][0][half:], "pair", 4)]
     return found
 
@@ -336,23 +321,21 @@
             piece = swap(after(piece, own[2]) if s == 3 else piece, "win", s)
         own.append(piece)
     for s, piece in enumerate(own):
-        if s >= 2:
+        if s >= 1:
             near = [part for at in (2, 4) for part in found[s - 1].get(at, [])]
-            piece = after(piece, *near, *found[s - 2].get(6, []))
-        found.append(gather_even(piece))
+            piece = after(piece, *near, *(found[s - 2].get(6, []) if s > 1 else []))
+        found.append(gather_even(piece, relay=s > 0))
     left = left_side(own, windows)
-    half, bins = rows // 2, rows // 2
-    waited = after(beside, left)
-    early = [swap(pick([cut(chunk, 0, rows)], waited), "pair", 1) for chunk in found[:-2]]
+    half = rows // 2
+    early = [swap(pick([cut(chunk, 0, rows)], beside), "pair", 1) for chunk in found[:-2]]
     late = [
         swap(pick([cut(chunk, at, at + half) for chunk in found[-2:]], beside), "pair", 1)
         for at in (0, half)
     ]
-    result = None
-    for part, (low, count) in enumerate(((0, bins // 2), (bins // 2, bins - bins // 2))):
-        other = [(array, 2 * low) for array in early] + [(late[part], 0), (late[part], half)]
-        result = correlate(mine, left, other, found, low, count, result)
-    return result
+    other = [[(n, 0, rows)] for n in range(len(early))]
+    for n in range(2):
+        other.append([(len(early) + part, n * half, half) for part in range(2)])
+    return correlate(mine, left, found, early + late, other)
 
 
 def solution(mesh):

time: 65.9 us -> 64.1 us (0.973)
  starting transfers between devices: 30.8 us -> 27.2 us
  waiting for transfers between devices: 15.5 us -> 18.4 us
  Pallas kernels: 17.8 us -> 16.2 us
    ppermute x23 -> x22, starting transfers between devices: 30.8 us -> 27.2 us  [swap(): return lax.ppermute(value, axis, [(i, i ^ distance) for i in range(count)])]
    ppermute x23 -> x22, waiting for transfers between devices: 15.5 us -> 18.4 us  [swap(): return lax.ppermute(value, axis, [(i, i ^ distance) for i in range(count)])]
    pallas_call x2 -> x1, Pallas kernels: 6.06 us -> 4.47 us  [correlate(): pl.pallas_call(functools.partial(correlate_kernel, scale, layout), in_spe...]
  transfers between devices with their start and end apart: 23 -> 22, of which waited for: 6 -> 8; matrix products, arithmetic and copies ran while one was open for 2% -> 2% of each run, Pallas kernels for 10% -> 5%
where the time goes in v4:
time: 64.1 us; the launch traced here: 63.4 us
  starting transfers between devices  27.2 us (42%)
  waiting for transfers between devices  18.4 us (29%)
  Pallas kernels  16.2 us (25%)
  local copies, waits for them, and re-layouts  0.72 us (1%)
  other arithmetic  0.7 us (1%)
    ppermute x22, starting transfers between devices, swap(): return lax.ppermute(value, axis, [(i, i ^ distance) for i in range(count)])  27.2 us
    ppermute x22, waiting for transfers between devices, swap(): return lax.ppermute(value, axis, [(i, i ^ distance) for i in range(count)])  18.4 us
    pallas_call x1, Pallas kernels, local_spectra(): pl.pallas_call(functools.partial(spectra_kernel, chan_rows, win_count, pi...  8.27 us
    pallas_call x1, Pallas kernels, correlate(): pl.pallas_call(functools.partial(correlate_kernel, scale, layout), in_spe...  4.47 us
    pallas_call x4, Pallas kernels, pick(): pl.pallas_call(functools.partial(pick_kernel, places), in_specs=[pl.Block...  2.47 us
  transfers between devices with their start and end apart: 22, of which 8 were waited for; matrix products, arithmetic and copies ran while one was open for 2% of the time, Pallas kernels for 5%

profile of v4, /device:TPU:0, one launch (start us, length us, event | category | flops | bytes accessed | tf_op | source)
XLA Modules:
  0.0 63.4 jit_solution(10399655516527333068)
XLA Ops:
  0.0 8.3 %spectra.1 = (bf16[16,32,256]{2,1,0:T(8,128)(2,1)S(1)}, bf16[16,32,256]{2,1,0:T(8,128)(2,1)S(1)}, bf16[16,32,256]{2,1,0:T(8,128)(2,1)S(1)}, bf16[16,32,256]{2,1,0:T(8,128)(2,1)S(1)}) custom-call(s32[1]{0:T(128)} %bitcast.win_ref, bf16[256,32,1024]{2,1,0:T(8,128)(2,1)} %traces_ref.1), custom_call_target="tpu_custom_call" | custom-call | flops 1073741824 | bytes 16777216 | tf_op jit(solution)/shard_map/spectra/pallas_call | solution.py:105
  8.3 3.1 %collective-permute-start = (bf16[16,32,256]{2,1,0:T(8,128)(2,1)S(1)}, bf16[16,32,256]{2,1,0:T(8,128)(2,1)S(1)}, u32[]{:S(2)}, u32[]{:S(2)}) collective-permute-start(bf16[16,32,256]{2,1,0:T(8,128)(2,1)S(1)} %get-tuple-element.14), channel_id=1, source_target_pairs={{0,1},{1,0},{2,3},{3,2},{4,5},{5,4},{6,7},{7,6},{8,9},{9,8},{10,11... | collective-permute-start | bytes 786440 | tf_op jit(solution)/shard_map/ppermute | solution.py:287
  11.4 1.5 %collective-permute-start.4 = (bf16[16,32,256]{2,1,0:T(8,128)(2,1)S(1)}, bf16[16,32,256]{2,1,0:T(8,128)(2,1)S(1)}, u32[]{:S(2)}, u32[]{:S(2)}) collective-permute-start(bf16[16,32,256]{2,1,0:T(8,128)(2,1)S(1)} %get-tuple-element.13.refs_0_), channel_id=1, source_target_pairs={{0,16},{4,20},{8,24},{12,28},{16,0},{20,4},{24,8},{28,12},{1,17},{... | collective-permute-start | bytes 786440 | tf_op jit(solution)/shard_map/ppermute | solution.py:287
  12.9 1.5 %collective-permute-start.3 = (bf16[16,32,256]{2,1,0:T(8,128)(2,1)S(1)}, bf16[16,32,256]{2,1,0:T(8,128)(2,1)S(1)}, u32[]{:S(2)}, u32[]{:S(2)}) collective-permute-start(bf16[16,32,256]{2,1,0:T(8,128)(2,1)S(1)} %get-tuple-element.13.refs_0_), channel_id=1, source_target_pairs={{0,8},{4,12},{8,0},{12,4},{16,24},{20,28},{24,16},{28,20},{1,9},{5... | collective-permute-start | bytes 786440 | tf_op jit(solution)/shard_map/ppermute | solution.py:287
  14.9 2.6 %collective-permute-start.1 = (bf16[16,32,256]{2,1,0:T(8,128)(2,1)S(1)}, bf16[16,32,256]{2,1,0:T(8,128)(2,1)S(1)}, u32[]{:S(2)}, u32[]{:S(2)}) collective-permute-start(bf16[16,32,256]{2,1,0:T(8,128)(2,1)S(1)} %get-tuple-element.15), channel_id=1, source_target_pairs={{0,2},{1,3},{2,0},{3,1},{4,6},{5,7},{6,4},{7,5},{8,10},{9,11},{10,... | collective-permute-start | bytes 786440 | tf_op jit(solution)/shard_map/ppermute | solution.py:287
  17.5 2.4 %collective-permute-done.refs_1_.refs_0_ = bf16[16,32,256]{2,1,0:T(8,128)(2,1)S(1)} collective-permute-done((bf16[16,32,256]{2,1,0:T(8,128)(2,1)S(1)}, bf16[16,32,256]{2,1,0:T(8,128)(2,1)S(1)}, u32[]{:S(2)}, u32[]{:S(2)}) %collective-permute-start) | collective-permute-done | bytes 262176 | tf_op jit(solution)/shard_map/ppermute | solution.py:287
  19.8 2.3 %collective-permute-done.3.refs_1_.refs_4_ = bf16[16,32,256]{2,1,0:T(8,128)(2,1)S(1)} collective-permute-done((bf16[16,32,256]{2,1,0:T(8,128)(2,1)S(1)}, bf16[16,32,256]{2,1,0:T(8,128)(2,1)S(1)}, u32[]{:S(2)}, u32[]{:S(2)}) %collective-permute-start.3) | collective-permute-done | bytes 262176 | tf_op jit(solution)/shard_map/ppermute | solution.py:287
  22.6 1.5 %collective-permute-start.7 = (bf16[16,32,256]{2,1,0:T(8,128)(2,1)S(1)}, bf16[16,32,256]{2,1,0:T(8,128)(2,1)S(1)}, u32[]{:S(2)}, u32[]{:S(2)}) collective-permute-start(bf16[16,32,256]{2,1,0:T(8,128)(2,1)S(1)} %collective-permute-done.refs_1_.refs_0_), channel_id=1, source_target_pairs={{0,8},{4,12},{8,0},{12,4},{16,24},{20,28},{24,16},{28,20},{1,9},{5... | collective-permute-start | bytes 786440 | tf_op jit(solution)/shard_map/ppermute | solution.py:287
  24.1 4.2 %collective-permute-done.1.refs_2_.refs_0_ = bf16[16,32,256]{2,1,0:T(8,128)(2,1)S(1)} collective-permute-done((bf16[16,32,256]{2,1,0:T(8,128)(2,1)S(1)}, bf16[16,32,256]{2,1,0:T(8,128)(2,1)S(1)}, u32[]{:S(2)}, u32[]{:S(2)}) %collective-permute-start.1) | collective-permute-done | bytes 262176 | tf_op jit(solution)/shard_map/ppermute | solution.py:287
  28.4 3.6 %collective-permute-start.2 = (bf16[16,32,256]{2,1,0:T(8,128)(2,1)S(1)}, bf16[16,32,256]{2,1,0:T(8,128)(2,1)S(1)}, u32[]{:S(2)}, u32[]{:S(2)}) collective-permute-start(bf16[16,32,256]{2,1,0:T(8,128)(2,1)S(1)} %get-tuple-element.17), channel_id=1, source_target_pairs={{0,3},{1,2},{2,1},{3,0},{4,7},{5,6},{6,5},{7,4},{8,11},{9,10},{10,... | collective-permute-start | bytes 786440 | tf_op jit(solution)/shard_map/ppermute | solution.py:287
  31.9 1.6 %collective-permute-start.13 = (bf16[16,32,256]{2,1,0:T(8,128)(2,1)S(1)}, bf16[16,32,256]{2,1,0:T(8,128)(2,1)S(1)}, u32[]{:S(2)}, u32[]{:S(2)}) collective-permute-start(bf16[16,32,256]{2,1,0:T(8,128)(2,1)S(1)} %collective-permute-done.1.refs_2_.refs_0_), channel_id=1, source_target_pairs={{0,16},{4,20},{8,24},{12,28},{16,0},{20,4},{24,8},{28,12},{1,17},{... | collective-permute-start | bytes 786440 | tf_op jit(solution)/shard_map/ppermute | solution.py:287
  33.5 1.5 %collective-permute-start.12 = (bf16[16,32,256]{2,1,0:T(8,128)(2,1)S(1)}, bf16[16,32,256]{2,1,0:T(8,128)(2,1)S(1)}, u32[]{:S(2)}, u32[]{:S(2)}) collective-permute-start(bf16[16,32,256]{2,1,0:T(8,128)(2,1)S(1)} %collective-permute-done.1.refs_2_.refs_0_), channel_id=1, source_target_pairs={{0,8},{4,12},{8,0},{12,4},{16,24},{20,28},{24,16},{28,20},{1,9},{5... | collective-permute-start | bytes 786440 | tf_op jit(solution)/shard_map/ppermute | solution.py:287
  35.1 0.6 collective-permute-start.9
  35.7 0.7 %slice.25 = bf16[8,32,256]{2,1,0:T(8,128)(2,1)} slice(bf16[16,32,256]{2,1,0:T(8,128)(2,1)S(1)} %collective-permute-done.7.refs_1_.refs_7_), slice={[8:16], [0:32], [0:256]} | slice | bytes 262144 | tf_op jit(solution)/shard_map/slice | solution.py:302
  36.4 0.5 collective-permute-start.10
  37.2 4.7 %collective-permute-done.9.refs_3_.refs_9_ = bf16[8,32,256]{2,1,0:T(8,128)(2,1)S(1)} collective-permute-done((bf16[8,32,256]{2,1,0:T(8,128)(2,1)S(1)}, bf16[8,32,256]{2,1,0:T(8,128)(2,1)S(1)}, u32[]{:S(2)}, u32[]{:S(2)}) %collective-permute-start.9) | collective-permute-done | bytes 131104 | tf_op jit(solution)/shard_map/ppermute | solution.py:287
  41.8 1.1 %collective-permute-start.16 = (bf16[16,32,256]{2,1,0:T(8,128)(2,1)S(1)}, bf16[16,32,256]{2,1,0:T(8,128)(2,1)S(1)}, u32[]{:S(2)}, u32[]{:S(2)}) collective-permute-start(bf16[16,32,256]{2,1,0:T(8,128)(2,1)S(1)} %collective-permute-done.2.refs_3_.refs_4_), channel_id=1, source_target_pairs={{0,16},{4,20},{8,24},{12,28},{16,0},{20,4},{24,8},{28,12},{1,17},{... | collective-permute-start | bytes 786440 | tf_op jit(solution)/shard_map/ppermute | solution.py:287
  42.9 1.5 %collective-permute-start.15 = (bf16[16,32,256]{2,1,0:T(8,128)(2,1)S(1)}, bf16[16,32,256]{2,1,0:T(8,128)(2,1)S(1)}, u32[]{:S(2)}, u32[]{:S(2)}) collective-permute-start(bf16[16,32,256]{2,1,0:T(8,128)(2,1)S(1)} %collective-permute-done.2.refs_3_.refs_4_), channel_id=1, source_target_pairs={{0,8},{4,12},{8,0},{12,4},{16,24},{20,28},{24,16},{28,20},{1,9},{5... | collective-permute-start | bytes 786440 | tf_op jit(solution)/shard_map/ppermute | solution.py:287
  44.8 0.6 collective-permute-start.14
  45.4 1.1 %collective-permute-start.19 = (bf16[8,32,256]{2,1,0:T(8,128)(2,1)S(1)}, bf16[8,32,256]{2,1,0:T(8,128)(2,1)S(1)}, u32[]{:S(2)}, u32[]{:S(2)}) collective-permute-start(bf16[8,32,256]{2,1,0:T(8,128)(2,1)S(1)} %slice.28), channel_id=1, source_target_pairs={{0,16},{4,20},{8,24},{12,28},{16,0},{20,4},{24,8},{28,12},{1,17},{... | collective-permute-start | bytes 393224 | tf_op jit(solution)/shard_map/ppermute | solution.py:287
  46.5 2.4 %collective-permute-done.16.refs_6_.refs_16_ = bf16[16,32,256]{2,1,0:T(8,128)(2,1)S(1)} collective-permute-done((bf16[16,32,256]{2,1,0:T(8,128)(2,1)S(1)}, bf16[16,32,256]{2,1,0:T(8,128)(2,1)S(1)}, u32[]{:S(2)}, u32[]{:S(2)}) %collective-permute-start.16) | collective-permute-done | bytes 262176 | tf_op jit(solution)/shard_map/ppermute | solution.py:287
  49.0 2.3 %collective-permute-start.17 = (bf16[8,32,256]{2,1,0:T(8,128)(2,1)S(1)}, bf16[8,32,256]{2,1,0:T(8,128)(2,1)S(1)}, u32[]{:S(2)}, u32[]{:S(2)}) collective-permute-start(bf16[8,32,256]{2,1,0:T(8,128)(2,1)S(1)} %slice.27), channel_id=1, source_target_pairs={{0,8},{4,12},{8,0},{12,4},{16,24},{20,28},{24,16},{28,20},{1,9},{5... | collective-permute-start | bytes 393224 | tf_op jit(solution)/shard_map/ppermute | solution.py:287
  51.3 1.0 %collective-permute-start.20 = (bf16[8,32,256]{2,1,0:T(8,128)(2,1)S(1)}, bf16[8,32,256]{2,1,0:T(8,128)(2,1)S(1)}, u32[]{:S(2)}, u32[]{:S(2)}) collective-permute-start(bf16[8,32,256]{2,1,0:T(8,128)(2,1)S(1)} %slice.29), channel_id=1, source_target_pairs={{0,16},{4,20},{8,24},{12,28},{16,0},{20,4},{24,8},{28,12},{1,17},{... | collective-permute-start | bytes 393224 | tf_op jit(solution)/shard_map/ppermute | solution.py:287
  52.2 0.6 pick.4
  52.9 0.6 pick.5
  53.6 0.6 collective-permute-start.11
  54.2 0.6 pick.6
  54.9 1.4 %collective-permute-done.20.refs_7_.refs_18_ = bf16[8,32,256]{2,1,0:T(8,128)(2,1)S(1)} collective-permute-done((bf16[8,32,256]{2,1,0:T(8,128)(2,1)S(1)}, bf16[8,32,256]{2,1,0:T(8,128)(2,1)S(1)}, u32[]{:S(2)}, u32[]{:S(2)}) %collective-permute-start.20) | collective-permute-done | bytes 131104 | tf_op jit(solution)/shard_map/ppermute | solution.py:287
  56.3 0.6 pick.7
  57.0 1.0 %left_side.1.left_ref = bf16[8,512,256]{2,1,0:T(8,128)(2,1)S(1)} custom-call(bf16[16,32,256]{2,1,0:T(8,128)(2,1)S(1)} %get-tuple-element.13.refs_0_, bf16[16,32,256]{2,1,0:T(8,128)(2,1)S(1)} %collective-permute-done.refs_1_.refs_0_, bf16[16,32,256]{2,1,0:T(8,128)(2,1)S(1)} %collective-permute-done.1.refs_2_.refs_0_, ...), custom_call_target="tpu_custom_call" | custom-call | tf_op jit(solution)/shard_map/left_side/pallas_call | solution.py:190
  58.0 0.9 %collective-permute-done.21.refs_3_ = bf16[2,16,32,256]{3,2,1,0:T(8,128)(2,1)S(1)} collective-permute-done((bf16[2,16,32,256]{3,2,1,0:T(8,128)(2,1)S(1)}, bf16[2,16,32,256]{3,2,1,0:T(8,128)(2,1)S(1)}, u32[]{:S(2)}, u32[]{:S(2)}) %collective-permute-start.21) | collective-permute-done | bytes 524320 | tf_op jit(solution)/shard_map/ppermute | solution.py:287
  58.9 4.5 %cross_spectra.1 = f32[2,8,2,256,256]{4,3,2,1,0:T(8,128)} custom-call(s32[2]{0:T(128)S(1)} %broadcast_xor_fusion.1.far_ref, bf16[8,512,256]{2,1,0:T(8,128)(2,1)S(1)} %left_side.1.left_ref, bf16[2,16,32,256]{3,2,1,0:T(8,128)(2,1)S(1)} %collective-permute-done.6.refs_0_, bf16[2,16,32,256]{3,2,1,0:T(8,128)(2,1)S(1)} %collective-permute-done.11.refs_1_, ...), custom_call_target="tpu_custom_call" | custom-call | flops 1073741824 | bytes 8388608 | tf_op jit(solution)/shard_map/cross_spectra/pallas_call | solution.py:261
  (37 shorter events, 2.1 us)
Async XLA Ops:
  0.0 35.0 %copy-start.1 = (s32[8]{0:T(128)S(1)}, s32[8]{0:T(128)}, u32[]{:S(2)}) copy-start(s32[8]{0:T(128)} %param.5) | copy-start | bytes 100
  0.0 37.0 %copy-start = (s32[2,8]{1,0:T(2,128)S(1)}, s32[2,8]{1,0:T(2,128)}, u32[]{:S(2)}) copy-start(s32[2,8]{1,0:T(2,128)} %param.4) | copy-start | bytes 196
  8.3 11.5 %collective-permute-start = (bf16[16,32,256]{2,1,0:T(8,128)(2,1)S(1)}, bf16[16,32,256]{2,1,0:T(8,128)(2,1)S(1)}, u32[]{:S(2)}, u32[]{:S(2)}) collective-permute-start(bf16[16,32,256]{2,1,0:T(8,128)(2,1)S(1)} %get-tuple-element.14), channel_id=1, source_target_pairs={{0,1},{1,0},{2,3},{3,2},{4,5},{5,4},{6,7},{7,6},{8,9},{9,8},{10,11... | collective-permute-start | bytes 786440 | tf_op jit(solution)/shard_map/ppermute | solution.py:287
  11.4 8.4 %collective-permute-start.4 = (bf16[16,32,256]{2,1,0:T(8,128)(2,1)S(1)}, bf16[16,32,256]{2,1,0:T(8,128)(2,1)S(1)}, u32[]{:S(2)}, u32[]{:S(2)}) collective-permute-start(bf16[16,32,256]{2,1,0:T(8,128)(2,1)S(1)} %get-tuple-element.13.refs_0_), channel_id=1, source_target_pairs={{0,16},{4,20},{8,24},{12,28},{16,0},{20,4},{24,8},{28,12},{1,17},{... | collective-permute-start | bytes 786440 | tf_op jit(solution)/shard_map/ppermute | solution.py:287
  12.9 9.2 %collective-permute-start.3 = (bf16[16,32,256]{2,1,0:T(8,128)(2,1)S(1)}, bf16[16,32,256]{2,1,0:T(8,128)(2,1)S(1)}, u32[]{:S(2)}, u32[]{:S(2)}) collective-permute-start(bf16[16,32,256]{2,1,0:T(8,128)(2,1)S(1)} %get-tuple-element.13.refs_0_), channel_id=1, source_target_pairs={{0,8},{4,12},{8,0},{12,4},{16,24},{20,28},{24,16},{28,20},{1,9},{5... | collective-permute-start | bytes 786440 | tf_op jit(solution)/shard_map/ppermute | solution.py:287
  14.4 17.6 %collective-permute-start.5 = (bf16[16,32,256]{2,1,0:T(8,128)(2,1)S(1)}, bf16[16,32,256]{2,1,0:T(8,128)(2,1)S(1)}, u32[]{:S(2)}, u32[]{:S(2)}) collective-permute-start(bf16[16,32,256]{2,1,0:T(8,128)(2,1)S(1)} %get-tuple-element.13.refs_0_), channel_id=1, source_target_pairs={{0,24},{4,28},{8,16},{12,20},{16,8},{20,12},{24,0},{28,4},{1,25},{... | collective-permute-start | bytes 786440 | tf_op jit(solution)/shard_map/ppermute | solution.py:287
  14.9 13.5 %collective-permute-start.1 = (bf16[16,32,256]{2,1,0:T(8,128)(2,1)S(1)}, bf16[16,32,256]{2,1,0:T(8,128)(2,1)S(1)}, u32[]{:S(2)}, u32[]{:S(2)}) collective-permute-start(bf16[16,32,256]{2,1,0:T(8,128)(2,1)S(1)} %get-tuple-element.15), channel_id=1, source_target_pairs={{0,2},{1,3},{2,0},{3,1},{4,6},{5,7},{6,4},{7,5},{8,10},{9,11},{10,... | collective-permute-start | bytes 786440 | tf_op jit(solution)/shard_map/ppermute | solution.py:287
  22.1 9.8 %collective-permute-start.8 = (bf16[16,32,256]{2,1,0:T(8,128)(2,1)S(1)}, bf16[16,32,256]{2,1,0:T(8,128)(2,1)S(1)}, u32[]{:S(2)}, u32[]{:S(2)}) collective-permute-start(bf16[16,32,256]{2,1,0:T(8,128)(2,1)S(1)} %collective-permute-done.refs_1_.refs_0_), channel_id=1, source_target_pairs={{0,16},{4,20},{8,24},{12,28},{16,0},{20,4},{24,8},{28,12},{1,17},{... | collective-permute-start | bytes 786440 | tf_op jit(solution)/shard_map/ppermute | solution.py:287
  22.6 9.3 %collective-permute-start.7 = (bf16[16,32,256]{2,1,0:T(8,128)(2,1)S(1)}, bf16[16,32,256]{2,1,0:T(8,128)(2,1)S(1)}, u32[]{:S(2)}, u32[]{:S(2)}) collective-permute-start(bf16[16,32,256]{2,1,0:T(8,128)(2,1)S(1)} %collective-permute-done.refs_1_.refs_0_), channel_id=1, source_target_pairs={{0,8},{4,12},{8,0},{12,4},{16,24},{20,28},{24,16},{28,20},{1,9},{5... | collective-permute-start | bytes 786440 | tf_op jit(solution)/shard_map/ppermute | solution.py:287
  28.4 8.8 %collective-permute-start.2 = (bf16[16,32,256]{2,1,0:T(8,128)(2,1)S(1)}, bf16[16,32,256]{2,1,0:T(8,128)(2,1)S(1)}, u32[]{:S(2)}, u32[]{:S(2)}) collective-permute-start(bf16[16,32,256]{2,1,0:T(8,128)(2,1)S(1)} %get-tuple-element.17), channel_id=1, source_target_pairs={{0,3},{1,2},{2,1},{3,0},{4,7},{5,6},{6,5},{7,4},{8,11},{9,10},{10,... | collective-permute-start | bytes 786440 | tf_op jit(solution)/shard_map/ppermute | solution.py:287
  31.9 9.9 %collective-permute-start.13 = (bf16[16,32,256]{2,1,0:T(8,128)(2,1)S(1)}, bf16[16,32,256]{2,1,0:T(8,128)(2,1)S(1)}, u32[]{:S(2)}, u32[]{:S(2)}) collective-permute-start(bf16[16,32,256]{2,1,0:T(8,128)(2,1)S(1)} %collective-permute-done.1.refs_2_.refs_0_), channel_id=1, source_target_pairs={{0,16},{4,20},{8,24},{12,28},{16,0},{20,4},{24,8},{28,12},{1,17},{... | collective-permute-start | bytes 786440 | tf_op jit(solution)/shard_map/ppermute | solution.py:287
  33.5 8.3 %collective-permute-start.12 = (bf16[16,32,256]{2,1,0:T(8,128)(2,1)S(1)}, bf16[16,32,256]{2,1,0:T(8,128)(2,1)S(1)}, u32[]{:S(2)}, u32[]{:S(2)}) collective-permute-start(bf16[16,32,256]{2,1,0:T(8,128)(2,1)S(1)} %collective-permute-done.1.refs_2_.refs_0_), channel_id=1, source_target_pairs={{0,8},{4,12},{8,0},{12,4},{16,24},{20,28},{24,16},{28,20},{1,9},{5... | collective-permute-start | bytes 786440 | tf_op jit(solution)/shard_map/ppermute | solution.py:287
  35.1 6.7 %collective-permute-start.9 = (bf16[8,32,256]{2,1,0:T(8,128)(2,1)S(1)}, bf16[8,32,256]{2,1,0:T(8,128)(2,1)S(1)}, u32[]{:S(2)}, u32[]{:S(2)}) collective-permute-start(bf16[8,32,256]{2,1,0:T(8,128)(2,1)S(1)} %slice.24), channel_id=1, source_target_pairs={{0,8},{4,12},{8,0},{12,4},{16,24},{20,28},{24,16},{28,20},{1,9},{5... | collective-permute-start | bytes 393224 | tf_op jit(solution)/shard_map/ppermute | solution.py:287
  36.4 5.5 %collective-permute-start.10 = (bf16[8,32,256]{2,1,0:T(8,128)(2,1)}, bf16[8,32,256]{2,1,0:T(8,128)(2,1)S(1)}, u32[]{:S(2)}, u32[]{:S(2)}) collective-permute-start(bf16[8,32,256]{2,1,0:T(8,128)(2,1)} %slice.25), channel_id=1, source_target_pairs={{0,16},{4,20},{8,24},{12,28},{16,0},{20,4},{24,8},{28,12},{1,17},{... | collective-permute-start | bytes 393224 | tf_op jit(solution)/shard_map/ppermute | solution.py:287
  41.8 7.1 %collective-permute-start.16 = (bf16[16,32,256]{2,1,0:T(8,128)(2,1)S(1)}, bf16[16,32,256]{2,1,0:T(8,128)(2,1)S(1)}, u32[]{:S(2)}, u32[]{:S(2)}) collective-permute-start(bf16[16,32,256]{2,1,0:T(8,128)(2,1)S(1)} %collective-permute-done.2.refs_3_.refs_4_), channel_id=1, source_target_pairs={{0,16},{4,20},{8,24},{12,28},{16,0},{20,4},{24,8},{28,12},{1,17},{... | collective-permute-start | bytes 786440 | tf_op jit(solution)/shard_map/ppermute | solution.py:287
  42.9 8.4 %collective-permute-start.15 = (bf16[16,32,256]{2,1,0:T(8,128)(2,1)S(1)}, bf16[16,32,256]{2,1,0:T(8,128)(2,1)S(1)}, u32[]{:S(2)}, u32[]{:S(2)}) collective-permute-start(bf16[16,32,256]{2,1,0:T(8,128)(2,1)S(1)} %collective-permute-done.2.refs_3_.refs_4_), channel_id=1, source_target_pairs={{0,8},{4,12},{8,0},{12,4},{16,24},{20,28},{24,16},{28,20},{1,9},{5... | collective-permute-start | bytes 786440 | tf_op jit(solution)/shard_map/ppermute | solution.py:287
  44.8 8.8 %collective-permute-start.14 = (bf16[8,32,256]{2,1,0:T(8,128)(2,1)S(1)}, bf16[8,32,256]{2,1,0:T(8,128)(2,1)S(1)}, u32[]{:S(2)}, u32[]{:S(2)}) collective-permute-start(bf16[8,32,256]{2,1,0:T(8,128)(2,1)S(1)} %slice.26), channel_id=1, source_target_pairs={{0,8},{4,12},{8,0},{12,4},{16,24},{20,28},{24,16},{28,20},{1,9},{5... | collective-permute-start | bytes 393224 | tf_op jit(solution)/shard_map/ppermute | solution.py:287
  45.4 9.5 %collective-permute-start.19 = (bf16[8,32,256]{2,1,0:T(8,128)(2,1)S(1)}, bf16[8,32,256]{2,1,0:T(8,128)(2,1)S(1)}, u32[]{:S(2)}, u32[]{:S(2)}) collective-permute-start(bf16[8,32,256]{2,1,0:T(8,128)(2,1)S(1)} %slice.28), channel_id=1, source_target_pairs={{0,16},{4,20},{8,24},{12,28},{16,0},{20,4},{24,8},{28,12},{1,17},{... | collective-permute-start | bytes 393224 | tf_op jit(solution)/shard_map/ppermute | solution.py:287
  49.0 5.3 %collective-permute-start.17 = (bf16[8,32,256]{2,1,0:T(8,128)(2,1)S(1)}, bf16[8,32,256]{2,1,0:T(8,128)(2,1)S(1)}, u32[]{:S(2)}, u32[]{:S(2)}) collective-permute-start(bf16[8,32,256]{2,1,0:T(8,128)(2,1)S(1)} %slice.27), channel_id=1, source_target_pairs={{0,8},{4,12},{8,0},{12,4},{16,24},{20,28},{24,16},{28,20},{1,9},{5... | collective-permute-start | bytes 393224 | tf_op jit(solution)/shard_map/ppermute | solution.py:287
  51.3 5.0 %collective-permute-start.20 = (bf16[8,32,256]{2,1,0:T(8,128)(2,1)S(1)}, bf16[8,32,256]{2,1,0:T(8,128)(2,1)S(1)}, u32[]{:S(2)}, u32[]{:S(2)}) collective-permute-start(bf16[8,32,256]{2,1,0:T(8,128)(2,1)S(1)} %slice.29), channel_id=1, source_target_pairs={{0,16},{4,20},{8,24},{12,28},{16,0},{20,4},{24,8},{28,12},{1,17},{... | collective-permute-start | bytes 393224 | tf_op jit(solution)/shard_map/ppermute | solution.py:287
  52.9 5.2 %collective-permute-start.6 = (bf16[2,16,32,256]{3,2,1,0:T(8,128)(2,1)S(1)}, bf16[2,16,32,256]{3,2,1,0:T(8,128)(2,1)S(1)}, u32[]{:S(2)}, u32[]{:S(2)}) collective-permute-start(bf16[2,16,32,256]{3,2,1,0:T(8,128)(2,1)S(1)} %pick.4), channel_id=1, source_target_pairs={{0,4},{4,0},{8,12},{12,8},{16,20},{20,16},{24,28},{28,24},{1,5},{5... | collective-permute-start | bytes 1572872 | tf_op jit(solution)/shard_map/ppermute | solution.py:287
  53.6 4.4 %collective-permute-start.11 = (bf16[2,16,32,256]{3,2,1,0:T(8,128)(2,1)S(1)}, bf16[2,16,32,256]{3,2,1,0:T(8,128)(2,1)S(1)}, u32[]{:S(2)}, u32[]{:S(2)}) collective-permute-start(bf16[2,16,32,256]{3,2,1,0:T(8,128)(2,1)S(1)} %pick.5), channel_id=1, source_target_pairs={{0,4},{4,0},{8,12},{12,8},{16,20},{20,16},{24,28},{28,24},{1,5},{5... | collective-permute-start | bytes 1572872 | tf_op jit(solution)/shard_map/ppermute | solution.py:287
  54.8 3.2 %collective-permute-start.18 = (bf16[2,16,32,256]{3,2,1,0:T(8,128)(2,1)S(1)}, bf16[2,16,32,256]{3,2,1,0:T(8,128)(2,1)S(1)}, u32[]{:S(2)}, u32[]{:S(2)}) collective-permute-start(bf16[2,16,32,256]{3,2,1,0:T(8,128)(2,1)S(1)} %pick.6), channel_id=1, source_target_pairs={{0,4},{4,0},{8,12},{12,8},{16,20},{20,16},{24,28},{28,24},{1,5},{5... | collective-permute-start | bytes 1572872 | tf_op jit(solution)/shard_map/ppermute | solution.py:287
  56.9 2.0 %collective-permute-start.21 = (bf16[2,16,32,256]{3,2,1,0:T(8,128)(2,1)S(1)}, bf16[2,16,32,256]{3,2,1,0:T(8,128)(2,1)S(1)}, u32[]{:S(2)}, u32[]{:S(2)}) collective-permute-start(bf16[2,16,32,256]{3,2,1,0:T(8,128)(2,1)S(1)} %pick.7), channel_id=1, source_target_pairs={{0,4},{4,0},{8,12},{12,8},{16,20},{20,16},{24,28},{28,24},{1,5},{5... | collective-permute-start | bytes 1572872 | tf_op jit(solution)/shard_map/ppermute | solution.py:287

commit v5 on v4

--- a/solution.py
+++ b/solution.py
@@ -226,7 +226,7 @@
     def send(bin_no, r):
         return pltpu.make_async_copy(result_ref.at[bin_no, r], out_hbm.at[r, bin_no], sems.at[bin_no, r])
 
-    @pl.loop(0, bins)
+    @pl.loop(0, bins, unroll=2)
     def _(bin_no):
         for r in range(ROUNDS):
             right = jnp.concatenate(
@@ -323,7 +323,7 @@
     for s, piece in enumerate(own):
         if s >= 1:
             near = [part for at in (2, 4) for part in found[s - 1].get(at, [])]
-            piece = after(piece, *near, *(found[s - 2].get(6, []) if s > 1 else []))
+            piece = after(piece, *near, *(found[s - 2].get(6, []) if s == 2 else []))
         found.append(gather_even(piece, relay=s > 0))
     left = left_side(own, windows)
     half = rows // 2

time: 64.1 us -> 63.4 us (0.989)
  local copies, waits for them, and re-layouts: 0.72 us -> 0.07 us
    ppermute x22, waiting for transfers between devices: 18.4 us -> 19 us  [swap(): return lax.ppermute(value, axis, [(i, i ^ distance) for i in range(count)])]
    slice x3, local copies, waits for them, and re-layouts: 0.68 us -> 0.03 us  [gather_even(): found[2][0][half:]]
  transfers between devices with their start and end apart: 22 -> 22, of which waited for: 8 -> 11; matrix products, arithmetic and copies ran while one was open for 2% -> 1% of each run, Pallas kernels for 5% -> 5%
where the time goes in v5:
time: 63.4 us; the launch traced here: 63.3 us
  starting transfers between devices  27.1 us (43%)
  waiting for transfers between devices  19 us (30%)
  Pallas kernels  16.2 us (26%)
  other arithmetic  0.7 us (1%)
    ppermute x22, starting transfers between devices, swap(): return lax.ppermute(value, axis, [(i, i ^ distance) for i in range(count)])  27.1 us
    ppermute x22, waiting for transfers between devices, swap(): return lax.ppermute(value, axis, [(i, i ^ distance) for i in range(count)])  19 us
    pallas_call x1, Pallas kernels, local_spectra(): pl.pallas_call(functools.partial(spectra_kernel, chan_rows, win_count, pi...  8.27 us
    pallas_call x1, Pallas kernels, correlate(): pl.pallas_call(functools.partial(correlate_kernel, scale, layout), in_spe...  4.45 us
    pallas_call x4, Pallas kernels, pick(): pl.pallas_call(functools.partial(pick_kernel, places), in_specs=[pl.Block...  2.47 us
  transfers between devices with their start and end apart: 22, of which 11 were waited for; matrix products, arithmetic and copies ran while one was open for 1% of the time, Pallas kernels for 5%

profile of v5, /device:TPU:0, one launch (start us, length us, event | category | flops | bytes accessed | tf_op | source)
XLA Modules:
  0.0 63.3 jit_solution(8451633641132656972)
XLA Ops:
  0.0 8.3 %spectra.1 = (bf16[16,32,256]{2,1,0:T(8,128)(2,1)S(1)}, bf16[16,32,256]{2,1,0:T(8,128)(2,1)S(1)}, bf16[16,32,256]{2,1,0:T(8,128)(2,1)S(1)}, bf16[16,32,256]{2,1,0:T(8,128)(2,1)S(1)}) custom-call(s32[1]{0:T(128)} %bitcast.win_ref, bf16[256,32,1024]{2,1,0:T(8,128)(2,1)} %traces_ref.1), custom_call_target="tpu_custom_call" | custom-call | flops 1073741824 | bytes 16777216 | tf_op jit(solution)/shard_map/spectra/pallas_call | solution.py:105
  8.3 3.1 %collective-permute-start = (bf16[16,32,256]{2,1,0:T(8,128)(2,1)S(1)}, bf16[16,32,256]{2,1,0:T(8,128)(2,1)S(1)}, u32[]{:S(2)}, u32[]{:S(2)}) collective-permute-start(bf16[16,32,256]{2,1,0:T(8,128)(2,1)S(1)} %get-tuple-element.14), channel_id=1, source_target_pairs={{0,1},{1,0},{2,3},{3,2},{4,5},{5,4},{6,7},{7,6},{8,9},{9,8},{10,11... | collective-permute-start | bytes 786440 | tf_op jit(solution)/shard_map/ppermute | solution.py:287
  11.4 1.5 %collective-permute-start.4 = (bf16[16,32,256]{2,1,0:T(8,128)(2,1)S(1)}, bf16[16,32,256]{2,1,0:T(8,128)(2,1)S(1)}, u32[]{:S(2)}, u32[]{:S(2)}) collective-permute-start(bf16[16,32,256]{2,1,0:T(8,128)(2,1)S(1)} %get-tuple-element.13.refs_0_), channel_id=1, source_target_pairs={{0,16},{4,20},{8,24},{12,28},{16,0},{20,4},{24,8},{28,12},{1,17},{... | collective-permute-start | bytes 786440 | tf_op jit(solution)/shard_map/ppermute | solution.py:287
  12.9 1.5 %collective-permute-start.3 = (bf16[16,32,256]{2,1,0:T(8,128)(2,1)S(1)}, bf16[16,32,256]{2,1,0:T(8,128)(2,1)S(1)}, u32[]{:S(2)}, u32[]{:S(2)}) collective-permute-start(bf16[16,32,256]{2,1,0:T(8,128)(2,1)S(1)} %get-tuple-element.13.refs_0_), channel_id=1, source_target_pairs={{0,8},{4,12},{8,0},{12,4},{16,24},{20,28},{24,16},{28,20},{1,9},{5... | collective-permute-start | bytes 786440 | tf_op jit(solution)/shard_map/ppermute | solution.py:287
  14.9 2.6 %collective-permute-start.1 = (bf16[16,32,256]{2,1,0:T(8,128)(2,1)S(1)}, bf16[16,32,256]{2,1,0:T(8,128)(2,1)S(1)}, u32[]{:S(2)}, u32[]{:S(2)}) collective-permute-start(bf16[16,32,256]{2,1,0:T(8,128)(2,1)S(1)} %get-tuple-element.15), channel_id=1, source_target_pairs={{0,2},{1,3},{2,0},{3,1},{4,6},{5,7},{6,4},{7,5},{8,10},{9,11},{10,... | collective-permute-start | bytes 786440 | tf_op jit(solution)/shard_map/ppermute | solution.py:287
  17.5 2.4 %collective-permute-done.refs_1_.refs_0_ = bf16[16,32,256]{2,1,0:T(8,128)(2,1)S(1)} collective-permute-done((bf16[16,32,256]{2,1,0:T(8,128)(2,1)S(1)}, bf16[16,32,256]{2,1,0:T(8,128)(2,1)S(1)}, u32[]{:S(2)}, u32[]{:S(2)}) %collective-permute-start) | collective-permute-done | bytes 262176 | tf_op jit(solution)/shard_map/ppermute | solution.py:287
  19.8 2.3 %collective-permute-done.3.refs_1_.refs_4_ = bf16[16,32,256]{2,1,0:T(8,128)(2,1)S(1)} collective-permute-done((bf16[16,32,256]{2,1,0:T(8,128)(2,1)S(1)}, bf16[16,32,256]{2,1,0:T(8,128)(2,1)S(1)}, u32[]{:S(2)}, u32[]{:S(2)}) %collective-permute-start.3) | collective-permute-done | bytes 262176 | tf_op jit(solution)/shard_map/ppermute | solution.py:287
  22.6 1.5 %collective-permute-start.7 = (bf16[16,32,256]{2,1,0:T(8,128)(2,1)S(1)}, bf16[16,32,256]{2,1,0:T(8,128)(2,1)S(1)}, u32[]{:S(2)}, u32[]{:S(2)}) collective-permute-start(bf16[16,32,256]{2,1,0:T(8,128)(2,1)S(1)} %collective-permute-done.refs_1_.refs_0_), channel_id=1, source_target_pairs={{0,8},{4,12},{8,0},{12,4},{16,24},{20,28},{24,16},{28,20},{1,9},{5... | collective-permute-start | bytes 786440 | tf_op jit(solution)/shard_map/ppermute | solution.py:287
  24.1 4.2 %collective-permute-done.1.refs_2_.refs_0_ = bf16[16,32,256]{2,1,0:T(8,128)(2,1)S(1)} collective-permute-done((bf16[16,32,256]{2,1,0:T(8,128)(2,1)S(1)}, bf16[16,32,256]{2,1,0:T(8,128)(2,1)S(1)}, u32[]{:S(2)}, u32[]{:S(2)}) %collective-permute-start.1) | collective-permute-done | bytes 262176 | tf_op jit(solution)/shard_map/ppermute | solution.py:287
  28.4 3.6 %collective-permute-start.2 = (bf16[16,32,256]{2,1,0:T(8,128)(2,1)S(1)}, bf16[16,32,256]{2,1,0:T(8,128)(2,1)S(1)}, u32[]{:S(2)}, u32[]{:S(2)}) collective-permute-start(bf16[16,32,256]{2,1,0:T(8,128)(2,1)S(1)} %get-tuple-element.17), channel_id=1, source_target_pairs={{0,3},{1,2},{2,1},{3,0},{4,7},{5,6},{6,5},{7,4},{8,11},{9,10},{10,... | collective-permute-start | bytes 786440 | tf_op jit(solution)/shard_map/ppermute | solution.py:287
  31.9 1.6 %collective-permute-start.13 = (bf16[16,32,256]{2,1,0:T(8,128)(2,1)S(1)}, bf16[16,32,256]{2,1,0:T(8,128)(2,1)S(1)}, u32[]{:S(2)}, u32[]{:S(2)}) collective-permute-start(bf16[16,32,256]{2,1,0:T(8,128)(2,1)S(1)} %collective-permute-done.1.refs_2_.refs_0_), channel_id=1, source_target_pairs={{0,16},{4,20},{8,24},{12,28},{16,0},{20,4},{24,8},{28,12},{1,17},{... | collective-permute-start | bytes 786440 | tf_op jit(solution)/shard_map/ppermute | solution.py:287
  33.5 1.5 %collective-permute-start.12 = (bf16[16,32,256]{2,1,0:T(8,128)(2,1)S(1)}, bf16[16,32,256]{2,1,0:T(8,128)(2,1)S(1)}, u32[]{:S(2)}, u32[]{:S(2)}) collective-permute-start(bf16[16,32,256]{2,1,0:T(8,128)(2,1)S(1)} %collective-permute-done.1.refs_2_.refs_0_), channel_id=1, source_target_pairs={{0,8},{4,12},{8,0},{12,4},{16,24},{20,28},{24,16},{28,20},{1,9},{5... | collective-permute-start | bytes 786440 | tf_op jit(solution)/shard_map/ppermute | solution.py:287
  35.4 1.3 %collective-permute-done.2.refs_3_.refs_4_ = bf16[16,32,256]{2,1,0:T(8,128)(2,1)S(1)} collective-permute-done((bf16[16,32,256]{2,1,0:T(8,128)(2,1)S(1)}, bf16[16,32,256]{2,1,0:T(8,128)(2,1)S(1)}, u32[]{:S(2)}, u32[]{:S(2)}) %collective-permute-start.2) | collective-permute-done | bytes 262176 | tf_op jit(solution)/shard_map/ppermute | solution.py:287
  36.6 1.7 %collective-permute-done.13.refs_2_.refs_12_ = bf16[16,32,256]{2,1,0:T(8,128)(2,1)S(1)} collective-permute-done((bf16[16,32,256]{2,1,0:T(8,128)(2,1)S(1)}, bf16[16,32,256]{2,1,0:T(8,128)(2,1)S(1)}, u32[]{:S(2)}, u32[]{:S(2)}) %collective-permute-start.13) | collective-permute-done | bytes 262176 | tf_op jit(solution)/shard_map/ppermute | solution.py:287
  38.4 1.7 %collective-permute-done.12.refs_1_.refs_11_ = bf16[16,32,256]{2,1,0:T(8,128)(2,1)S(1)} collective-permute-done((bf16[16,32,256]{2,1,0:T(8,128)(2,1)S(1)}, bf16[16,32,256]{2,1,0:T(8,128)(2,1)S(1)}, u32[]{:S(2)}, u32[]{:S(2)}) %collective-permute-start.12) | collective-permute-done | bytes 262176 | tf_op jit(solution)/shard_map/ppermute | solution.py:287
  40.4 1.5 %collective-permute-start.15 = (bf16[16,32,256]{2,1,0:T(8,128)(2,1)S(1)}, bf16[16,32,256]{2,1,0:T(8,128)(2,1)S(1)}, u32[]{:S(2)}, u32[]{:S(2)}) collective-permute-start(bf16[16,32,256]{2,1,0:T(8,128)(2,1)S(1)} %collective-permute-done.2.refs_3_.refs_4_), channel_id=1, source_target_pairs={{0,8},{4,12},{8,0},{12,4},{16,24},{20,28},{24,16},{28,20},{1,9},{5... | collective-permute-start | bytes 786440 | tf_op jit(solution)/shard_map/ppermute | solution.py:287
  42.1 0.6 collective-permute-start.9
  42.9 1.8 %collective-permute-start.10 = (bf16[8,32,256]{2,1,0:T(8,128)(2,1)S(1)}, bf16[8,32,256]{2,1,0:T(8,128)(2,1)S(1)}, u32[]{:S(2)}, u32[]{:S(2)}) collective-permute-start(bf16[8,32,256]{2,1,0:T(8,128)(2,1)S(1)} %slice.25), channel_id=1, source_target_pairs={{0,16},{4,20},{8,24},{12,28},{16,0},{20,4},{24,8},{28,12},{1,17},{... | collective-permute-start | bytes 393224 | tf_op jit(solution)/shard_map/ppermute | solution.py:287
  44.7 1.6 %collective-permute-start.14 = (bf16[8,32,256]{2,1,0:T(8,128)(2,1)S(1)}, bf16[8,32,256]{2,1,0:T(8,128)(2,1)S(1)}, u32[]{:S(2)}, u32[]{:S(2)}) collective-permute-start(bf16[8,32,256]{2,1,0:T(8,128)(2,1)S(1)} %slice.26), channel_id=1, source_target_pairs={{0,8},{4,12},{8,0},{12,4},{16,24},{20,28},{24,16},{28,20},{1,9},{5... | collective-permute-start | bytes 393224 | tf_op jit(solution)/shard_map/ppermute | solution.py:287
  46.3 2.5 %collective-permute-done.16.refs_6_.refs_16_ = bf16[16,32,256]{2,1,0:T(8,128)(2,1)S(1)} collective-permute-done((bf16[16,32,256]{2,1,0:T(8,128)(2,1)S(1)}, bf16[16,32,256]{2,1,0:T(8,128)(2,1)S(1)}, u32[]{:S(2)}, u32[]{:S(2)}) %collective-permute-start.16) | collective-permute-done | bytes 262176 | tf_op jit(solution)/shard_map/ppermute | solution.py:287
  48.8 0.8 %collective-permute-done.15.refs_5_.refs_15_ = bf16[16,32,256]{2,1,0:T(8,128)(2,1)S(1)} collective-permute-done((bf16[16,32,256]{2,1,0:T(8,128)(2,1)S(1)}, bf16[16,32,256]{2,1,0:T(8,128)(2,1)S(1)}, u32[]{:S(2)}, u32[]{:S(2)}) %collective-permute-start.15) | collective-permute-done | bytes 262176 | tf_op jit(solution)/shard_map/ppermute | solution.py:287
  49.7 1.5 %collective-permute-start.17 = (bf16[8,32,256]{2,1,0:T(8,128)(2,1)S(1)}, bf16[8,32,256]{2,1,0:T(8,128)(2,1)S(1)}, u32[]{:S(2)}, u32[]{:S(2)}) collective-permute-start(bf16[8,32,256]{2,1,0:T(8,128)(2,1)S(1)} %slice.27), channel_id=1, source_target_pairs={{0,8},{4,12},{8,0},{12,4},{16,24},{20,28},{24,16},{28,20},{1,9},{5... | collective-permute-start | bytes 393224 | tf_op jit(solution)/shard_map/ppermute | solution.py:287
  51.2 1.3 %collective-permute-start.20 = (bf16[8,32,256]{2,1,0:T(8,128)(2,1)S(1)}, bf16[8,32,256]{2,1,0:T(8,128)(2,1)S(1)}, u32[]{:S(2)}, u32[]{:S(2)}) collective-permute-start(bf16[8,32,256]{2,1,0:T(8,128)(2,1)S(1)} %slice.29), channel_id=1, source_target_pairs={{0,16},{4,20},{8,24},{12,28},{16,0},{20,4},{24,8},{28,12},{1,17},{... | collective-permute-start | bytes 393224 | tf_op jit(solution)/shard_map/ppermute | solution.py:287
  52.5 0.6 pick.4
  53.2 0.6 pick.5
  53.8 0.6 collective-permute-start.11
  54.6 0.6 pick.6
  55.3 0.9 %collective-permute-done.20.refs_7_.refs_18_ = bf16[8,32,256]{2,1,0:T(8,128)(2,1)S(1)} collective-permute-done((bf16[8,32,256]{2,1,0:T(8,128)(2,1)S(1)}, bf16[8,32,256]{2,1,0:T(8,128)(2,1)S(1)}, u32[]{:S(2)}, u32[]{:S(2)}) %collective-permute-start.20) | collective-permute-done | bytes 131104 | tf_op jit(solution)/shard_map/ppermute | solution.py:287
  56.2 0.6 pick.7
  56.9 1.0 %left_side.1.left_ref = bf16[8,512,256]{2,1,0:T(8,128)(2,1)S(1)} custom-call(bf16[16,32,256]{2,1,0:T(8,128)(2,1)S(1)} %get-tuple-element.13.refs_0_, bf16[16,32,256]{2,1,0:T(8,128)(2,1)S(1)} %collective-permute-done.refs_1_.refs_0_, bf16[16,32,256]{2,1,0:T(8,128)(2,1)S(1)} %collective-permute-done.1.refs_2_.refs_0_, ...), custom_call_target="tpu_custom_call" | custom-call | tf_op jit(solution)/shard_map/left_side/pallas_call | solution.py:190
  57.9 0.9 %collective-permute-done.21.refs_3_ = bf16[2,16,32,256]{3,2,1,0:T(8,128)(2,1)S(1)} collective-permute-done((bf16[2,16,32,256]{3,2,1,0:T(8,128)(2,1)S(1)}, bf16[2,16,32,256]{3,2,1,0:T(8,128)(2,1)S(1)}, u32[]{:S(2)}, u32[]{:S(2)}) %collective-permute-start.21) | collective-permute-done | bytes 524320 | tf_op jit(solution)/shard_map/ppermute | solution.py:287
  58.8 4.5 %cross_spectra.1 = f32[2,8,2,256,256]{4,3,2,1,0:T(8,128)} custom-call(s32[2]{0:T(128)S(1)} %broadcast_xor_fusion.1.far_ref, bf16[8,512,256]{2,1,0:T(8,128)(2,1)S(1)} %left_side.1.left_ref, bf16[2,16,32,256]{3,2,1,0:T(8,128)(2,1)S(1)} %collective-permute-done.6.refs_0_, bf16[2,16,32,256]{3,2,1,0:T(8,128)(2,1)S(1)} %collective-permute-done.11.refs_1_, ...), custom_call_target="tpu_custom_call" | custom-call | flops 1073741824 | bytes 8388608 | tf_op jit(solution)/shard_map/cross_spectra/pallas_call | solution.py:261
  (37 shorter events, 2.5 us)
Async XLA Ops:
  0.0 35.0 %copy-start.1 = (s32[8]{0:T(128)S(1)}, s32[8]{0:T(128)}, u32[]{:S(2)}) copy-start(s32[8]{0:T(128)} %param.5) | copy-start | bytes 100
  0.0 35.2 %copy-start = (s32[2,8]{1,0:T(2,128)S(1)}, s32[2,8]{1,0:T(2,128)}, u32[]{:S(2)}) copy-start(s32[2,8]{1,0:T(2,128)} %param.4) | copy-start | bytes 196
  8.3 11.5 %collective-permute-start = (bf16[16,32,256]{2,1,0:T(8,128)(2,1)S(1)}, bf16[16,32,256]{2,1,0:T(8,128)(2,1)S(1)}, u32[]{:S(2)}, u32[]{:S(2)}) collective-permute-start(bf16[16,32,256]{2,1,0:T(8,128)(2,1)S(1)} %get-tuple-element.14), channel_id=1, source_target_pairs={{0,1},{1,0},{2,3},{3,2},{4,5},{5,4},{6,7},{7,6},{8,9},{9,8},{10,11... | collective-permute-start | bytes 786440 | tf_op jit(solution)/shard_map/ppermute | solution.py:287
  11.4 8.4 %collective-permute-start.4 = (bf16[16,32,256]{2,1,0:T(8,128)(2,1)S(1)}, bf16[16,32,256]{2,1,0:T(8,128)(2,1)S(1)}, u32[]{:S(2)}, u32[]{:S(2)}) collective-permute-start(bf16[16,32,256]{2,1,0:T(8,128)(2,1)S(1)} %get-tuple-element.13.refs_0_), channel_id=1, source_target_pairs={{0,16},{4,20},{8,24},{12,28},{16,0},{20,4},{24,8},{28,12},{1,17},{... | collective-permute-start | bytes 786440 | tf_op jit(solution)/shard_map/ppermute | solution.py:287
  12.9 9.2 %collective-permute-start.3 = (bf16[16,32,256]{2,1,0:T(8,128)(2,1)S(1)}, bf16[16,32,256]{2,1,0:T(8,128)(2,1)S(1)}, u32[]{:S(2)}, u32[]{:S(2)}) collective-permute-start(bf16[16,32,256]{2,1,0:T(8,128)(2,1)S(1)} %get-tuple-element.13.refs_0_), channel_id=1, source_target_pairs={{0,8},{4,12},{8,0},{12,4},{16,24},{20,28},{24,16},{28,20},{1,9},{5... | collective-permute-start | bytes 786440 | tf_op jit(solution)/shard_map/ppermute | solution.py:287
  14.4 17.6 %collective-permute-start.5 = (bf16[16,32,256]{2,1,0:T(8,128)(2,1)S(1)}, bf16[16,32,256]{2,1,0:T(8,128)(2,1)S(1)}, u32[]{:S(2)}, u32[]{:S(2)}) collective-permute-start(bf16[16,32,256]{2,1,0:T(8,128)(2,1)S(1)} %get-tuple-element.13.refs_0_), channel_id=1, source_target_pairs={{0,24},{4,28},{8,16},{12,20},{16,8},{20,12},{24,0},{28,4},{1,25},{... | collective-permute-start | bytes 786440 | tf_op jit(solution)/shard_map/ppermute | solution.py:287
  14.9 13.5 %collective-permute-start.1 = (bf16[16,32,256]{2,1,0:T(8,128)(2,1)S(1)}, bf16[16,32,256]{2,1,0:T(8,128)(2,1)S(1)}, u32[]{:S(2)}, u32[]{:S(2)}) collective-permute-start(bf16[16,32,256]{2,1,0:T(8,128)(2,1)S(1)} %get-tuple-element.15), channel_id=1, source_target_pairs={{0,2},{1,3},{2,0},{3,1},{4,6},{5,7},{6,4},{7,5},{8,10},{9,11},{10,... | collective-permute-start | bytes 786440 | tf_op jit(solution)/shard_map/ppermute | solution.py:287
  22.1 9.8 %collective-permute-start.8 = (bf16[16,32,256]{2,1,0:T(8,128)(2,1)S(1)}, bf16[16,32,256]{2,1,0:T(8,128)(2,1)S(1)}, u32[]{:S(2)}, u32[]{:S(2)}) collective-permute-start(bf16[16,32,256]{2,1,0:T(8,128)(2,1)S(1)} %collective-permute-done.refs_1_.refs_0_), channel_id=1, source_target_pairs={{0,16},{4,20},{8,24},{12,28},{16,0},{20,4},{24,8},{28,12},{1,17},{... | collective-permute-start | bytes 786440 | tf_op jit(solution)/shard_map/ppermute | solution.py:287
  22.6 9.3 %collective-permute-start.7 = (bf16[16,32,256]{2,1,0:T(8,128)(2,1)S(1)}, bf16[16,32,256]{2,1,0:T(8,128)(2,1)S(1)}, u32[]{:S(2)}, u32[]{:S(2)}) collective-permute-start(bf16[16,32,256]{2,1,0:T(8,128)(2,1)S(1)} %collective-permute-done.refs_1_.refs_0_), channel_id=1, source_target_pairs={{0,8},{4,12},{8,0},{12,4},{16,24},{20,28},{24,16},{28,20},{1,9},{5... | collective-permute-start | bytes 786440 | tf_op jit(solution)/shard_map/ppermute | solution.py:287
  28.4 8.3 %collective-permute-start.2 = (bf16[16,32,256]{2,1,0:T(8,128)(2,1)S(1)}, bf16[16,32,256]{2,1,0:T(8,128)(2,1)S(1)}, u32[]{:S(2)}, u32[]{:S(2)}) collective-permute-start(bf16[16,32,256]{2,1,0:T(8,128)(2,1)S(1)} %get-tuple-element.17), channel_id=1, source_target_pairs={{0,3},{1,2},{2,1},{3,0},{4,7},{5,6},{6,5},{7,4},{8,11},{9,10},{10,... | collective-permute-start | bytes 786440 | tf_op jit(solution)/shard_map/ppermute | solution.py:287
  31.9 6.4 %collective-permute-start.13 = (bf16[16,32,256]{2,1,0:T(8,128)(2,1)S(1)}, bf16[16,32,256]{2,1,0:T(8,128)(2,1)S(1)}, u32[]{:S(2)}, u32[]{:S(2)}) collective-permute-start(bf16[16,32,256]{2,1,0:T(8,128)(2,1)S(1)} %collective-permute-done.1.refs_2_.refs_0_), channel_id=1, source_target_pairs={{0,16},{4,20},{8,24},{12,28},{16,0},{20,4},{24,8},{28,12},{1,17},{... | collective-permute-start | bytes 786440 | tf_op jit(solution)/shard_map/ppermute | solution.py:287
  33.5 6.6 %collective-permute-start.12 = (bf16[16,32,256]{2,1,0:T(8,128)(2,1)S(1)}, bf16[16,32,256]{2,1,0:T(8,128)(2,1)S(1)}, u32[]{:S(2)}, u32[]{:S(2)}) collective-permute-start(bf16[16,32,256]{2,1,0:T(8,128)(2,1)S(1)} %collective-permute-done.1.refs_2_.refs_0_), channel_id=1, source_target_pairs={{0,8},{4,12},{8,0},{12,4},{16,24},{20,28},{24,16},{28,20},{1,9},{5... | collective-permute-start | bytes 786440 | tf_op jit(solution)/shard_map/ppermute | solution.py:287
  40.1 8.7 %collective-permute-start.16 = (bf16[16,32,256]{2,1,0:T(8,128)(2,1)S(1)}, bf16[16,32,256]{2,1,0:T(8,128)(2,1)S(1)}, u32[]{:S(2)}, u32[]{:S(2)}) collective-permute-start(bf16[16,32,256]{2,1,0:T(8,128)(2,1)S(1)} %collective-permute-done.2.refs_3_.refs_4_), channel_id=1, source_target_pairs={{0,16},{4,20},{8,24},{12,28},{16,0},{20,4},{24,8},{28,12},{1,17},{... | collective-permute-start | bytes 786440 | tf_op jit(solution)/shard_map/ppermute | solution.py:287
  40.4 9.2 %collective-permute-start.15 = (bf16[16,32,256]{2,1,0:T(8,128)(2,1)S(1)}, bf16[16,32,256]{2,1,0:T(8,128)(2,1)S(1)}, u32[]{:S(2)}, u32[]{:S(2)}) collective-permute-start(bf16[16,32,256]{2,1,0:T(8,128)(2,1)S(1)} %collective-permute-done.2.refs_3_.refs_4_), channel_id=1, source_target_pairs={{0,8},{4,12},{8,0},{12,4},{16,24},{20,28},{24,16},{28,20},{1,9},{5... | collective-permute-start | bytes 786440 | tf_op jit(solution)/shard_map/ppermute | solution.py:287
  42.1 9.0 %collective-permute-start.9 = (bf16[8,32,256]{2,1,0:T(8,128)(2,1)S(1)}, bf16[8,32,256]{2,1,0:T(8,128)(2,1)S(1)}, u32[]{:S(2)}, u32[]{:S(2)}) collective-permute-start(bf16[8,32,256]{2,1,0:T(8,128)(2,1)S(1)} %slice.24), channel_id=1, source_target_pairs={{0,8},{4,12},{8,0},{12,4},{16,24},{20,28},{24,16},{28,20},{1,9},{5... | collective-permute-start | bytes 393224 | tf_op jit(solution)/shard_map/ppermute | solution.py:287
  42.9 10.2 %collective-permute-start.10 = (bf16[8,32,256]{2,1,0:T(8,128)(2,1)S(1)}, bf16[8,32,256]{2,1,0:T(8,128)(2,1)S(1)}, u32[]{:S(2)}, u32[]{:S(2)}) collective-permute-start(bf16[8,32,256]{2,1,0:T(8,128)(2,1)S(1)} %slice.25), channel_id=1, source_target_pairs={{0,16},{4,20},{8,24},{12,28},{16,0},{20,4},{24,8},{28,12},{1,17},{... | collective-permute-start | bytes 393224 | tf_op jit(solution)/shard_map/ppermute | solution.py:287
  44.7 9.1 %collective-permute-start.14 = (bf16[8,32,256]{2,1,0:T(8,128)(2,1)S(1)}, bf16[8,32,256]{2,1,0:T(8,128)(2,1)S(1)}, u32[]{:S(2)}, u32[]{:S(2)}) collective-permute-start(bf16[8,32,256]{2,1,0:T(8,128)(2,1)S(1)} %slice.26), channel_id=1, source_target_pairs={{0,8},{4,12},{8,0},{12,4},{16,24},{20,28},{24,16},{28,20},{1,9},{5... | collective-permute-start | bytes 393224 | tf_op jit(solution)/shard_map/ppermute | solution.py:287
  48.8 6.5 %collective-permute-start.19 = (bf16[8,32,256]{2,1,0:T(8,128)(2,1)S(1)}, bf16[8,32,256]{2,1,0:T(8,128)(2,1)S(1)}, u32[]{:S(2)}, u32[]{:S(2)}) collective-permute-start(bf16[8,32,256]{2,1,0:T(8,128)(2,1)S(1)} %slice.28), channel_id=1, source_target_pairs={{0,16},{4,20},{8,24},{12,28},{16,0},{20,4},{24,8},{28,12},{1,17},{... | collective-permute-start | bytes 393224 | tf_op jit(solution)/shard_map/ppermute | solution.py:287
  49.7 5.0 %collective-permute-start.17 = (bf16[8,32,256]{2,1,0:T(8,128)(2,1)S(1)}, bf16[8,32,256]{2,1,0:T(8,128)(2,1)S(1)}, u32[]{:S(2)}, u32[]{:S(2)}) collective-permute-start(bf16[8,32,256]{2,1,0:T(8,128)(2,1)S(1)} %slice.27), channel_id=1, source_target_pairs={{0,8},{4,12},{8,0},{12,4},{16,24},{20,28},{24,16},{28,20},{1,9},{5... | collective-permute-start | bytes 393224 | tf_op jit(solution)/shard_map/ppermute | solution.py:287
  51.2 5.0 %collective-permute-start.20 = (bf16[8,32,256]{2,1,0:T(8,128)(2,1)S(1)}, bf16[8,32,256]{2,1,0:T(8,128)(2,1)S(1)}, u32[]{:S(2)}, u32[]{:S(2)}) collective-permute-start(bf16[8,32,256]{2,1,0:T(8,128)(2,1)S(1)} %slice.29), channel_id=1, source_target_pairs={{0,16},{4,20},{8,24},{12,28},{16,0},{20,4},{24,8},{28,12},{1,17},{... | collective-permute-start | bytes 393224 | tf_op jit(solution)/shard_map/ppermute | solution.py:287
  53.1 4.8 %collective-permute-start.6 = (bf16[2,16,32,256]{3,2,1,0:T(8,128)(2,1)S(1)}, bf16[2,16,32,256]{3,2,1,0:T(8,128)(2,1)S(1)}, u32[]{:S(2)}, u32[]{:S(2)}) collective-permute-start(bf16[2,16,32,256]{3,2,1,0:T(8,128)(2,1)S(1)} %pick.4), channel_id=1, source_target_pairs={{0,4},{4,0},{8,12},{12,8},{16,20},{20,16},{24,28},{28,24},{1,5},{5... | collective-permute-start | bytes 1572872 | tf_op jit(solution)/shard_map/ppermute | solution.py:287
  53.8 4.1 %collective-permute-start.11 = (bf16[2,16,32,256]{3,2,1,0:T(8,128)(2,1)S(1)}, bf16[2,16,32,256]{3,2,1,0:T(8,128)(2,1)S(1)}, u32[]{:S(2)}, u32[]{:S(2)}) collective-permute-start(bf16[2,16,32,256]{3,2,1,0:T(8,128)(2,1)S(1)} %pick.5), channel_id=1, source_target_pairs={{0,4},{4,0},{8,12},{12,8},{16,20},{20,16},{24,28},{28,24},{1,5},{5... | collective-permute-start | bytes 1572872 | tf_op jit(solution)/shard_map/ppermute | solution.py:287
  55.3 2.7 %collective-permute-start.18 = (bf16[2,16,32,256]{3,2,1,0:T(8,128)(2,1)S(1)}, bf16[2,16,32,256]{3,2,1,0:T(8,128)(2,1)S(1)}, u32[]{:S(2)}, u32[]{:S(2)}) collective-permute-start(bf16[2,16,32,256]{3,2,1,0:T(8,128)(2,1)S(1)} %pick.6), channel_id=1, source_target_pairs={{0,4},{4,0},{8,12},{12,8},{16,20},{20,16},{24,28},{28,24},{1,5},{5... | collective-permute-start | bytes 1572872 | tf_op jit(solution)/shard_map/ppermute | solution.py:287
  56.8 2.0 %collective-permute-start.21 = (bf16[2,16,32,256]{3,2,1,0:T(8,128)(2,1)S(1)}, bf16[2,16,32,256]{3,2,1,0:T(8,128)(2,1)S(1)}, u32[]{:S(2)}, u32[]{:S(2)}) collective-permute-start(bf16[2,16,32,256]{3,2,1,0:T(8,128)(2,1)S(1)} %pick.7), channel_id=1, source_target_pairs={{0,4},{4,0},{8,12},{12,8},{16,20},{20,16},{24,28},{28,24},{1,5},{5... | collective-permute-start | bytes 1572872 | tf_op jit(solution)/shard_map/ppermute | solution.py:287

commit v6 on v5

--- a/solution.py
+++ b/solution.py
@@ -318,12 +318,12 @@
     own, found = [], []
     for s, piece in enumerate(sent):
         if s:
-            piece = swap(after(piece, own[2]) if s == 3 else piece, "win", s)
+            piece = swap(after(piece, own[2], own[1]) if s == 3 else piece, "win", s)
         own.append(piece)
     for s, piece in enumerate(own):
         if s >= 1:
             near = [part for at in (2, 4) for part in found[s - 1].get(at, [])]
-            piece = after(piece, *near, *(found[s - 2].get(6, []) if s == 2 else []))
+            piece = after(piece, *(near if s < 3 else near[:1]), *(found[s - 2].get(6, []) if s == 2 else []))
         found.append(gather_even(piece, relay=s > 0))
     left = left_side(own, windows)
     half = rows // 2

time: 63.4 us -> 63.1 us (level)
  waiting for transfers between devices: 19 us -> 17.8 us
  starting transfers between devices: 27.1 us -> 28.1 us
    ppermute x22, waiting for transfers between devices: 19 us -> 17.8 us  [swap(): return lax.ppermute(value, axis, [(i, i ^ distance) for i in range(count)])]
    ppermute x22, starting transfers between devices: 27.1 us -> 28.1 us  [swap(): return lax.ppermute(value, axis, [(i, i ^ distance) for i in range(count)])]
  transfers between devices with their start and end apart: 22 -> 22, of which waited for: 11 -> 8; matrix products, arithmetic and copies ran while one was open for 1% -> 1% of each run, Pallas kernels for 5% -> 5%
where the time goes in v6:
time: 63.1 us; the launch traced here: 63 us
  starting transfers between devices  28.1 us (45%)
  waiting for transfers between devices  17.8 us (28%)
  Pallas kernels  16.2 us (26%)
  other arithmetic  0.69 us (1%)
    ppermute x22, starting transfers between devices, swap(): return lax.ppermute(value, axis, [(i, i ^ distance) for i in range(count)])  28.1 us
    ppermute x22, waiting for transfers between devices, swap(): return lax.ppermute(value, axis, [(i, i ^ distance) for i in range(count)])  17.8 us
    pallas_call x1, Pallas kernels, local_spectra(): pl.pallas_call(functools.partial(spectra_kernel, chan_rows, win_count, pi...  8.27 us
    pallas_call x1, Pallas kernels, correlate(): pl.pallas_call(functools.partial(correlate_kernel, scale, layout), in_spe...  4.45 us
    pallas_call x4, Pallas kernels, pick(): pl.pallas_call(functools.partial(pick_kernel, places), in_specs=[pl.Block...  2.47 us
  transfers between devices with their start and end apart: 22, of which 8 were waited for; matrix products, arithmetic and copies ran while one was open for 1% of the time, Pallas kernels for 5%

profile of v6, /device:TPU:0, one launch (start us, length us, event | category | flops | bytes accessed | tf_op | source)
XLA Modules:
  0.0 63.0 jit_solution(16188856786790324852)
XLA Ops:
  0.0 8.3 %spectra.1 = (bf16[16,32,256]{2,1,0:T(8,128)(2,1)S(1)}, bf16[16,32,256]{2,1,0:T(8,128)(2,1)S(1)}, bf16[16,32,256]{2,1,0:T(8,128)(2,1)S(1)}, bf16[16,32,256]{2,1,0:T(8,128)(2,1)S(1)}) custom-call(s32[1]{0:T(128)} %bitcast.win_ref, bf16[256,32,1024]{2,1,0:T(8,128)(2,1)} %traces_ref.1), custom_call_target="tpu_custom_call" | custom-call | flops 1073741824 | bytes 16777216 | tf_op jit(solution)/shard_map/spectra/pallas_call | solution.py:105
  8.3 3.1 %collective-permute-start = (bf16[16,32,256]{2,1,0:T(8,128)(2,1)S(1)}, bf16[16,32,256]{2,1,0:T(8,128)(2,1)S(1)}, u32[]{:S(2)}, u32[]{:S(2)}) collective-permute-start(bf16[16,32,256]{2,1,0:T(8,128)(2,1)S(1)} %get-tuple-element.14), channel_id=1, source_target_pairs={{0,1},{1,0},{2,3},{3,2},{4,5},{5,4},{6,7},{7,6},{8,9},{9,8},{10,11... | collective-permute-start | bytes 786440 | tf_op jit(solution)/shard_map/ppermute | solution.py:287
  11.4 1.5 %collective-permute-start.4 = (bf16[16,32,256]{2,1,0:T(8,128)(2,1)S(1)}, bf16[16,32,256]{2,1,0:T(8,128)(2,1)S(1)}, u32[]{:S(2)}, u32[]{:S(2)}) collective-permute-start(bf16[16,32,256]{2,1,0:T(8,128)(2,1)S(1)} %get-tuple-element.13.refs_0_), channel_id=1, source_target_pairs={{0,16},{4,20},{8,24},{12,28},{16,0},{20,4},{24,8},{28,12},{1,17},{... | collective-permute-start | bytes 786440 | tf_op jit(solution)/shard_map/ppermute | solution.py:287
  12.9 1.5 %collective-permute-start.3 = (bf16[16,32,256]{2,1,0:T(8,128)(2,1)S(1)}, bf16[16,32,256]{2,1,0:T(8,128)(2,1)S(1)}, u32[]{:S(2)}, u32[]{:S(2)}) collective-permute-start(bf16[16,32,256]{2,1,0:T(8,128)(2,1)S(1)} %get-tuple-element.13.refs_0_), channel_id=1, source_target_pairs={{0,8},{4,12},{8,0},{12,4},{16,24},{20,28},{24,16},{28,20},{1,9},{5... | collective-permute-start | bytes 786440 | tf_op jit(solution)/shard_map/ppermute | solution.py:287
  14.9 2.6 %collective-permute-start.1 = (bf16[16,32,256]{2,1,0:T(8,128)(2,1)S(1)}, bf16[16,32,256]{2,1,0:T(8,128)(2,1)S(1)}, u32[]{:S(2)}, u32[]{:S(2)}) collective-permute-start(bf16[16,32,256]{2,1,0:T(8,128)(2,1)S(1)} %get-tuple-element.15), channel_id=1, source_target_pairs={{0,2},{1,3},{2,0},{3,1},{4,6},{5,7},{6,4},{7,5},{8,10},{9,11},{10,... | collective-permute-start | bytes 786440 | tf_op jit(solution)/shard_map/ppermute | solution.py:287
  17.5 2.4 %collective-permute-done.refs_1_.refs_0_ = bf16[16,32,256]{2,1,0:T(8,128)(2,1)S(1)} collective-permute-done((bf16[16,32,256]{2,1,0:T(8,128)(2,1)S(1)}, bf16[16,32,256]{2,1,0:T(8,128)(2,1)S(1)}, u32[]{:S(2)}, u32[]{:S(2)}) %collective-permute-start) | collective-permute-done | bytes 262176 | tf_op jit(solution)/shard_map/ppermute | solution.py:287
  19.8 2.3 %collective-permute-done.3.refs_1_.refs_4_ = bf16[16,32,256]{2,1,0:T(8,128)(2,1)S(1)} collective-permute-done((bf16[16,32,256]{2,1,0:T(8,128)(2,1)S(1)}, bf16[16,32,256]{2,1,0:T(8,128)(2,1)S(1)}, u32[]{:S(2)}, u32[]{:S(2)}) %collective-permute-start.3) | collective-permute-done | bytes 262176 | tf_op jit(solution)/shard_map/ppermute | solution.py:287
  22.6 1.5 %collective-permute-start.7 = (bf16[16,32,256]{2,1,0:T(8,128)(2,1)S(1)}, bf16[16,32,256]{2,1,0:T(8,128)(2,1)S(1)}, u32[]{:S(2)}, u32[]{:S(2)}) collective-permute-start(bf16[16,32,256]{2,1,0:T(8,128)(2,1)S(1)} %collective-permute-done.refs_1_.refs_0_), channel_id=1, source_target_pairs={{0,8},{4,12},{8,0},{12,4},{16,24},{20,28},{24,16},{28,20},{1,9},{5... | collective-permute-start | bytes 786440 | tf_op jit(solution)/shard_map/ppermute | solution.py:287
  24.1 4.2 %collective-permute-done.1.refs_2_.refs_0_ = bf16[16,32,256]{2,1,0:T(8,128)(2,1)S(1)} collective-permute-done((bf16[16,32,256]{2,1,0:T(8,128)(2,1)S(1)}, bf16[16,32,256]{2,1,0:T(8,128)(2,1)S(1)}, u32[]{:S(2)}, u32[]{:S(2)}) %collective-permute-start.1) | collective-permute-done | bytes 262176 | tf_op jit(solution)/shard_map/ppermute | solution.py:287
  28.4 3.6 %collective-permute-start.2 = (bf16[16,32,256]{2,1,0:T(8,128)(2,1)S(1)}, bf16[16,32,256]{2,1,0:T(8,128)(2,1)S(1)}, u32[]{:S(2)}, u32[]{:S(2)}) collective-permute-start(bf16[16,32,256]{2,1,0:T(8,128)(2,1)S(1)} %get-tuple-element.17), channel_id=1, source_target_pairs={{0,3},{1,2},{2,1},{3,0},{4,7},{5,6},{6,5},{7,4},{8,11},{9,10},{10,... | collective-permute-start | bytes 786440 | tf_op jit(solution)/shard_map/ppermute | solution.py:287
  31.9 1.6 %collective-permute-start.12 = (bf16[16,32,256]{2,1,0:T(8,128)(2,1)S(1)}, bf16[16,32,256]{2,1,0:T(8,128)(2,1)S(1)}, u32[]{:S(2)}, u32[]{:S(2)}) collective-permute-start(bf16[16,32,256]{2,1,0:T(8,128)(2,1)S(1)} %collective-permute-done.1.refs_2_.refs_0_), channel_id=1, source_target_pairs={{0,8},{4,12},{8,0},{12,4},{16,24},{20,28},{24,16},{28,20},{1,9},{5... | collective-permute-start | bytes 786440 | tf_op jit(solution)/shard_map/ppermute | solution.py:287
  33.8 1.6 %collective-permute-start.13 = (bf16[16,32,256]{2,1,0:T(8,128)(2,1)S(1)}, bf16[16,32,256]{2,1,0:T(8,128)(2,1)S(1)}, u32[]{:S(2)}, u32[]{:S(2)}) collective-permute-start(bf16[16,32,256]{2,1,0:T(8,128)(2,1)S(1)} %collective-permute-done.1.refs_2_.refs_0_), channel_id=1, source_target_pairs={{0,16},{4,20},{8,24},{12,28},{16,0},{20,4},{24,8},{28,12},{1,17},{... | collective-permute-start | bytes 786440 | tf_op jit(solution)/shard_map/ppermute | solution.py:287
  35.4 1.2 %collective-permute-done.2.refs_3_.refs_4_ = bf16[16,32,256]{2,1,0:T(8,128)(2,1)S(1)} collective-permute-done((bf16[16,32,256]{2,1,0:T(8,128)(2,1)S(1)}, bf16[16,32,256]{2,1,0:T(8,128)(2,1)S(1)}, u32[]{:S(2)}, u32[]{:S(2)}) %collective-permute-start.2) | collective-permute-done | bytes 262176 | tf_op jit(solution)/shard_map/ppermute | solution.py:287
  36.6 1.7 %collective-permute-done.12.refs_1_.refs_11_ = bf16[16,32,256]{2,1,0:T(8,128)(2,1)S(1)} collective-permute-done((bf16[16,32,256]{2,1,0:T(8,128)(2,1)S(1)}, bf16[16,32,256]{2,1,0:T(8,128)(2,1)S(1)}, u32[]{:S(2)}, u32[]{:S(2)}) %collective-permute-start.12) | collective-permute-done | bytes 262176 | tf_op jit(solution)/shard_map/ppermute | solution.py:287
  38.4 1.5 %collective-permute-start.16 = (bf16[16,32,256]{2,1,0:T(8,128)(2,1)S(1)}, bf16[16,32,256]{2,1,0:T(8,128)(2,1)S(1)}, u32[]{:S(2)}, u32[]{:S(2)}) collective-permute-start(bf16[16,32,256]{2,1,0:T(8,128)(2,1)S(1)} %collective-permute-done.2.refs_3_.refs_4_), channel_id=1, source_target_pairs={{0,16},{4,20},{8,24},{12,28},{16,0},{20,4},{24,8},{28,12},{1,17},{... | collective-permute-start | bytes 786440 | tf_op jit(solution)/shard_map/ppermute | solution.py:287
  39.9 1.5 %collective-permute-start.15 = (bf16[16,32,256]{2,1,0:T(8,128)(2,1)S(1)}, bf16[16,32,256]{2,1,0:T(8,128)(2,1)S(1)}, u32[]{:S(2)}, u32[]{:S(2)}) collective-permute-start(bf16[16,32,256]{2,1,0:T(8,128)(2,1)S(1)} %collective-permute-done.2.refs_3_.refs_4_), channel_id=1, source_target_pairs={{0,8},{4,12},{8,0},{12,4},{16,24},{20,28},{24,16},{28,20},{1,9},{5... | collective-permute-start | bytes 786440 | tf_op jit(solution)/shard_map/ppermute | solution.py:287
  41.6 0.6 collective-permute-start.9
  42.4 0.6 collective-permute-start.10
  43.0 1.6 %collective-permute-start.14 = (bf16[8,32,256]{2,1,0:T(8,128)(2,1)S(1)}, bf16[8,32,256]{2,1,0:T(8,128)(2,1)S(1)}, u32[]{:S(2)}, u32[]{:S(2)}) collective-permute-start(bf16[8,32,256]{2,1,0:T(8,128)(2,1)S(1)} %slice.26), channel_id=1, source_target_pairs={{0,8},{4,12},{8,0},{12,4},{16,24},{20,28},{24,16},{28,20},{1,9},{5... | collective-permute-start | bytes 393224 | tf_op jit(solution)/shard_map/ppermute | solution.py:287
  44.6 3.5 %collective-permute-done.16.refs_6_.refs_16_ = bf16[16,32,256]{2,1,0:T(8,128)(2,1)S(1)} collective-permute-done((bf16[16,32,256]{2,1,0:T(8,128)(2,1)S(1)}, bf16[16,32,256]{2,1,0:T(8,128)(2,1)S(1)}, u32[]{:S(2)}, u32[]{:S(2)}) %collective-permute-start.16) | collective-permute-done | bytes 262176 | tf_op jit(solution)/shard_map/ppermute | solution.py:287
  48.1 1.9 %collective-permute-start.19 = (bf16[8,32,256]{2,1,0:T(8,128)(2,1)S(1)}, bf16[8,32,256]{2,1,0:T(8,128)(2,1)S(1)}, u32[]{:S(2)}, u32[]{:S(2)}) collective-permute-start(bf16[8,32,256]{2,1,0:T(8,128)(2,1)S(1)} %slice.28), channel_id=1, source_target_pairs={{0,16},{4,20},{8,24},{12,28},{16,0},{20,4},{24,8},{28,12},{1,17},{... | collective-permute-start | bytes 393224 | tf_op jit(solution)/shard_map/ppermute | solution.py:287
  50.0 0.7 %collective-permute-start.17 = (bf16[8,32,256]{2,1,0:T(8,128)(2,1)S(1)}, bf16[8,32,256]{2,1,0:T(8,128)(2,1)S(1)}, u32[]{:S(2)}, u32[]{:S(2)}) collective-permute-start(bf16[8,32,256]{2,1,0:T(8,128)(2,1)S(1)} %slice.27), channel_id=1, source_target_pairs={{0,8},{4,12},{8,0},{12,4},{16,24},{20,28},{24,16},{28,20},{1,9},{5... | collective-permute-start | bytes 393224 | tf_op jit(solution)/shard_map/ppermute | solution.py:287
  50.8 0.6 collective-permute-start.20
  51.3 0.6 pick.4
  52.0 0.6 pick.5
  52.7 0.6 collective-permute-start.11
  53.2 1.8 %collective-permute-done.17.refs_7_.refs_17_ = bf16[8,32,256]{2,1,0:T(8,128)(2,1)S(1)} collective-permute-done((bf16[8,32,256]{2,1,0:T(8,128)(2,1)S(1)}, bf16[8,32,256]{2,1,0:T(8,128)(2,1)S(1)}, u32[]{:S(2)}, u32[]{:S(2)}) %collective-permute-start.17) | collective-permute-done | bytes 131104 | tf_op jit(solution)/shard_map/ppermute | solution.py:287
  55.1 0.6 pick.6
  55.8 0.6 pick.7
  56.4 0.5 collective-permute-start.21
  57.0 1.0 %left_side.1.left_ref = bf16[8,512,256]{2,1,0:T(8,128)(2,1)S(1)} custom-call(bf16[16,32,256]{2,1,0:T(8,128)(2,1)S(1)} %get-tuple-element.13.refs_0_, bf16[16,32,256]{2,1,0:T(8,128)(2,1)S(1)} %collective-permute-done.refs_1_.refs_0_, bf16[16,32,256]{2,1,0:T(8,128)(2,1)S(1)} %collective-permute-done.1.refs_2_.refs_0_, ...), custom_call_target="tpu_custom_call" | custom-call | tf_op jit(solution)/shard_map/left_side/pallas_call | solution.py:190
  58.5 4.4 %cross_spectra.1 = f32[2,8,2,256,256]{4,3,2,1,0:T(8,128)} custom-call(s32[2]{0:T(128)S(1)} %broadcast_xor_fusion.1.far_ref, bf16[8,512,256]{2,1,0:T(8,128)(2,1)S(1)} %left_side.1.left_ref, bf16[2,16,32,256]{3,2,1,0:T(8,128)(2,1)S(1)} %collective-permute-done.6.refs_0_, bf16[2,16,32,256]{3,2,1,0:T(8,128)(2,1)S(1)} %collective-permute-done.11.refs_1_, ...), custom_call_target="tpu_custom_call" | custom-call | flops 1073741824 | bytes 8388608 | tf_op jit(solution)/shard_map/cross_spectra/pallas_call | solution.py:261
  (37 shorter events, 2.4 us)
Async XLA Ops:
  0.0 33.5 %copy-start.1 = (s32[8]{0:T(128)S(1)}, s32[8]{0:T(128)}, u32[]{:S(2)}) copy-start(s32[8]{0:T(128)} %param.5) | copy-start | bytes 100
  0.0 33.7 %copy-start = (s32[2,8]{1,0:T(2,128)S(1)}, s32[2,8]{1,0:T(2,128)}, u32[]{:S(2)}) copy-start(s32[2,8]{1,0:T(2,128)} %param.4) | copy-start | bytes 196
  8.3 11.5 %collective-permute-start = (bf16[16,32,256]{2,1,0:T(8,128)(2,1)S(1)}, bf16[16,32,256]{2,1,0:T(8,128)(2,1)S(1)}, u32[]{:S(2)}, u32[]{:S(2)}) collective-permute-start(bf16[16,32,256]{2,1,0:T(8,128)(2,1)S(1)} %get-tuple-element.14), channel_id=1, source_target_pairs={{0,1},{1,0},{2,3},{3,2},{4,5},{5,4},{6,7},{7,6},{8,9},{9,8},{10,11... | collective-permute-start | bytes 786440 | tf_op jit(solution)/shard_map/ppermute | solution.py:287
  11.4 8.4 %collective-permute-start.4 = (bf16[16,32,256]{2,1,0:T(8,128)(2,1)S(1)}, bf16[16,32,256]{2,1,0:T(8,128)(2,1)S(1)}, u32[]{:S(2)}, u32[]{:S(2)}) collective-permute-start(bf16[16,32,256]{2,1,0:T(8,128)(2,1)S(1)} %get-tuple-element.13.refs_0_), channel_id=1, source_target_pairs={{0,16},{4,20},{8,24},{12,28},{16,0},{20,4},{24,8},{28,12},{1,17},{... | collective-permute-start | bytes 786440 | tf_op jit(solution)/shard_map/ppermute | solution.py:287
  12.9 9.2 %collective-permute-start.3 = (bf16[16,32,256]{2,1,0:T(8,128)(2,1)S(1)}, bf16[16,32,256]{2,1,0:T(8,128)(2,1)S(1)}, u32[]{:S(2)}, u32[]{:S(2)}) collective-permute-start(bf16[16,32,256]{2,1,0:T(8,128)(2,1)S(1)} %get-tuple-element.13.refs_0_), channel_id=1, source_target_pairs={{0,8},{4,12},{8,0},{12,4},{16,24},{20,28},{24,16},{28,20},{1,9},{5... | collective-permute-start | bytes 786440 | tf_op jit(solution)/shard_map/ppermute | solution.py:287
  14.4 17.6 %collective-permute-start.5 = (bf16[16,32,256]{2,1,0:T(8,128)(2,1)S(1)}, bf16[16,32,256]{2,1,0:T(8,128)(2,1)S(1)}, u32[]{:S(2)}, u32[]{:S(2)}) collective-permute-start(bf16[16,32,256]{2,1,0:T(8,128)(2,1)S(1)} %get-tuple-element.13.refs_0_), channel_id=1, source_target_pairs={{0,24},{4,28},{8,16},{12,20},{16,8},{20,12},{24,0},{28,4},{1,25},{... | collective-permute-start | bytes 786440 | tf_op jit(solution)/shard_map/ppermute | solution.py:287
  14.9 13.5 %collective-permute-start.1 = (bf16[16,32,256]{2,1,0:T(8,128)(2,1)S(1)}, bf16[16,32,256]{2,1,0:T(8,128)(2,1)S(1)}, u32[]{:S(2)}, u32[]{:S(2)}) collective-permute-start(bf16[16,32,256]{2,1,0:T(8,128)(2,1)S(1)} %get-tuple-element.15), channel_id=1, source_target_pairs={{0,2},{1,3},{2,0},{3,1},{4,6},{5,7},{6,4},{7,5},{8,10},{9,11},{10,... | collective-permute-start | bytes 786440 | tf_op jit(solution)/shard_map/ppermute | solution.py:287
  22.1 9.8 %collective-permute-start.8 = (bf16[16,32,256]{2,1,0:T(8,128)(2,1)S(1)}, bf16[16,32,256]{2,1,0:T(8,128)(2,1)S(1)}, u32[]{:S(2)}, u32[]{:S(2)}) collective-permute-start(bf16[16,32,256]{2,1,0:T(8,128)(2,1)S(1)} %collective-permute-done.refs_1_.refs_0_), channel_id=1, source_target_pairs={{0,16},{4,20},{8,24},{12,28},{16,0},{20,4},{24,8},{28,12},{1,17},{... | collective-permute-start | bytes 786440 | tf_op jit(solution)/shard_map/ppermute | solution.py:287
  22.6 9.3 %collective-permute-start.7 = (bf16[16,32,256]{2,1,0:T(8,128)(2,1)S(1)}, bf16[16,32,256]{2,1,0:T(8,128)(2,1)S(1)}, u32[]{:S(2)}, u32[]{:S(2)}) collective-permute-start(bf16[16,32,256]{2,1,0:T(8,128)(2,1)S(1)} %collective-permute-done.refs_1_.refs_0_), channel_id=1, source_target_pairs={{0,8},{4,12},{8,0},{12,4},{16,24},{20,28},{24,16},{28,20},{1,9},{5... | collective-permute-start | bytes 786440 | tf_op jit(solution)/shard_map/ppermute | solution.py:287
  28.4 8.3 %collective-permute-start.2 = (bf16[16,32,256]{2,1,0:T(8,128)(2,1)S(1)}, bf16[16,32,256]{2,1,0:T(8,128)(2,1)S(1)}, u32[]{:S(2)}, u32[]{:S(2)}) collective-permute-start(bf16[16,32,256]{2,1,0:T(8,128)(2,1)S(1)} %get-tuple-element.17), channel_id=1, source_target_pairs={{0,3},{1,2},{2,1},{3,0},{4,7},{5,6},{6,5},{7,4},{8,11},{9,10},{10,... | collective-permute-start | bytes 786440 | tf_op jit(solution)/shard_map/ppermute | solution.py:287
  31.9 6.4 %collective-permute-start.12 = (bf16[16,32,256]{2,1,0:T(8,128)(2,1)S(1)}, bf16[16,32,256]{2,1,0:T(8,128)(2,1)S(1)}, u32[]{:S(2)}, u32[]{:S(2)}) collective-permute-start(bf16[16,32,256]{2,1,0:T(8,128)(2,1)S(1)} %collective-permute-done.1.refs_2_.refs_0_), channel_id=1, source_target_pairs={{0,8},{4,12},{8,0},{12,4},{16,24},{20,28},{24,16},{28,20},{1,9},{5... | collective-permute-start | bytes 786440 | tf_op jit(solution)/shard_map/ppermute | solution.py:287
  33.8 9.1 %collective-permute-start.13 = (bf16[16,32,256]{2,1,0:T(8,128)(2,1)S(1)}, bf16[16,32,256]{2,1,0:T(8,128)(2,1)S(1)}, u32[]{:S(2)}, u32[]{:S(2)}) collective-permute-start(bf16[16,32,256]{2,1,0:T(8,128)(2,1)S(1)} %collective-permute-done.1.refs_2_.refs_0_), channel_id=1, source_target_pairs={{0,16},{4,20},{8,24},{12,28},{16,0},{20,4},{24,8},{28,12},{1,17},{... | collective-permute-start | bytes 786440 | tf_op jit(solution)/shard_map/ppermute | solution.py:287
  38.4 9.7 %collective-permute-start.16 = (bf16[16,32,256]{2,1,0:T(8,128)(2,1)S(1)}, bf16[16,32,256]{2,1,0:T(8,128)(2,1)S(1)}, u32[]{:S(2)}, u32[]{:S(2)}) collective-permute-start(bf16[16,32,256]{2,1,0:T(8,128)(2,1)S(1)} %collective-permute-done.2.refs_3_.refs_4_), channel_id=1, source_target_pairs={{0,16},{4,20},{8,24},{12,28},{16,0},{20,4},{24,8},{28,12},{1,17},{... | collective-permute-start | bytes 786440 | tf_op jit(solution)/shard_map/ppermute | solution.py:287
  39.9 10.1 %collective-permute-start.15 = (bf16[16,32,256]{2,1,0:T(8,128)(2,1)S(1)}, bf16[16,32,256]{2,1,0:T(8,128)(2,1)S(1)}, u32[]{:S(2)}, u32[]{:S(2)}) collective-permute-start(bf16[16,32,256]{2,1,0:T(8,128)(2,1)S(1)} %collective-permute-done.2.refs_3_.refs_4_), channel_id=1, source_target_pairs={{0,8},{4,12},{8,0},{12,4},{16,24},{20,28},{24,16},{28,20},{1,9},{5... | collective-permute-start | bytes 786440 | tf_op jit(solution)/shard_map/ppermute | solution.py:287
  41.6 9.1 %collective-permute-start.9 = (bf16[8,32,256]{2,1,0:T(8,128)(2,1)S(1)}, bf16[8,32,256]{2,1,0:T(8,128)(2,1)S(1)}, u32[]{:S(2)}, u32[]{:S(2)}) collective-permute-start(bf16[8,32,256]{2,1,0:T(8,128)(2,1)S(1)} %slice.24), channel_id=1, source_target_pairs={{0,8},{4,12},{8,0},{12,4},{16,24},{20,28},{24,16},{28,20},{1,9},{5... | collective-permute-start | bytes 393224 | tf_op jit(solution)/shard_map/ppermute | solution.py:287
  42.4 9.6 %collective-permute-start.10 = (bf16[8,32,256]{2,1,0:T(8,128)(2,1)S(1)}, bf16[8,32,256]{2,1,0:T(8,128)(2,1)S(1)}, u32[]{:S(2)}, u32[]{:S(2)}) collective-permute-start(bf16[8,32,256]{2,1,0:T(8,128)(2,1)S(1)} %slice.25), channel_id=1, source_target_pairs={{0,16},{4,20},{8,24},{12,28},{16,0},{20,4},{24,8},{28,12},{1,17},{... | collective-permute-start | bytes 393224 | tf_op jit(solution)/shard_map/ppermute | solution.py:287
  43.0 9.7 %collective-permute-start.14 = (bf16[8,32,256]{2,1,0:T(8,128)(2,1)S(1)}, bf16[8,32,256]{2,1,0:T(8,128)(2,1)S(1)}, u32[]{:S(2)}, u32[]{:S(2)}) collective-permute-start(bf16[8,32,256]{2,1,0:T(8,128)(2,1)S(1)} %slice.26), channel_id=1, source_target_pairs={{0,8},{4,12},{8,0},{12,4},{16,24},{20,28},{24,16},{28,20},{1,9},{5... | collective-permute-start | bytes 393224 | tf_op jit(solution)/shard_map/ppermute | solution.py:287
  48.1 7.7 %collective-permute-start.19 = (bf16[8,32,256]{2,1,0:T(8,128)(2,1)S(1)}, bf16[8,32,256]{2,1,0:T(8,128)(2,1)S(1)}, u32[]{:S(2)}, u32[]{:S(2)}) collective-permute-start(bf16[8,32,256]{2,1,0:T(8,128)(2,1)S(1)} %slice.28), channel_id=1, source_target_pairs={{0,16},{4,20},{8,24},{12,28},{16,0},{20,4},{24,8},{28,12},{1,17},{... | collective-permute-start | bytes 393224 | tf_op jit(solution)/shard_map/ppermute | solution.py:287
  50.0 5.0 %collective-permute-start.17 = (bf16[8,32,256]{2,1,0:T(8,128)(2,1)S(1)}, bf16[8,32,256]{2,1,0:T(8,128)(2,1)S(1)}, u32[]{:S(2)}, u32[]{:S(2)}) collective-permute-start(bf16[8,32,256]{2,1,0:T(8,128)(2,1)S(1)} %slice.27), channel_id=1, source_target_pairs={{0,8},{4,12},{8,0},{12,4},{16,24},{20,28},{24,16},{28,20},{1,9},{5... | collective-permute-start | bytes 393224 | tf_op jit(solution)/shard_map/ppermute | solution.py:287
  50.8 5.0 %collective-permute-start.20 = (bf16[8,32,256]{2,1,0:T(8,128)(2,1)S(1)}, bf16[8,32,256]{2,1,0:T(8,128)(2,1)S(1)}, u32[]{:S(2)}, u32[]{:S(2)}) collective-permute-start(bf16[8,32,256]{2,1,0:T(8,128)(2,1)S(1)} %slice.29), channel_id=1, source_target_pairs={{0,16},{4,20},{8,24},{12,28},{16,0},{20,4},{24,8},{28,12},{1,17},{... | collective-permute-start | bytes 393224 | tf_op jit(solution)/shard_map/ppermute | solution.py:287
  52.0 6.0 %collective-permute-start.6 = (bf16[2,16,32,256]{3,2,1,0:T(8,128)(2,1)S(1)}, bf16[2,16,32,256]{3,2,1,0:T(8,128)(2,1)S(1)}, u32[]{:S(2)}, u32[]{:S(2)}) collective-permute-start(bf16[2,16,32,256]{3,2,1,0:T(8,128)(2,1)S(1)} %pick.4), channel_id=1, source_target_pairs={{0,4},{4,0},{8,12},{12,8},{16,20},{20,16},{24,28},{28,24},{1,5},{5... | collective-permute-start | bytes 1572872 | tf_op jit(solution)/shard_map/ppermute | solution.py:287
  52.7 5.3 %collective-permute-start.11 = (bf16[2,16,32,256]{3,2,1,0:T(8,128)(2,1)S(1)}, bf16[2,16,32,256]{3,2,1,0:T(8,128)(2,1)S(1)}, u32[]{:S(2)}, u32[]{:S(2)}) collective-permute-start(bf16[2,16,32,256]{3,2,1,0:T(8,128)(2,1)S(1)} %pick.5), channel_id=1, source_target_pairs={{0,4},{4,0},{8,12},{12,8},{16,20},{20,16},{24,28},{28,24},{1,5},{5... | collective-permute-start | bytes 1572872 | tf_op jit(solution)/shard_map/ppermute | solution.py:287
  55.7 2.3 %collective-permute-start.18 = (bf16[2,16,32,256]{3,2,1,0:T(8,128)(2,1)S(1)}, bf16[2,16,32,256]{3,2,1,0:T(8,128)(2,1)S(1)}, u32[]{:S(2)}, u32[]{:S(2)}) collective-permute-start(bf16[2,16,32,256]{3,2,1,0:T(8,128)(2,1)S(1)} %pick.6), channel_id=1, source_target_pairs={{0,4},{4,0},{8,12},{12,8},{16,20},{20,16},{24,28},{28,24},{1,5},{5... | collective-permute-start | bytes 1572872 | tf_op jit(solution)/shard_map/ppermute | solution.py:287
  56.4 2.1 %collective-permute-start.21 = (bf16[2,16,32,256]{3,2,1,0:T(8,128)(2,1)S(1)}, bf16[2,16,32,256]{3,2,1,0:T(8,128)(2,1)S(1)}, u32[]{:S(2)}, u32[]{:S(2)}) collective-permute-start(bf16[2,16,32,256]{3,2,1,0:T(8,128)(2,1)S(1)} %pick.7), channel_id=1, source_target_pairs={{0,4},{4,0},{8,12},{12,8},{16,20},{20,16},{24,28},{28,24},{1,5},{5... | collective-permute-start | bytes 1572872 | tf_op jit(solution)/shard_map/ppermute | solution.py:287

commit v7 on v6

--- a/solution.py
+++ b/solution.py
@@ -99,7 +99,7 @@
 def local_spectra(traces, win_count, pieces):
     channels, windows, samples = traces.shape
     columns = 2 * BINS
-    chan_rows = 32
+    chan_rows = 64
     steps, halves = LANES // chan_rows, windows // WIN_ROWS
     flops = 2 * channels * windows * samples * columns
     return pl.pallas_call(

time: 63.1 us -> 63 us (level)
  transfers between devices with their start and end apart: 22 -> 22, of which waited for: 8 -> 9; matrix products, arithmetic and copies ran while one was open for 1% -> 1% of each run, Pallas kernels for 5% -> 5%
where the time goes in v7:
time: 63 us; the launch traced here: 62.8 us
  starting transfers between devices  28.1 us (45%)
  waiting for transfers between devices  17.7 us (28%)
  Pallas kernels  16 us (25%)
  other arithmetic  0.69 us (1%)
    ppermute x22, starting transfers between devices, swap(): return lax.ppermute(value, axis, [(i, i ^ distance) for i in range(count)])  28.1 us
    ppermute x22, waiting for transfers between devices, swap(): return lax.ppermute(value, axis, [(i, i ^ distance) for i in range(count)])  17.7 us
    pallas_call x1, Pallas kernels, local_spectra(): pl.pallas_call(functools.partial(spectra_kernel, chan_rows, win_count, pi...  8.16 us
    pallas_call x1, Pallas kernels, correlate(): pl.pallas_call(functools.partial(correlate_kernel, scale, layout), in_spe...  4.45 us
    pallas_call x4, Pallas kernels, pick(): pl.pallas_call(functools.partial(pick_kernel, places), in_specs=[pl.Block...  2.47 us
  transfers between devices with their start and end apart: 22, of which 9 were waited for; matrix products, arithmetic and copies ran while one was open for 1% of the time, Pallas kernels for 5%

profile of v7, /device:TPU:0, one launch (start us, length us, event | category | flops | bytes accessed | tf_op | source)
XLA Modules:
  0.0 62.8 jit_solution(4867928957069149801)
XLA Ops:
  0.0 8.2 %spectra.1 = (bf16[16,32,256]{2,1,0:T(8,128)(2,1)S(1)}, bf16[16,32,256]{2,1,0:T(8,128)(2,1)S(1)}, bf16[16,32,256]{2,1,0:T(8,128)(2,1)S(1)}, bf16[16,32,256]{2,1,0:T(8,128)(2,1)S(1)}) custom-call(s32[1]{0:T(128)} %bitcast.win_ref, bf16[256,32,1024]{2,1,0:T(8,128)(2,1)} %traces_ref.1), custom_call_target="tpu_custom_call" | custom-call | flops 1073741824 | bytes 16777216 | tf_op jit(solution)/shard_map/spectra/pallas_call | solution.py:105
  8.2 3.1 %collective-permute-start = (bf16[16,32,256]{2,1,0:T(8,128)(2,1)S(1)}, bf16[16,32,256]{2,1,0:T(8,128)(2,1)S(1)}, u32[]{:S(2)}, u32[]{:S(2)}) collective-permute-start(bf16[16,32,256]{2,1,0:T(8,128)(2,1)S(1)} %get-tuple-element.14), channel_id=1, source_target_pairs={{0,1},{1,0},{2,3},{3,2},{4,5},{5,4},{6,7},{7,6},{8,9},{9,8},{10,11... | collective-permute-start | bytes 786440 | tf_op jit(solution)/shard_map/ppermute | solution.py:287
  11.3 1.5 %collective-permute-start.4 = (bf16[16,32,256]{2,1,0:T(8,128)(2,1)S(1)}, bf16[16,32,256]{2,1,0:T(8,128)(2,1)S(1)}, u32[]{:S(2)}, u32[]{:S(2)}) collective-permute-start(bf16[16,32,256]{2,1,0:T(8,128)(2,1)S(1)} %get-tuple-element.13.refs_0_), channel_id=1, source_target_pairs={{0,16},{4,20},{8,24},{12,28},{16,0},{20,4},{24,8},{28,12},{1,17},{... | collective-permute-start | bytes 786440 | tf_op jit(solution)/shard_map/ppermute | solution.py:287
  12.8 1.5 %collective-permute-start.3 = (bf16[16,32,256]{2,1,0:T(8,128)(2,1)S(1)}, bf16[16,32,256]{2,1,0:T(8,128)(2,1)S(1)}, u32[]{:S(2)}, u32[]{:S(2)}) collective-permute-start(bf16[16,32,256]{2,1,0:T(8,128)(2,1)S(1)} %get-tuple-element.13.refs_0_), channel_id=1, source_target_pairs={{0,8},{4,12},{8,0},{12,4},{16,24},{20,28},{24,16},{28,20},{1,9},{5... | collective-permute-start | bytes 786440 | tf_op jit(solution)/shard_map/ppermute | solution.py:287
  14.8 2.6 %collective-permute-start.1 = (bf16[16,32,256]{2,1,0:T(8,128)(2,1)S(1)}, bf16[16,32,256]{2,1,0:T(8,128)(2,1)S(1)}, u32[]{:S(2)}, u32[]{:S(2)}) collective-permute-start(bf16[16,32,256]{2,1,0:T(8,128)(2,1)S(1)} %get-tuple-element.15), channel_id=1, source_target_pairs={{0,2},{1,3},{2,0},{3,1},{4,6},{5,7},{6,4},{7,5},{8,10},{9,11},{10,... | collective-permute-start | bytes 786440 | tf_op jit(solution)/shard_map/ppermute | solution.py:287
  17.3 2.4 %collective-permute-done.refs_1_.refs_0_ = bf16[16,32,256]{2,1,0:T(8,128)(2,1)S(1)} collective-permute-done((bf16[16,32,256]{2,1,0:T(8,128)(2,1)S(1)}, bf16[16,32,256]{2,1,0:T(8,128)(2,1)S(1)}, u32[]{:S(2)}, u32[]{:S(2)}) %collective-permute-start) | collective-permute-done | bytes 262176 | tf_op jit(solution)/shard_map/ppermute | solution.py:287
  19.7 2.3 %collective-permute-done.3.refs_1_.refs_4_ = bf16[16,32,256]{2,1,0:T(8,128)(2,1)S(1)} collective-permute-done((bf16[16,32,256]{2,1,0:T(8,128)(2,1)S(1)}, bf16[16,32,256]{2,1,0:T(8,128)(2,1)S(1)}, u32[]{:S(2)}, u32[]{:S(2)}) %collective-permute-start.3) | collective-permute-done | bytes 262176 | tf_op jit(solution)/shard_map/ppermute | solution.py:287
  22.5 1.5 %collective-permute-start.7 = (bf16[16,32,256]{2,1,0:T(8,128)(2,1)S(1)}, bf16[16,32,256]{2,1,0:T(8,128)(2,1)S(1)}, u32[]{:S(2)}, u32[]{:S(2)}) collective-permute-start(bf16[16,32,256]{2,1,0:T(8,128)(2,1)S(1)} %collective-permute-done.refs_1_.refs_0_), channel_id=1, source_target_pairs={{0,8},{4,12},{8,0},{12,4},{16,24},{20,28},{24,16},{28,20},{1,9},{5... | collective-permute-start | bytes 786440 | tf_op jit(solution)/shard_map/ppermute | solution.py:287
  24.0 4.2 %collective-permute-done.1.refs_2_.refs_0_ = bf16[16,32,256]{2,1,0:T(8,128)(2,1)S(1)} collective-permute-done((bf16[16,32,256]{2,1,0:T(8,128)(2,1)S(1)}, bf16[16,32,256]{2,1,0:T(8,128)(2,1)S(1)}, u32[]{:S(2)}, u32[]{:S(2)}) %collective-permute-start.1) | collective-permute-done | bytes 262176 | tf_op jit(solution)/shard_map/ppermute | solution.py:287
  28.2 3.6 %collective-permute-start.2 = (bf16[16,32,256]{2,1,0:T(8,128)(2,1)S(1)}, bf16[16,32,256]{2,1,0:T(8,128)(2,1)S(1)}, u32[]{:S(2)}, u32[]{:S(2)}) collective-permute-start(bf16[16,32,256]{2,1,0:T(8,128)(2,1)S(1)} %get-tuple-element.17), channel_id=1, source_target_pairs={{0,3},{1,2},{2,1},{3,0},{4,7},{5,6},{6,5},{7,4},{8,11},{9,10},{10,... | collective-permute-start | bytes 786440 | tf_op jit(solution)/shard_map/ppermute | solution.py:287
  31.8 1.6 %collective-permute-start.12 = (bf16[16,32,256]{2,1,0:T(8,128)(2,1)S(1)}, bf16[16,32,256]{2,1,0:T(8,128)(2,1)S(1)}, u32[]{:S(2)}, u32[]{:S(2)}) collective-permute-start(bf16[16,32,256]{2,1,0:T(8,128)(2,1)S(1)} %collective-permute-done.1.refs_2_.refs_0_), channel_id=1, source_target_pairs={{0,8},{4,12},{8,0},{12,4},{16,24},{20,28},{24,16},{28,20},{1,9},{5... | collective-permute-start | bytes 786440 | tf_op jit(solution)/shard_map/ppermute | solution.py:287
  33.7 1.6 %collective-permute-start.13 = (bf16[16,32,256]{2,1,0:T(8,128)(2,1)S(1)}, bf16[16,32,256]{2,1,0:T(8,128)(2,1)S(1)}, u32[]{:S(2)}, u32[]{:S(2)}) collective-permute-start(bf16[16,32,256]{2,1,0:T(8,128)(2,1)S(1)} %collective-permute-done.1.refs_2_.refs_0_), channel_id=1, source_target_pairs={{0,16},{4,20},{8,24},{12,28},{16,0},{20,4},{24,8},{28,12},{1,17},{... | collective-permute-start | bytes 786440 | tf_op jit(solution)/shard_map/ppermute | solution.py:287
  35.3 1.2 %collective-permute-done.2.refs_3_.refs_4_ = bf16[16,32,256]{2,1,0:T(8,128)(2,1)S(1)} collective-permute-done((bf16[16,32,256]{2,1,0:T(8,128)(2,1)S(1)}, bf16[16,32,256]{2,1,0:T(8,128)(2,1)S(1)}, u32[]{:S(2)}, u32[]{:S(2)}) %collective-permute-start.2) | collective-permute-done | bytes 262176 | tf_op jit(solution)/shard_map/ppermute | solution.py:287
  36.5 1.8 %collective-permute-done.12.refs_1_.refs_11_ = bf16[16,32,256]{2,1,0:T(8,128)(2,1)S(1)} collective-permute-done((bf16[16,32,256]{2,1,0:T(8,128)(2,1)S(1)}, bf16[16,32,256]{2,1,0:T(8,128)(2,1)S(1)}, u32[]{:S(2)}, u32[]{:S(2)}) %collective-permute-start.12) | collective-permute-done | bytes 262176 | tf_op jit(solution)/shard_map/ppermute | solution.py:287
  38.3 1.5 %collective-permute-start.16 = (bf16[16,32,256]{2,1,0:T(8,128)(2,1)S(1)}, bf16[16,32,256]{2,1,0:T(8,128)(2,1)S(1)}, u32[]{:S(2)}, u32[]{:S(2)}) collective-permute-start(bf16[16,32,256]{2,1,0:T(8,128)(2,1)S(1)} %collective-permute-done.2.refs_3_.refs_4_), channel_id=1, source_target_pairs={{0,16},{4,20},{8,24},{12,28},{16,0},{20,4},{24,8},{28,12},{1,17},{... | collective-permute-start | bytes 786440 | tf_op jit(solution)/shard_map/ppermute | solution.py:287
  39.8 1.5 %collective-permute-start.15 = (bf16[16,32,256]{2,1,0:T(8,128)(2,1)S(1)}, bf16[16,32,256]{2,1,0:T(8,128)(2,1)S(1)}, u32[]{:S(2)}, u32[]{:S(2)}) collective-permute-start(bf16[16,32,256]{2,1,0:T(8,128)(2,1)S(1)} %collective-permute-done.2.refs_3_.refs_4_), channel_id=1, source_target_pairs={{0,8},{4,12},{8,0},{12,4},{16,24},{20,28},{24,16},{28,20},{1,9},{5... | collective-permute-start | bytes 786440 | tf_op jit(solution)/shard_map/ppermute | solution.py:287
  41.5 0.6 collective-permute-start.9
  42.3 0.6 collective-permute-start.10
  42.9 1.6 %collective-permute-start.14 = (bf16[8,32,256]{2,1,0:T(8,128)(2,1)S(1)}, bf16[8,32,256]{2,1,0:T(8,128)(2,1)S(1)}, u32[]{:S(2)}, u32[]{:S(2)}) collective-permute-start(bf16[8,32,256]{2,1,0:T(8,128)(2,1)S(1)} %slice.26), channel_id=1, source_target_pairs={{0,8},{4,12},{8,0},{12,4},{16,24},{20,28},{24,16},{28,20},{1,9},{5... | collective-permute-start | bytes 393224 | tf_op jit(solution)/shard_map/ppermute | solution.py:287
  44.4 3.5 %collective-permute-done.16.refs_6_.refs_16_ = bf16[16,32,256]{2,1,0:T(8,128)(2,1)S(1)} collective-permute-done((bf16[16,32,256]{2,1,0:T(8,128)(2,1)S(1)}, bf16[16,32,256]{2,1,0:T(8,128)(2,1)S(1)}, u32[]{:S(2)}, u32[]{:S(2)}) %collective-permute-start.16) | collective-permute-done | bytes 262176 | tf_op jit(solution)/shard_map/ppermute | solution.py:287
  47.9 1.9 %collective-permute-start.19 = (bf16[8,32,256]{2,1,0:T(8,128)(2,1)S(1)}, bf16[8,32,256]{2,1,0:T(8,128)(2,1)S(1)}, u32[]{:S(2)}, u32[]{:S(2)}) collective-permute-start(bf16[8,32,256]{2,1,0:T(8,128)(2,1)S(1)} %slice.28), channel_id=1, source_target_pairs={{0,16},{4,20},{8,24},{12,28},{16,0},{20,4},{24,8},{28,12},{1,17},{... | collective-permute-start | bytes 393224 | tf_op jit(solution)/shard_map/ppermute | solution.py:287
  49.9 0.8 %collective-permute-start.17 = (bf16[8,32,256]{2,1,0:T(8,128)(2,1)S(1)}, bf16[8,32,256]{2,1,0:T(8,128)(2,1)S(1)}, u32[]{:S(2)}, u32[]{:S(2)}) collective-permute-start(bf16[8,32,256]{2,1,0:T(8,128)(2,1)S(1)} %slice.27), channel_id=1, source_target_pairs={{0,8},{4,12},{8,0},{12,4},{16,24},{20,28},{24,16},{28,20},{1,9},{5... | collective-permute-start | bytes 393224 | tf_op jit(solution)/shard_map/ppermute | solution.py:287
  50.6 0.6 collective-permute-start.20
  51.2 0.6 pick.4
  51.9 0.6 pick.5
  52.6 0.6 collective-permute-start.11
  53.1 1.8 %collective-permute-done.17.refs_7_.refs_17_ = bf16[8,32,256]{2,1,0:T(8,128)(2,1)S(1)} collective-permute-done((bf16[8,32,256]{2,1,0:T(8,128)(2,1)S(1)}, bf16[8,32,256]{2,1,0:T(8,128)(2,1)S(1)}, u32[]{:S(2)}, u32[]{:S(2)}) %collective-permute-start.17) | collective-permute-done | bytes 131104 | tf_op jit(solution)/shard_map/ppermute | solution.py:287
  54.9 0.6 pick.6
  55.7 0.6 pick.7
  56.8 1.0 %left_side.1.left_ref = bf16[8,512,256]{2,1,0:T(8,128)(2,1)S(1)} custom-call(bf16[16,32,256]{2,1,0:T(8,128)(2,1)S(1)} %get-tuple-element.13.refs_0_, bf16[16,32,256]{2,1,0:T(8,128)(2,1)S(1)} %collective-permute-done.refs_1_.refs_0_, bf16[16,32,256]{2,1,0:T(8,128)(2,1)S(1)} %collective-permute-done.1.refs_2_.refs_0_, ...), custom_call_target="tpu_custom_call" | custom-call | tf_op jit(solution)/shard_map/left_side/pallas_call | solution.py:190
  57.8 0.5 collective-permute-done.21.refs_3_
  58.3 4.4 %cross_spectra.1 = f32[2,8,2,256,256]{4,3,2,1,0:T(8,128)} custom-call(s32[2]{0:T(128)S(1)} %broadcast_xor_fusion.1.far_ref, bf16[8,512,256]{2,1,0:T(8,128)(2,1)S(1)} %left_side.1.left_ref, bf16[2,16,32,256]{3,2,1,0:T(8,128)(2,1)S(1)} %collective-permute-done.6.refs_0_, bf16[2,16,32,256]{3,2,1,0:T(8,128)(2,1)S(1)} %collective-permute-done.11.refs_1_, ...), custom_call_target="tpu_custom_call" | custom-call | flops 1073741824 | bytes 8388608 | tf_op jit(solution)/shard_map/cross_spectra/pallas_call | solution.py:261
  (37 shorter events, 2.5 us)
Async XLA Ops:
  0.0 33.4 %copy-start.1 = (s32[8]{0:T(128)S(1)}, s32[8]{0:T(128)}, u32[]{:S(2)}) copy-start(s32[8]{0:T(128)} %param.5) | copy-start | bytes 100
  0.0 33.6 %copy-start = (s32[2,8]{1,0:T(2,128)S(1)}, s32[2,8]{1,0:T(2,128)}, u32[]{:S(2)}) copy-start(s32[2,8]{1,0:T(2,128)} %param.4) | copy-start | bytes 196
  8.2 11.6 %collective-permute-start = (bf16[16,32,256]{2,1,0:T(8,128)(2,1)S(1)}, bf16[16,32,256]{2,1,0:T(8,128)(2,1)S(1)}, u32[]{:S(2)}, u32[]{:S(2)}) collective-permute-start(bf16[16,32,256]{2,1,0:T(8,128)(2,1)S(1)} %get-tuple-element.14), channel_id=1, source_target_pairs={{0,1},{1,0},{2,3},{3,2},{4,5},{5,4},{6,7},{7,6},{8,9},{9,8},{10,11... | collective-permute-start | bytes 786440 | tf_op jit(solution)/shard_map/ppermute | solution.py:287
  11.3 8.5 %collective-permute-start.4 = (bf16[16,32,256]{2,1,0:T(8,128)(2,1)S(1)}, bf16[16,32,256]{2,1,0:T(8,128)(2,1)S(1)}, u32[]{:S(2)}, u32[]{:S(2)}) collective-permute-start(bf16[16,32,256]{2,1,0:T(8,128)(2,1)S(1)} %get-tuple-element.13.refs_0_), channel_id=1, source_target_pairs={{0,16},{4,20},{8,24},{12,28},{16,0},{20,4},{24,8},{28,12},{1,17},{... | collective-permute-start | bytes 786440 | tf_op jit(solution)/shard_map/ppermute | solution.py:287
  12.8 9.2 %collective-permute-start.3 = (bf16[16,32,256]{2,1,0:T(8,128)(2,1)S(1)}, bf16[16,32,256]{2,1,0:T(8,128)(2,1)S(1)}, u32[]{:S(2)}, u32[]{:S(2)}) collective-permute-start(bf16[16,32,256]{2,1,0:T(8,128)(2,1)S(1)} %get-tuple-element.13.refs_0_), channel_id=1, source_target_pairs={{0,8},{4,12},{8,0},{12,4},{16,24},{20,28},{24,16},{28,20},{1,9},{5... | collective-permute-start | bytes 786440 | tf_op jit(solution)/shard_map/ppermute | solution.py:287
  14.3 17.6 %collective-permute-start.5 = (bf16[16,32,256]{2,1,0:T(8,128)(2,1)S(1)}, bf16[16,32,256]{2,1,0:T(8,128)(2,1)S(1)}, u32[]{:S(2)}, u32[]{:S(2)}) collective-permute-start(bf16[16,32,256]{2,1,0:T(8,128)(2,1)S(1)} %get-tuple-element.13.refs_0_), channel_id=1, source_target_pairs={{0,24},{4,28},{8,16},{12,20},{16,8},{20,12},{24,0},{28,4},{1,25},{... | collective-permute-start | bytes 786440 | tf_op jit(solution)/shard_map/ppermute | solution.py:287
  14.8 13.5 %collective-permute-start.1 = (bf16[16,32,256]{2,1,0:T(8,128)(2,1)S(1)}, bf16[16,32,256]{2,1,0:T(8,128)(2,1)S(1)}, u32[]{:S(2)}, u32[]{:S(2)}) collective-permute-start(bf16[16,32,256]{2,1,0:T(8,128)(2,1)S(1)} %get-tuple-element.15), channel_id=1, source_target_pairs={{0,2},{1,3},{2,0},{3,1},{4,6},{5,7},{6,4},{7,5},{8,10},{9,11},{10,... | collective-permute-start | bytes 786440 | tf_op jit(solution)/shard_map/ppermute | solution.py:287
  22.0 9.8 %collective-permute-start.8 = (bf16[16,32,256]{2,1,0:T(8,128)(2,1)S(1)}, bf16[16,32,256]{2,1,0:T(8,128)(2,1)S(1)}, u32[]{:S(2)}, u32[]{:S(2)}) collective-permute-start(bf16[16,32,256]{2,1,0:T(8,128)(2,1)S(1)} %collective-permute-done.refs_1_.refs_0_), channel_id=1, source_target_pairs={{0,16},{4,20},{8,24},{12,28},{16,0},{20,4},{24,8},{28,12},{1,17},{... | collective-permute-start | bytes 786440 | tf_op jit(solution)/shard_map/ppermute | solution.py:287
  22.5 9.3 %collective-permute-start.7 = (bf16[16,32,256]{2,1,0:T(8,128)(2,1)S(1)}, bf16[16,32,256]{2,1,0:T(8,128)(2,1)S(1)}, u32[]{:S(2)}, u32[]{:S(2)}) collective-permute-start(bf16[16,32,256]{2,1,0:T(8,128)(2,1)S(1)} %collective-permute-done.refs_1_.refs_0_), channel_id=1, source_target_pairs={{0,8},{4,12},{8,0},{12,4},{16,24},{20,28},{24,16},{28,20},{1,9},{5... | collective-permute-start | bytes 786440 | tf_op jit(solution)/shard_map/ppermute | solution.py:287
  28.2 8.3 %collective-permute-start.2 = (bf16[16,32,256]{2,1,0:T(8,128)(2,1)S(1)}, bf16[16,32,256]{2,1,0:T(8,128)(2,1)S(1)}, u32[]{:S(2)}, u32[]{:S(2)}) collective-permute-start(bf16[16,32,256]{2,1,0:T(8,128)(2,1)S(1)} %get-tuple-element.17), channel_id=1, source_target_pairs={{0,3},{1,2},{2,1},{3,0},{4,7},{5,6},{6,5},{7,4},{8,11},{9,10},{10,... | collective-permute-start | bytes 786440 | tf_op jit(solution)/shard_map/ppermute | solution.py:287
  31.8 6.4 %collective-permute-start.12 = (bf16[16,32,256]{2,1,0:T(8,128)(2,1)S(1)}, bf16[16,32,256]{2,1,0:T(8,128)(2,1)S(1)}, u32[]{:S(2)}, u32[]{:S(2)}) collective-permute-start(bf16[16,32,256]{2,1,0:T(8,128)(2,1)S(1)} %collective-permute-done.1.refs_2_.refs_0_), channel_id=1, source_target_pairs={{0,8},{4,12},{8,0},{12,4},{16,24},{20,28},{24,16},{28,20},{1,9},{5... | collective-permute-start | bytes 786440 | tf_op jit(solution)/shard_map/ppermute | solution.py:287
  33.7 9.1 %collective-permute-start.13 = (bf16[16,32,256]{2,1,0:T(8,128)(2,1)S(1)}, bf16[16,32,256]{2,1,0:T(8,128)(2,1)S(1)}, u32[]{:S(2)}, u32[]{:S(2)}) collective-permute-start(bf16[16,32,256]{2,1,0:T(8,128)(2,1)S(1)} %collective-permute-done.1.refs_2_.refs_0_), channel_id=1, source_target_pairs={{0,16},{4,20},{8,24},{12,28},{16,0},{20,4},{24,8},{28,12},{1,17},{... | collective-permute-start | bytes 786440 | tf_op jit(solution)/shard_map/ppermute | solution.py:287
  38.3 9.6 %collective-permute-start.16 = (bf16[16,32,256]{2,1,0:T(8,128)(2,1)S(1)}, bf16[16,32,256]{2,1,0:T(8,128)(2,1)S(1)}, u32[]{:S(2)}, u32[]{:S(2)}) collective-permute-start(bf16[16,32,256]{2,1,0:T(8,128)(2,1)S(1)} %collective-permute-done.2.refs_3_.refs_4_), channel_id=1, source_target_pairs={{0,16},{4,20},{8,24},{12,28},{16,0},{20,4},{24,8},{28,12},{1,17},{... | collective-permute-start | bytes 786440 | tf_op jit(solution)/shard_map/ppermute | solution.py:287
  39.8 10.1 %collective-permute-start.15 = (bf16[16,32,256]{2,1,0:T(8,128)(2,1)S(1)}, bf16[16,32,256]{2,1,0:T(8,128)(2,1)S(1)}, u32[]{:S(2)}, u32[]{:S(2)}) collective-permute-start(bf16[16,32,256]{2,1,0:T(8,128)(2,1)S(1)} %collective-permute-done.2.refs_3_.refs_4_), channel_id=1, source_target_pairs={{0,8},{4,12},{8,0},{12,4},{16,24},{20,28},{24,16},{28,20},{1,9},{5... | collective-permute-start | bytes 786440 | tf_op jit(solution)/shard_map/ppermute | solution.py:287
  41.5 9.1 %collective-permute-start.9 = (bf16[8,32,256]{2,1,0:T(8,128)(2,1)S(1)}, bf16[8,32,256]{2,1,0:T(8,128)(2,1)S(1)}, u32[]{:S(2)}, u32[]{:S(2)}) collective-permute-start(bf16[8,32,256]{2,1,0:T(8,128)(2,1)S(1)} %slice.24), channel_id=1, source_target_pairs={{0,8},{4,12},{8,0},{12,4},{16,24},{20,28},{24,16},{28,20},{1,9},{5... | collective-permute-start | bytes 393224 | tf_op jit(solution)/shard_map/ppermute | solution.py:287
  42.3 9.6 %collective-permute-start.10 = (bf16[8,32,256]{2,1,0:T(8,128)(2,1)S(1)}, bf16[8,32,256]{2,1,0:T(8,128)(2,1)S(1)}, u32[]{:S(2)}, u32[]{:S(2)}) collective-permute-start(bf16[8,32,256]{2,1,0:T(8,128)(2,1)S(1)} %slice.25), channel_id=1, source_target_pairs={{0,16},{4,20},{8,24},{12,28},{16,0},{20,4},{24,8},{28,12},{1,17},{... | collective-permute-start | bytes 393224 | tf_op jit(solution)/shard_map/ppermute | solution.py:287
  42.9 9.7 %collective-permute-start.14 = (bf16[8,32,256]{2,1,0:T(8,128)(2,1)S(1)}, bf16[8,32,256]{2,1,0:T(8,128)(2,1)S(1)}, u32[]{:S(2)}, u32[]{:S(2)}) collective-permute-start(bf16[8,32,256]{2,1,0:T(8,128)(2,1)S(1)} %slice.26), channel_id=1, source_target_pairs={{0,8},{4,12},{8,0},{12,4},{16,24},{20,28},{24,16},{28,20},{1,9},{5... | collective-permute-start | bytes 393224 | tf_op jit(solution)/shard_map/ppermute | solution.py:287
  47.9 7.7 %collective-permute-start.19 = (bf16[8,32,256]{2,1,0:T(8,128)(2,1)S(1)}, bf16[8,32,256]{2,1,0:T(8,128)(2,1)S(1)}, u32[]{:S(2)}, u32[]{:S(2)}) collective-permute-start(bf16[8,32,256]{2,1,0:T(8,128)(2,1)S(1)} %slice.28), channel_id=1, source_target_pairs={{0,16},{4,20},{8,24},{12,28},{16,0},{20,4},{24,8},{28,12},{1,17},{... | collective-permute-start | bytes 393224 | tf_op jit(solution)/shard_map/ppermute | solution.py:287
  49.9 5.0 %collective-permute-start.17 = (bf16[8,32,256]{2,1,0:T(8,128)(2,1)S(1)}, bf16[8,32,256]{2,1,0:T(8,128)(2,1)S(1)}, u32[]{:S(2)}, u32[]{:S(2)}) collective-permute-start(bf16[8,32,256]{2,1,0:T(8,128)(2,1)S(1)} %slice.27), channel_id=1, source_target_pairs={{0,8},{4,12},{8,0},{12,4},{16,24},{20,28},{24,16},{28,20},{1,9},{5... | collective-permute-start | bytes 393224 | tf_op jit(solution)/shard_map/ppermute | solution.py:287
  50.6 5.0 %collective-permute-start.20 = (bf16[8,32,256]{2,1,0:T(8,128)(2,1)S(1)}, bf16[8,32,256]{2,1,0:T(8,128)(2,1)S(1)}, u32[]{:S(2)}, u32[]{:S(2)}) collective-permute-start(bf16[8,32,256]{2,1,0:T(8,128)(2,1)S(1)} %slice.29), channel_id=1, source_target_pairs={{0,16},{4,20},{8,24},{12,28},{16,0},{20,4},{24,8},{28,12},{1,17},{... | collective-permute-start | bytes 393224 | tf_op jit(solution)/shard_map/ppermute | solution.py:287
  51.9 5.9 %collective-permute-start.6 = (bf16[2,16,32,256]{3,2,1,0:T(8,128)(2,1)S(1)}, bf16[2,16,32,256]{3,2,1,0:T(8,128)(2,1)S(1)}, u32[]{:S(2)}, u32[]{:S(2)}) collective-permute-start(bf16[2,16,32,256]{3,2,1,0:T(8,128)(2,1)S(1)} %pick.4), channel_id=1, source_target_pairs={{0,4},{4,0},{8,12},{12,8},{16,20},{20,16},{24,28},{28,24},{1,5},{5... | collective-permute-start | bytes 1572872 | tf_op jit(solution)/shard_map/ppermute | solution.py:287
  52.6 5.2 %collective-permute-start.11 = (bf16[2,16,32,256]{3,2,1,0:T(8,128)(2,1)S(1)}, bf16[2,16,32,256]{3,2,1,0:T(8,128)(2,1)S(1)}, u32[]{:S(2)}, u32[]{:S(2)}) collective-permute-start(bf16[2,16,32,256]{3,2,1,0:T(8,128)(2,1)S(1)} %pick.5), channel_id=1, source_target_pairs={{0,4},{4,0},{8,12},{12,8},{16,20},{20,16},{24,28},{28,24},{1,5},{5... | collective-permute-start | bytes 1572872 | tf_op jit(solution)/shard_map/ppermute | solution.py:287
  55.5 2.3 %collective-permute-start.18 = (bf16[2,16,32,256]{3,2,1,0:T(8,128)(2,1)S(1)}, bf16[2,16,32,256]{3,2,1,0:T(8,128)(2,1)S(1)}, u32[]{:S(2)}, u32[]{:S(2)}) collective-permute-start(bf16[2,16,32,256]{3,2,1,0:T(8,128)(2,1)S(1)} %pick.6), channel_id=1, source_target_pairs={{0,4},{4,0},{8,12},{12,8},{16,20},{20,16},{24,28},{28,24},{1,5},{5... | collective-permute-start | bytes 1572872 | tf_op jit(solution)/shard_map/ppermute | solution.py:287
  56.3 2.0 %collective-permute-start.21 = (bf16[2,16,32,256]{3,2,1,0:T(8,128)(2,1)S(1)}, bf16[2,16,32,256]{3,2,1,0:T(8,128)(2,1)S(1)}, u32[]{:S(2)}, u32[]{:S(2)}) collective-permute-start(bf16[2,16,32,256]{3,2,1,0:T(8,128)(2,1)S(1)} %pick.7), channel_id=1, source_target_pairs={{0,4},{4,0},{8,12},{12,8},{16,20},{20,16},{24,28},{28,24},{1,5},{5... | collective-permute-start | bytes 1572872 | tf_op jit(solution)/shard_map/ppermute | solution.py:287

commit v8 on v7

--- a/solution.py
+++ b/solution.py
@@ -226,7 +226,7 @@
     def send(bin_no, r):
         return pltpu.make_async_copy(result_ref.at[bin_no, r], out_hbm.at[r, bin_no], sems.at[bin_no, r])
 
-    @pl.loop(0, bins, unroll=2)
+    @pl.loop(0, bins, unroll=4)
     def _(bin_no):
         for r in range(ROUNDS):
             right = jnp.concatenate(

time: 63 us -> 63 us (level)
  no operation moved by 1% of the time
where the time goes in v8:
time: 63 us; the launch traced here: 62.8 us
  starting transfers between devices  28.1 us (45%)
  waiting for transfers between devices  17.7 us (28%)
  Pallas kernels  16 us (25%)
  other arithmetic  0.69 us (1%)
    ppermute x22, starting transfers between devices, swap(): return lax.ppermute(value, axis, [(i, i ^ distance) for i in range(count)])  28.1 us
    ppermute x22, waiting for transfers between devices, swap(): return lax.ppermute(value, axis, [(i, i ^ distance) for i in range(count)])  17.7 us
    pallas_call x1, Pallas kernels, local_spectra(): pl.pallas_call(functools.partial(spectra_kernel, chan_rows, win_count, pi...  8.16 us
    pallas_call x1, Pallas kernels, correlate(): pl.pallas_call(functools.partial(correlate_kernel, scale, layout), in_spe...  4.45 us
    pallas_call x4, Pallas kernels, pick(): pl.pallas_call(functools.partial(pick_kernel, places), in_specs=[pl.Block...  2.47 us
  transfers between devices with their start and end apart: 22, of which 9 were waited for; matrix products, arithmetic and copies ran while one was open for 1% of the time, Pallas kernels for 5%

profile of v8, /device:TPU:0, one launch (start us, length us, event | category | flops | bytes accessed | tf_op | source)
XLA Modules:
  0.0 62.8 jit_solution(1980914940508622459)
XLA Ops:
  0.0 8.2 %spectra.1 = (bf16[16,32,256]{2,1,0:T(8,128)(2,1)S(1)}, bf16[16,32,256]{2,1,0:T(8,128)(2,1)S(1)}, bf16[16,32,256]{2,1,0:T(8,128)(2,1)S(1)}, bf16[16,32,256]{2,1,0:T(8,128)(2,1)S(1)}) custom-call(s32[1]{0:T(128)} %bitcast.win_ref, bf16[256,32,1024]{2,1,0:T(8,128)(2,1)} %traces_ref.1), custom_call_target="tpu_custom_call" | custom-call | flops 1073741824 | bytes 16777216 | tf_op jit(solution)/shard_map/spectra/pallas_call | solution.py:105
  8.2 3.1 %collective-permute-start = (bf16[16,32,256]{2,1,0:T(8,128)(2,1)S(1)}, bf16[16,32,256]{2,1,0:T(8,128)(2,1)S(1)}, u32[]{:S(2)}, u32[]{:S(2)}) collective-permute-start(bf16[16,32,256]{2,1,0:T(8,128)(2,1)S(1)} %get-tuple-element.14), channel_id=1, source_target_pairs={{0,1},{1,0},{2,3},{3,2},{4,5},{5,4},{6,7},{7,6},{8,9},{9,8},{10,11... | collective-permute-start | bytes 786440 | tf_op jit(solution)/shard_map/ppermute | solution.py:287
  11.3 1.5 %collective-permute-start.4 = (bf16[16,32,256]{2,1,0:T(8,128)(2,1)S(1)}, bf16[16,32,256]{2,1,0:T(8,128)(2,1)S(1)}, u32[]{:S(2)}, u32[]{:S(2)}) collective-permute-start(bf16[16,32,256]{2,1,0:T(8,128)(2,1)S(1)} %get-tuple-element.13.refs_0_), channel_id=1, source_target_pairs={{0,16},{4,20},{8,24},{12,28},{16,0},{20,4},{24,8},{28,12},{1,17},{... | collective-permute-start | bytes 786440 | tf_op jit(solution)/shard_map/ppermute | solution.py:287
  12.8 1.5 %collective-permute-start.3 = (bf16[16,32,256]{2,1,0:T(8,128)(2,1)S(1)}, bf16[16,32,256]{2,1,0:T(8,128)(2,1)S(1)}, u32[]{:S(2)}, u32[]{:S(2)}) collective-permute-start(bf16[16,32,256]{2,1,0:T(8,128)(2,1)S(1)} %get-tuple-element.13.refs_0_), channel_id=1, source_target_pairs={{0,8},{4,12},{8,0},{12,4},{16,24},{20,28},{24,16},{28,20},{1,9},{5... | collective-permute-start | bytes 786440 | tf_op jit(solution)/shard_map/ppermute | solution.py:287
  14.8 2.6 %collective-permute-start.1 = (bf16[16,32,256]{2,1,0:T(8,128)(2,1)S(1)}, bf16[16,32,256]{2,1,0:T(8,128)(2,1)S(1)}, u32[]{:S(2)}, u32[]{:S(2)}) collective-permute-start(bf16[16,32,256]{2,1,0:T(8,128)(2,1)S(1)} %get-tuple-element.15), channel_id=1, source_target_pairs={{0,2},{1,3},{2,0},{3,1},{4,6},{5,7},{6,4},{7,5},{8,10},{9,11},{10,... | collective-permute-start | bytes 786440 | tf_op jit(solution)/shard_map/ppermute | solution.py:287
  17.3 2.4 %collective-permute-done.refs_1_.refs_0_ = bf16[16,32,256]{2,1,0:T(8,128)(2,1)S(1)} collective-permute-done((bf16[16,32,256]{2,1,0:T(8,128)(2,1)S(1)}, bf16[16,32,256]{2,1,0:T(8,128)(2,1)S(1)}, u32[]{:S(2)}, u32[]{:S(2)}) %collective-permute-start) | collective-permute-done | bytes 262176 | tf_op jit(solution)/shard_map/ppermute | solution.py:287
  19.7 2.3 %collective-permute-done.3.refs_1_.refs_4_ = bf16[16,32,256]{2,1,0:T(8,128)(2,1)S(1)} collective-permute-done((bf16[16,32,256]{2,1,0:T(8,128)(2,1)S(1)}, bf16[16,32,256]{2,1,0:T(8,128)(2,1)S(1)}, u32[]{:S(2)}, u32[]{:S(2)}) %collective-permute-start.3) | collective-permute-done | bytes 262176 | tf_op jit(solution)/shard_map/ppermute | solution.py:287
  22.5 1.5 %collective-permute-start.7 = (bf16[16,32,256]{2,1,0:T(8,128)(2,1)S(1)}, bf16[16,32,256]{2,1,0:T(8,128)(2,1)S(1)}, u32[]{:S(2)}, u32[]{:S(2)}) collective-permute-start(bf16[16,32,256]{2,1,0:T(8,128)(2,1)S(1)} %collective-permute-done.refs_1_.refs_0_), channel_id=1, source_target_pairs={{0,8},{4,12},{8,0},{12,4},{16,24},{20,28},{24,16},{28,20},{1,9},{5... | collective-permute-start | bytes 786440 | tf_op jit(solution)/shard_map/ppermute | solution.py:287
  24.0 4.2 %collective-permute-done.1.refs_2_.refs_0_ = bf16[16,32,256]{2,1,0:T(8,128)(2,1)S(1)} collective-permute-done((bf16[16,32,256]{2,1,0:T(8,128)(2,1)S(1)}, bf16[16,32,256]{2,1,0:T(8,128)(2,1)S(1)}, u32[]{:S(2)}, u32[]{:S(2)}) %collective-permute-start.1) | collective-permute-done | bytes 262176 | tf_op jit(solution)/shard_map/ppermute | solution.py:287
  28.2 3.6 %collective-permute-start.2 = (bf16[16,32,256]{2,1,0:T(8,128)(2,1)S(1)}, bf16[16,32,256]{2,1,0:T(8,128)(2,1)S(1)}, u32[]{:S(2)}, u32[]{:S(2)}) collective-permute-start(bf16[16,32,256]{2,1,0:T(8,128)(2,1)S(1)} %get-tuple-element.17), channel_id=1, source_target_pairs={{0,3},{1,2},{2,1},{3,0},{4,7},{5,6},{6,5},{7,4},{8,11},{9,10},{10,... | collective-permute-start | bytes 786440 | tf_op jit(solution)/shard_map/ppermute | solution.py:287
  31.8 1.6 %collective-permute-start.12 = (bf16[16,32,256]{2,1,0:T(8,128)(2,1)S(1)}, bf16[16,32,256]{2,1,0:T(8,128)(2,1)S(1)}, u32[]{:S(2)}, u32[]{:S(2)}) collective-permute-start(bf16[16,32,256]{2,1,0:T(8,128)(2,1)S(1)} %collective-permute-done.1.refs_2_.refs_0_), channel_id=1, source_target_pairs={{0,8},{4,12},{8,0},{12,4},{16,24},{20,28},{24,16},{28,20},{1,9},{5... | collective-permute-start | bytes 786440 | tf_op jit(solution)/shard_map/ppermute | solution.py:287
  33.7 1.6 %collective-permute-start.13 = (bf16[16,32,256]{2,1,0:T(8,128)(2,1)S(1)}, bf16[16,32,256]{2,1,0:T(8,128)(2,1)S(1)}, u32[]{:S(2)}, u32[]{:S(2)}) collective-permute-start(bf16[16,32,256]{2,1,0:T(8,128)(2,1)S(1)} %collective-permute-done.1.refs_2_.refs_0_), channel_id=1, source_target_pairs={{0,16},{4,20},{8,24},{12,28},{16,0},{20,4},{24,8},{28,12},{1,17},{... | collective-permute-start | bytes 786440 | tf_op jit(solution)/shard_map/ppermute | solution.py:287
  35.3 1.2 %collective-permute-done.2.refs_3_.refs_4_ = bf16[16,32,256]{2,1,0:T(8,128)(2,1)S(1)} collective-permute-done((bf16[16,32,256]{2,1,0:T(8,128)(2,1)S(1)}, bf16[16,32,256]{2,1,0:T(8,128)(2,1)S(1)}, u32[]{:S(2)}, u32[]{:S(2)}) %collective-permute-start.2) | collective-permute-done | bytes 262176 | tf_op jit(solution)/shard_map/ppermute | solution.py:287
  36.5 1.8 %collective-permute-done.12.refs_1_.refs_11_ = bf16[16,32,256]{2,1,0:T(8,128)(2,1)S(1)} collective-permute-done((bf16[16,32,256]{2,1,0:T(8,128)(2,1)S(1)}, bf16[16,32,256]{2,1,0:T(8,128)(2,1)S(1)}, u32[]{:S(2)}, u32[]{:S(2)}) %collective-permute-start.12) | collective-permute-done | bytes 262176 | tf_op jit(solution)/shard_map/ppermute | solution.py:287
  38.3 1.5 %collective-permute-start.16 = (bf16[16,32,256]{2,1,0:T(8,128)(2,1)S(1)}, bf16[16,32,256]{2,1,0:T(8,128)(2,1)S(1)}, u32[]{:S(2)}, u32[]{:S(2)}) collective-permute-start(bf16[16,32,256]{2,1,0:T(8,128)(2,1)S(1)} %collective-permute-done.2.refs_3_.refs_4_), channel_id=1, source_target_pairs={{0,16},{4,20},{8,24},{12,28},{16,0},{20,4},{24,8},{28,12},{1,17},{... | collective-permute-start | bytes 786440 | tf_op jit(solution)/shard_map/ppermute | solution.py:287
  39.8 1.5 %collective-permute-start.15 = (bf16[16,32,256]{2,1,0:T(8,128)(2,1)S(1)}, bf16[16,32,256]{2,1,0:T(8,128)(2,1)S(1)}, u32[]{:S(2)}, u32[]{:S(2)}) collective-permute-start(bf16[16,32,256]{2,1,0:T(8,128)(2,1)S(1)} %collective-permute-done.2.refs_3_.refs_4_), channel_id=1, source_target_pairs={{0,8},{4,12},{8,0},{12,4},{16,24},{20,28},{24,16},{28,20},{1,9},{5... | collective-permute-start | bytes 786440 | tf_op jit(solution)/shard_map/ppermute | solution.py:287
  41.5 0.6 collective-permute-start.9
  42.3 0.6 collective-permute-start.10
  42.9 1.6 %collective-permute-start.14 = (bf16[8,32,256]{2,1,0:T(8,128)(2,1)S(1)}, bf16[8,32,256]{2,1,0:T(8,128)(2,1)S(1)}, u32[]{:S(2)}, u32[]{:S(2)}) collective-permute-start(bf16[8,32,256]{2,1,0:T(8,128)(2,1)S(1)} %slice.26), channel_id=1, source_target_pairs={{0,8},{4,12},{8,0},{12,4},{16,24},{20,28},{24,16},{28,20},{1,9},{5... | collective-permute-start | bytes 393224 | tf_op jit(solution)/shard_map/ppermute | solution.py:287
  44.4 3.5 %collective-permute-done.16.refs_6_.refs_16_ = bf16[16,32,256]{2,1,0:T(8,128)(2,1)S(1)} collective-permute-done((bf16[16,32,256]{2,1,0:T(8,128)(2,1)S(1)}, bf16[16,32,256]{2,1,0:T(8,128)(2,1)S(1)}, u32[]{:S(2)}, u32[]{:S(2)}) %collective-permute-start.16) | collective-permute-done | bytes 262176 | tf_op jit(solution)/shard_map/ppermute | solution.py:287
  47.9 1.9 %collective-permute-start.19 = (bf16[8,32,256]{2,1,0:T(8,128)(2,1)S(1)}, bf16[8,32,256]{2,1,0:T(8,128)(2,1)S(1)}, u32[]{:S(2)}, u32[]{:S(2)}) collective-permute-start(bf16[8,32,256]{2,1,0:T(8,128)(2,1)S(1)} %slice.28), channel_id=1, source_target_pairs={{0,16},{4,20},{8,24},{12,28},{16,0},{20,4},{24,8},{28,12},{1,17},{... | collective-permute-start | bytes 393224 | tf_op jit(solution)/shard_map/ppermute | solution.py:287
  49.9 0.8 %collective-permute-start.17 = (bf16[8,32,256]{2,1,0:T(8,128)(2,1)S(1)}, bf16[8,32,256]{2,1,0:T(8,128)(2,1)S(1)}, u32[]{:S(2)}, u32[]{:S(2)}) collective-permute-start(bf16[8,32,256]{2,1,0:T(8,128)(2,1)S(1)} %slice.27), channel_id=1, source_target_pairs={{0,8},{4,12},{8,0},{12,4},{16,24},{20,28},{24,16},{28,20},{1,9},{5... | collective-permute-start | bytes 393224 | tf_op jit(solution)/shard_map/ppermute | solution.py:287
  50.6 0.6 collective-permute-start.20
  51.2 0.6 pick.4
  51.9 0.6 pick.5
  52.6 0.6 collective-permute-start.11
  53.1 1.8 %collective-permute-done.17.refs_7_.refs_17_ = bf16[8,32,256]{2,1,0:T(8,128)(2,1)S(1)} collective-permute-done((bf16[8,32,256]{2,1,0:T(8,128)(2,1)S(1)}, bf16[8,32,256]{2,1,0:T(8,128)(2,1)S(1)}, u32[]{:S(2)}, u32[]{:S(2)}) %collective-permute-start.17) | collective-permute-done | bytes 131104 | tf_op jit(solution)/shard_map/ppermute | solution.py:287
  54.9 0.6 pick.6
  55.7 0.6 pick.7
  56.8 1.0 %left_side.1.left_ref = bf16[8,512,256]{2,1,0:T(8,128)(2,1)S(1)} custom-call(bf16[16,32,256]{2,1,0:T(8,128)(2,1)S(1)} %get-tuple-element.13.refs_0_, bf16[16,32,256]{2,1,0:T(8,128)(2,1)S(1)} %collective-permute-done.refs_1_.refs_0_, bf16[16,32,256]{2,1,0:T(8,128)(2,1)S(1)} %collective-permute-done.1.refs_2_.refs_0_, ...), custom_call_target="tpu_custom_call" | custom-call | tf_op jit(solution)/shard_map/left_side/pallas_call | solution.py:190
  57.8 0.5 collective-permute-done.21.refs_3_
  58.3 4.4 %cross_spectra.1 = f32[2,8,2,256,256]{4,3,2,1,0:T(8,128)} custom-call(s32[2]{0:T(128)S(1)} %broadcast_xor_fusion.1.far_ref, bf16[8,512,256]{2,1,0:T(8,128)(2,1)S(1)} %left_side.1.left_ref, bf16[2,16,32,256]{3,2,1,0:T(8,128)(2,1)S(1)} %collective-permute-done.6.refs_0_, bf16[2,16,32,256]{3,2,1,0:T(8,128)(2,1)S(1)} %collective-permute-done.11.refs_1_, ...), custom_call_target="tpu_custom_call" | custom-call | flops 1073741824 | bytes 8388608 | tf_op jit(solution)/shard_map/cross_spectra/pallas_call | solution.py:261
  (37 shorter events, 2.5 us)
Async XLA Ops:
  0.0 33.4 %copy-start.1 = (s32[8]{0:T(128)S(1)}, s32[8]{0:T(128)}, u32[]{:S(2)}) copy-start(s32[8]{0:T(128)} %param.5) | copy-start | bytes 100
  0.0 33.6 %copy-start = (s32[2,8]{1,0:T(2,128)S(1)}, s32[2,8]{1,0:T(2,128)}, u32[]{:S(2)}) copy-start(s32[2,8]{1,0:T(2,128)} %param.4) | copy-start | bytes 196
  8.2 11.6 %collective-permute-start = (bf16[16,32,256]{2,1,0:T(8,128)(2,1)S(1)}, bf16[16,32,256]{2,1,0:T(8,128)(2,1)S(1)}, u32[]{:S(2)}, u32[]{:S(2)}) collective-permute-start(bf16[16,32,256]{2,1,0:T(8,128)(2,1)S(1)} %get-tuple-element.14), channel_id=1, source_target_pairs={{0,1},{1,0},{2,3},{3,2},{4,5},{5,4},{6,7},{7,6},{8,9},{9,8},{10,11... | collective-permute-start | bytes 786440 | tf_op jit(solution)/shard_map/ppermute | solution.py:287
  11.3 8.5 %collective-permute-start.4 = (bf16[16,32,256]{2,1,0:T(8,128)(2,1)S(1)}, bf16[16,32,256]{2,1,0:T(8,128)(2,1)S(1)}, u32[]{:S(2)}, u32[]{:S(2)}) collective-permute-start(bf16[16,32,256]{2,1,0:T(8,128)(2,1)S(1)} %get-tuple-element.13.refs_0_), channel_id=1, source_target_pairs={{0,16},{4,20},{8,24},{12,28},{16,0},{20,4},{24,8},{28,12},{1,17},{... | collective-permute-start | bytes 786440 | tf_op jit(solution)/shard_map/ppermute | solution.py:287
  12.8 9.2 %collective-permute-start.3 = (bf16[16,32,256]{2,1,0:T(8,128)(2,1)S(1)}, bf16[16,32,256]{2,1,0:T(8,128)(2,1)S(1)}, u32[]{:S(2)}, u32[]{:S(2)}) collective-permute-start(bf16[16,32,256]{2,1,0:T(8,128)(2,1)S(1)} %get-tuple-element.13.refs_0_), channel_id=1, source_target_pairs={{0,8},{4,12},{8,0},{12,4},{16,24},{20,28},{24,16},{28,20},{1,9},{5... | collective-permute-start | bytes 786440 | tf_op jit(solution)/shard_map/ppermute | solution.py:287
  14.3 17.6 %collective-permute-start.5 = (bf16[16,32,256]{2,1,0:T(8,128)(2,1)S(1)}, bf16[16,32,256]{2,1,0:T(8,128)(2,1)S(1)}, u32[]{:S(2)}, u32[]{:S(2)}) collective-permute-start(bf16[16,32,256]{2,1,0:T(8,128)(2,1)S(1)} %get-tuple-element.13.refs_0_), channel_id=1, source_target_pairs={{0,24},{4,28},{8,16},{12,20},{16,8},{20,12},{24,0},{28,4},{1,25},{... | collective-permute-start | bytes 786440 | tf_op jit(solution)/shard_map/ppermute | solution.py:287
  14.8 13.5 %collective-permute-start.1 = (bf16[16,32,256]{2,1,0:T(8,128)(2,1)S(1)}, bf16[16,32,256]{2,1,0:T(8,128)(2,1)S(1)}, u32[]{:S(2)}, u32[]{:S(2)}) collective-permute-start(bf16[16,32,256]{2,1,0:T(8,128)(2,1)S(1)} %get-tuple-element.15), channel_id=1, source_target_pairs={{0,2},{1,3},{2,0},{3,1},{4,6},{5,7},{6,4},{7,5},{8,10},{9,11},{10,... | collective-permute-start | bytes 786440 | tf_op jit(solution)/shard_map/ppermute | solution.py:287
  22.0 9.8 %collective-permute-start.8 = (bf16[16,32,256]{2,1,0:T(8,128)(2,1)S(1)}, bf16[16,32,256]{2,1,0:T(8,128)(2,1)S(1)}, u32[]{:S(2)}, u32[]{:S(2)}) collective-permute-start(bf16[16,32,256]{2,1,0:T(8,128)(2,1)S(1)} %collective-permute-done.refs_1_.refs_0_), channel_id=1, source_target_pairs={{0,16},{4,20},{8,24},{12,28},{16,0},{20,4},{24,8},{28,12},{1,17},{... | collective-permute-start | bytes 786440 | tf_op jit(solution)/shard_map/ppermute | solution.py:287
  22.5 9.3 %collective-permute-start.7 = (bf16[16,32,256]{2,1,0:T(8,128)(2,1)S(1)}, bf16[16,32,256]{2,1,0:T(8,128)(2,1)S(1)}, u32[]{:S(2)}, u32[]{:S(2)}) collective-permute-start(bf16[16,32,256]{2,1,0:T(8,128)(2,1)S(1)} %collective-permute-done.refs_1_.refs_0_), channel_id=1, source_target_pairs={{0,8},{4,12},{8,0},{12,4},{16,24},{20,28},{24,16},{28,20},{1,9},{5... | collective-permute-start | bytes 786440 | tf_op jit(solution)/shard_map/ppermute | solution.py:287
  28.2 8.3 %collective-permute-start.2 = (bf16[16,32,256]{2,1,0:T(8,128)(2,1)S(1)}, bf16[16,32,256]{2,1,0:T(8,128)(2,1)S(1)}, u32[]{:S(2)}, u32[]{:S(2)}) collective-permute-start(bf16[16,32,256]{2,1,0:T(8,128)(2,1)S(1)} %get-tuple-element.17), channel_id=1, source_target_pairs={{0,3},{1,2},{2,1},{3,0},{4,7},{5,6},{6,5},{7,4},{8,11},{9,10},{10,... | collective-permute-start | bytes 786440 | tf_op jit(solution)/shard_map/ppermute | solution.py:287
  31.8 6.4 %collective-permute-start.12 = (bf16[16,32,256]{2,1,0:T(8,128)(2,1)S(1)}, bf16[16,32,256]{2,1,0:T(8,128)(2,1)S(1)}, u32[]{:S(2)}, u32[]{:S(2)}) collective-permute-start(bf16[16,32,256]{2,1,0:T(8,128)(2,1)S(1)} %collective-permute-done.1.refs_2_.refs_0_), channel_id=1, source_target_pairs={{0,8},{4,12},{8,0},{12,4},{16,24},{20,28},{24,16},{28,20},{1,9},{5... | collective-permute-start | bytes 786440 | tf_op jit(solution)/shard_map/ppermute | solution.py:287
  33.7 9.1 %collective-permute-start.13 = (bf16[16,32,256]{2,1,0:T(8,128)(2,1)S(1)}, bf16[16,32,256]{2,1,0:T(8,128)(2,1)S(1)}, u32[]{:S(2)}, u32[]{:S(2)}) collective-permute-start(bf16[16,32,256]{2,1,0:T(8,128)(2,1)S(1)} %collective-permute-done.1.refs_2_.refs_0_), channel_id=1, source_target_pairs={{0,16},{4,20},{8,24},{12,28},{16,0},{20,4},{24,8},{28,12},{1,17},{... | collective-permute-start | bytes 786440 | tf_op jit(solution)/shard_map/ppermute | solution.py:287
  38.3 9.6 %collective-permute-start.16 = (bf16[16,32,256]{2,1,0:T(8,128)(2,1)S(1)}, bf16[16,32,256]{2,1,0:T(8,128)(2,1)S(1)}, u32[]{:S(2)}, u32[]{:S(2)}) collective-permute-start(bf16[16,32,256]{2,1,0:T(8,128)(2,1)S(1)} %collective-permute-done.2.refs_3_.refs_4_), channel_id=1, source_target_pairs={{0,16},{4,20},{8,24},{12,28},{16,0},{20,4},{24,8},{28,12},{1,17},{... | collective-permute-start | bytes 786440 | tf_op jit(solution)/shard_map/ppermute | solution.py:287
  39.8 10.1 %collective-permute-start.15 = (bf16[16,32,256]{2,1,0:T(8,128)(2,1)S(1)}, bf16[16,32,256]{2,1,0:T(8,128)(2,1)S(1)}, u32[]{:S(2)}, u32[]{:S(2)}) collective-permute-start(bf16[16,32,256]{2,1,0:T(8,128)(2,1)S(1)} %collective-permute-done.2.refs_3_.refs_4_), channel_id=1, source_target_pairs={{0,8},{4,12},{8,0},{12,4},{16,24},{20,28},{24,16},{28,20},{1,9},{5... | collective-permute-start | bytes 786440 | tf_op jit(solution)/shard_map/ppermute | solution.py:287
  41.5 9.1 %collective-permute-start.9 = (bf16[8,32,256]{2,1,0:T(8,128)(2,1)S(1)}, bf16[8,32,256]{2,1,0:T(8,128)(2,1)S(1)}, u32[]{:S(2)}, u32[]{:S(2)}) collective-permute-start(bf16[8,32,256]{2,1,0:T(8,128)(2,1)S(1)} %slice.24), channel_id=1, source_target_pairs={{0,8},{4,12},{8,0},{12,4},{16,24},{20,28},{24,16},{28,20},{1,9},{5... | collective-permute-start | bytes 393224 | tf_op jit(solution)/shard_map/ppermute | solution.py:287
  42.3 9.6 %collective-permute-start.10 = (bf16[8,32,256]{2,1,0:T(8,128)(2,1)S(1)}, bf16[8,32,256]{2,1,0:T(8,128)(2,1)S(1)}, u32[]{:S(2)}, u32[]{:S(2)}) collective-permute-start(bf16[8,32,256]{2,1,0:T(8,128)(2,1)S(1)} %slice.25), channel_id=1, source_target_pairs={{0,16},{4,20},{8,24},{12,28},{16,0},{20,4},{24,8},{28,12},{1,17},{... | collective-permute-start | bytes 393224 | tf_op jit(solution)/shard_map/ppermute | solution.py:287
  42.9 9.7 %collective-permute-start.14 = (bf16[8,32,256]{2,1,0:T(8,128)(2,1)S(1)}, bf16[8,32,256]{2,1,0:T(8,128)(2,1)S(1)}, u32[]{:S(2)}, u32[]{:S(2)}) collective-permute-start(bf16[8,32,256]{2,1,0:T(8,128)(2,1)S(1)} %slice.26), channel_id=1, source_target_pairs={{0,8},{4,12},{8,0},{12,4},{16,24},{20,28},{24,16},{28,20},{1,9},{5... | collective-permute-start | bytes 393224 | tf_op jit(solution)/shard_map/ppermute | solution.py:287
  47.9 7.7 %collective-permute-start.19 = (bf16[8,32,256]{2,1,0:T(8,128)(2,1)S(1)}, bf16[8,32,256]{2,1,0:T(8,128)(2,1)S(1)}, u32[]{:S(2)}, u32[]{:S(2)}) collective-permute-start(bf16[8,32,256]{2,1,0:T(8,128)(2,1)S(1)} %slice.28), channel_id=1, source_target_pairs={{0,16},{4,20},{8,24},{12,28},{16,0},{20,4},{24,8},{28,12},{1,17},{... | collective-permute-start | bytes 393224 | tf_op jit(solution)/shard_map/ppermute | solution.py:287
  49.9 5.0 %collective-permute-start.17 = (bf16[8,32,256]{2,1,0:T(8,128)(2,1)S(1)}, bf16[8,32,256]{2,1,0:T(8,128)(2,1)S(1)}, u32[]{:S(2)}, u32[]{:S(2)}) collective-permute-start(bf16[8,32,256]{2,1,0:T(8,128)(2,1)S(1)} %slice.27), channel_id=1, source_target_pairs={{0,8},{4,12},{8,0},{12,4},{16,24},{20,28},{24,16},{28,20},{1,9},{5... | collective-permute-start | bytes 393224 | tf_op jit(solution)/shard_map/ppermute | solution.py:287
  50.6 5.0 %collective-permute-start.20 = (bf16[8,32,256]{2,1,0:T(8,128)(2,1)S(1)}, bf16[8,32,256]{2,1,0:T(8,128)(2,1)S(1)}, u32[]{:S(2)}, u32[]{:S(2)}) collective-permute-start(bf16[8,32,256]{2,1,0:T(8,128)(2,1)S(1)} %slice.29), channel_id=1, source_target_pairs={{0,16},{4,20},{8,24},{12,28},{16,0},{20,4},{24,8},{28,12},{1,17},{... | collective-permute-start | bytes 393224 | tf_op jit(solution)/shard_map/ppermute | solution.py:287
  51.9 5.9 %collective-permute-start.6 = (bf16[2,16,32,256]{3,2,1,0:T(8,128)(2,1)S(1)}, bf16[2,16,32,256]{3,2,1,0:T(8,128)(2,1)S(1)}, u32[]{:S(2)}, u32[]{:S(2)}) collective-permute-start(bf16[2,16,32,256]{3,2,1,0:T(8,128)(2,1)S(1)} %pick.4), channel_id=1, source_target_pairs={{0,4},{4,0},{8,12},{12,8},{16,20},{20,16},{24,28},{28,24},{1,5},{5... | collective-permute-start | bytes 1572872 | tf_op jit(solution)/shard_map/ppermute | solution.py:287
  52.6 5.2 %collective-permute-start.11 = (bf16[2,16,32,256]{3,2,1,0:T(8,128)(2,1)S(1)}, bf16[2,16,32,256]{3,2,1,0:T(8,128)(2,1)S(1)}, u32[]{:S(2)}, u32[]{:S(2)}) collective-permute-start(bf16[2,16,32,256]{3,2,1,0:T(8,128)(2,1)S(1)} %pick.5), channel_id=1, source_target_pairs={{0,4},{4,0},{8,12},{12,8},{16,20},{20,16},{24,28},{28,24},{1,5},{5... | collective-permute-start | bytes 1572872 | tf_op jit(solution)/shard_map/ppermute | solution.py:287
  55.5 2.3 %collective-permute-start.18 = (bf16[2,16,32,256]{3,2,1,0:T(8,128)(2,1)S(1)}, bf16[2,16,32,256]{3,2,1,0:T(8,128)(2,1)S(1)}, u32[]{:S(2)}, u32[]{:S(2)}) collective-permute-start(bf16[2,16,32,256]{3,2,1,0:T(8,128)(2,1)S(1)} %pick.6), channel_id=1, source_target_pairs={{0,4},{4,0},{8,12},{12,8},{16,20},{20,16},{24,28},{28,24},{1,5},{5... | collective-permute-start | bytes 1572872 | tf_op jit(solution)/shard_map/ppermute | solution.py:287
  56.3 2.0 %collective-permute-start.21 = (bf16[2,16,32,256]{3,2,1,0:T(8,128)(2,1)S(1)}, bf16[2,16,32,256]{3,2,1,0:T(8,128)(2,1)S(1)}, u32[]{:S(2)}, u32[]{:S(2)}) collective-permute-start(bf16[2,16,32,256]{3,2,1,0:T(8,128)(2,1)S(1)} %pick.7), channel_id=1, source_target_pairs={{0,4},{4,0},{8,12},{12,8},{16,20},{20,16},{24,28},{28,24},{1,5},{5... | collective-permute-start | bytes 1572872 | tf_op jit(solution)/shard_map/ppermute | solution.py:287

commit v9 on v7

--- a/solution.py
+++ b/solution.py
@@ -299,7 +299,7 @@
         if distance != 6 or not relay:
             found[distance] = [swap(piece, "pair", distance)]
     if relay and 6 < pair_count:
-        found[6] = [swap(found[4][0][:half], "pair", 2), swap(found[2][0][half:], "pair", 4)]
+        found[6] = [swap(found[2][0][:half], "pair", 4), swap(found[4][0][half:], "pair", 2)]
     return found
 
 

time: 63 us -> 63 us (level)
  no operation moved by 1% of the time
where the time goes in v9:
time: 63 us; the launch traced here: 62.8 us
  starting transfers between devices  28.1 us (45%)
  waiting for transfers between devices  17.7 us (28%)
  Pallas kernels  16 us (25%)
  other arithmetic  0.69 us (1%)
    ppermute x22, starting transfers between devices, swap(): return lax.ppermute(value, axis, [(i, i ^ distance) for i in range(count)])  28.1 us
    ppermute x22, waiting for transfers between devices, swap(): return lax.ppermute(value, axis, [(i, i ^ distance) for i in range(count)])  17.7 us
    pallas_call x1, Pallas kernels, local_spectra(): pl.pallas_call(functools.partial(spectra_kernel, chan_rows, win_count, pi...  8.16 us
    pallas_call x1, Pallas kernels, correlate(): pl.pallas_call(functools.partial(correlate_kernel, scale, layout), in_spe...  4.45 us
    pallas_call x4, Pallas kernels, pick(): pl.pallas_call(functools.partial(pick_kernel, places), in_specs=[pl.Block...  2.47 us
  transfers between devices with their start and end apart: 22, of which 9 were waited for; matrix products, arithmetic and copies ran while one was open for 1% of the time, Pallas kernels for 5%

profile of v9, /device:TPU:0, one launch (start us, length us, event | category | flops | bytes accessed | tf_op | source)
XLA Modules:
  0.0 62.8 jit_solution(11559807060067017212)
XLA Ops:
  0.0 8.2 %spectra.1 = (bf16[16,32,256]{2,1,0:T(8,128)(2,1)S(1)}, bf16[16,32,256]{2,1,0:T(8,128)(2,1)S(1)}, bf16[16,32,256]{2,1,0:T(8,128)(2,1)S(1)}, bf16[16,32,256]{2,1,0:T(8,128)(2,1)S(1)}) custom-call(s32[1]{0:T(128)} %bitcast.win_ref, bf16[256,32,1024]{2,1,0:T(8,128)(2,1)} %traces_ref.1), custom_call_target="tpu_custom_call" | custom-call | flops 1073741824 | bytes 16777216 | tf_op jit(solution)/shard_map/spectra/pallas_call | solution.py:105
  8.2 3.1 %collective-permute-start = (bf16[16,32,256]{2,1,0:T(8,128)(2,1)S(1)}, bf16[16,32,256]{2,1,0:T(8,128)(2,1)S(1)}, u32[]{:S(2)}, u32[]{:S(2)}) collective-permute-start(bf16[16,32,256]{2,1,0:T(8,128)(2,1)S(1)} %get-tuple-element.14), channel_id=1, source_target_pairs={{0,1},{1,0},{2,3},{3,2},{4,5},{5,4},{6,7},{7,6},{8,9},{9,8},{10,11... | collective-permute-start | bytes 786440 | tf_op jit(solution)/shard_map/ppermute | solution.py:287
  11.3 1.5 %collective-permute-start.4 = (bf16[16,32,256]{2,1,0:T(8,128)(2,1)S(1)}, bf16[16,32,256]{2,1,0:T(8,128)(2,1)S(1)}, u32[]{:S(2)}, u32[]{:S(2)}) collective-permute-start(bf16[16,32,256]{2,1,0:T(8,128)(2,1)S(1)} %get-tuple-element.13.refs_0_), channel_id=1, source_target_pairs={{0,16},{4,20},{8,24},{12,28},{16,0},{20,4},{24,8},{28,12},{1,17},{... | collective-permute-start | bytes 786440 | tf_op jit(solution)/shard_map/ppermute | solution.py:287
  12.8 1.5 %collective-permute-start.3 = (bf16[16,32,256]{2,1,0:T(8,128)(2,1)S(1)}, bf16[16,32,256]{2,1,0:T(8,128)(2,1)S(1)}, u32[]{:S(2)}, u32[]{:S(2)}) collective-permute-start(bf16[16,32,256]{2,1,0:T(8,128)(2,1)S(1)} %get-tuple-element.13.refs_0_), channel_id=1, source_target_pairs={{0,8},{4,12},{8,0},{12,4},{16,24},{20,28},{24,16},{28,20},{1,9},{5... | collective-permute-start | bytes 786440 | tf_op jit(solution)/shard_map/ppermute | solution.py:287
  14.8 2.6 %collective-permute-start.1 = (bf16[16,32,256]{2,1,0:T(8,128)(2,1)S(1)}, bf16[16,32,256]{2,1,0:T(8,128)(2,1)S(1)}, u32[]{:S(2)}, u32[]{:S(2)}) collective-permute-start(bf16[16,32,256]{2,1,0:T(8,128)(2,1)S(1)} %get-tuple-element.15), channel_id=1, source_target_pairs={{0,2},{1,3},{2,0},{3,1},{4,6},{5,7},{6,4},{7,5},{8,10},{9,11},{10,... | collective-permute-start | bytes 786440 | tf_op jit(solution)/shard_map/ppermute | solution.py:287
  17.3 2.4 %collective-permute-done.refs_1_.refs_0_ = bf16[16,32,256]{2,1,0:T(8,128)(2,1)S(1)} collective-permute-done((bf16[16,32,256]{2,1,0:T(8,128)(2,1)S(1)}, bf16[16,32,256]{2,1,0:T(8,128)(2,1)S(1)}, u32[]{:S(2)}, u32[]{:S(2)}) %collective-permute-start) | collective-permute-done | bytes 262176 | tf_op jit(solution)/shard_map/ppermute | solution.py:287
  19.7 2.3 %collective-permute-done.3.refs_1_.refs_4_ = bf16[16,32,256]{2,1,0:T(8,128)(2,1)S(1)} collective-permute-done((bf16[16,32,256]{2,1,0:T(8,128)(2,1)S(1)}, bf16[16,32,256]{2,1,0:T(8,128)(2,1)S(1)}, u32[]{:S(2)}, u32[]{:S(2)}) %collective-permute-start.3) | collective-permute-done | bytes 262176 | tf_op jit(solution)/shard_map/ppermute | solution.py:287
  22.5 1.5 %collective-permute-start.7 = (bf16[16,32,256]{2,1,0:T(8,128)(2,1)S(1)}, bf16[16,32,256]{2,1,0:T(8,128)(2,1)S(1)}, u32[]{:S(2)}, u32[]{:S(2)}) collective-permute-start(bf16[16,32,256]{2,1,0:T(8,128)(2,1)S(1)} %collective-permute-done.refs_1_.refs_0_), channel_id=1, source_target_pairs={{0,8},{4,12},{8,0},{12,4},{16,24},{20,28},{24,16},{28,20},{1,9},{5... | collective-permute-start | bytes 786440 | tf_op jit(solution)/shard_map/ppermute | solution.py:287
  24.0 4.2 %collective-permute-done.1.refs_2_.refs_0_ = bf16[16,32,256]{2,1,0:T(8,128)(2,1)S(1)} collective-permute-done((bf16[16,32,256]{2,1,0:T(8,128)(2,1)S(1)}, bf16[16,32,256]{2,1,0:T(8,128)(2,1)S(1)}, u32[]{:S(2)}, u32[]{:S(2)}) %collective-permute-start.1) | collective-permute-done | bytes 262176 | tf_op jit(solution)/shard_map/ppermute | solution.py:287
  28.2 3.6 %collective-permute-start.2 = (bf16[16,32,256]{2,1,0:T(8,128)(2,1)S(1)}, bf16[16,32,256]{2,1,0:T(8,128)(2,1)S(1)}, u32[]{:S(2)}, u32[]{:S(2)}) collective-permute-start(bf16[16,32,256]{2,1,0:T(8,128)(2,1)S(1)} %get-tuple-element.17), channel_id=1, source_target_pairs={{0,3},{1,2},{2,1},{3,0},{4,7},{5,6},{6,5},{7,4},{8,11},{9,10},{10,... | collective-permute-start | bytes 786440 | tf_op jit(solution)/shard_map/ppermute | solution.py:287
  31.8 1.6 %collective-permute-start.12 = (bf16[16,32,256]{2,1,0:T(8,128)(2,1)S(1)}, bf16[16,32,256]{2,1,0:T(8,128)(2,1)S(1)}, u32[]{:S(2)}, u32[]{:S(2)}) collective-permute-start(bf16[16,32,256]{2,1,0:T(8,128)(2,1)S(1)} %collective-permute-done.1.refs_2_.refs_0_), channel_id=1, source_target_pairs={{0,8},{4,12},{8,0},{12,4},{16,24},{20,28},{24,16},{28,20},{1,9},{5... | collective-permute-start | bytes 786440 | tf_op jit(solution)/shard_map/ppermute | solution.py:287
  33.7 1.6 %collective-permute-start.13 = (bf16[16,32,256]{2,1,0:T(8,128)(2,1)S(1)}, bf16[16,32,256]{2,1,0:T(8,128)(2,1)S(1)}, u32[]{:S(2)}, u32[]{:S(2)}) collective-permute-start(bf16[16,32,256]{2,1,0:T(8,128)(2,1)S(1)} %collective-permute-done.1.refs_2_.refs_0_), channel_id=1, source_target_pairs={{0,16},{4,20},{8,24},{12,28},{16,0},{20,4},{24,8},{28,12},{1,17},{... | collective-permute-start | bytes 786440 | tf_op jit(solution)/shard_map/ppermute | solution.py:287
  35.3 1.2 %collective-permute-done.2.refs_3_.refs_4_ = bf16[16,32,256]{2,1,0:T(8,128)(2,1)S(1)} collective-permute-done((bf16[16,32,256]{2,1,0:T(8,128)(2,1)S(1)}, bf16[16,32,256]{2,1,0:T(8,128)(2,1)S(1)}, u32[]{:S(2)}, u32[]{:S(2)}) %collective-permute-start.2) | collective-permute-done | bytes 262176 | tf_op jit(solution)/shard_map/ppermute | solution.py:287
  36.5 1.8 %collective-permute-done.12.refs_1_.refs_11_ = bf16[16,32,256]{2,1,0:T(8,128)(2,1)S(1)} collective-permute-done((bf16[16,32,256]{2,1,0:T(8,128)(2,1)S(1)}, bf16[16,32,256]{2,1,0:T(8,128)(2,1)S(1)}, u32[]{:S(2)}, u32[]{:S(2)}) %collective-permute-start.12) | collective-permute-done | bytes 262176 | tf_op jit(solution)/shard_map/ppermute | solution.py:287
  38.3 1.5 %collective-permute-start.16 = (bf16[16,32,256]{2,1,0:T(8,128)(2,1)S(1)}, bf16[16,32,256]{2,1,0:T(8,128)(2,1)S(1)}, u32[]{:S(2)}, u32[]{:S(2)}) collective-permute-start(bf16[16,32,256]{2,1,0:T(8,128)(2,1)S(1)} %collective-permute-done.2.refs_3_.refs_4_), channel_id=1, source_target_pairs={{0,16},{4,20},{8,24},{12,28},{16,0},{20,4},{24,8},{28,12},{1,17},{... | collective-permute-start | bytes 786440 | tf_op jit(solution)/shard_map/ppermute | solution.py:287
  39.8 1.5 %collective-permute-start.15 = (bf16[16,32,256]{2,1,0:T(8,128)(2,1)S(1)}, bf16[16,32,256]{2,1,0:T(8,128)(2,1)S(1)}, u32[]{:S(2)}, u32[]{:S(2)}) collective-permute-start(bf16[16,32,256]{2,1,0:T(8,128)(2,1)S(1)} %collective-permute-done.2.refs_3_.refs_4_), channel_id=1, source_target_pairs={{0,8},{4,12},{8,0},{12,4},{16,24},{20,28},{24,16},{28,20},{1,9},{5... | collective-permute-start | bytes 786440 | tf_op jit(solution)/shard_map/ppermute | solution.py:287
  41.5 0.6 collective-permute-start.10
  42.3 0.6 collective-permute-start.9
  42.9 1.6 %collective-permute-start.19 = (bf16[8,32,256]{2,1,0:T(8,128)(2,1)S(1)}, bf16[8,32,256]{2,1,0:T(8,128)(2,1)S(1)}, u32[]{:S(2)}, u32[]{:S(2)}) collective-permute-start(bf16[8,32,256]{2,1,0:T(8,128)(2,1)S(1)} %slice.28), channel_id=1, source_target_pairs={{0,8},{4,12},{8,0},{12,4},{16,24},{20,28},{24,16},{28,20},{1,9},{5... | collective-permute-start | bytes 393224 | tf_op jit(solution)/shard_map/ppermute | solution.py:287
  44.4 3.5 %collective-permute-done.16.refs_6_.refs_16_ = bf16[16,32,256]{2,1,0:T(8,128)(2,1)S(1)} collective-permute-done((bf16[16,32,256]{2,1,0:T(8,128)(2,1)S(1)}, bf16[16,32,256]{2,1,0:T(8,128)(2,1)S(1)}, u32[]{:S(2)}, u32[]{:S(2)}) %collective-permute-start.16) | collective-permute-done | bytes 262176 | tf_op jit(solution)/shard_map/ppermute | solution.py:287
  47.9 1.9 %collective-permute-start.14 = (bf16[8,32,256]{2,1,0:T(8,128)(2,1)S(1)}, bf16[8,32,256]{2,1,0:T(8,128)(2,1)S(1)}, u32[]{:S(2)}, u32[]{:S(2)}) collective-permute-start(bf16[8,32,256]{2,1,0:T(8,128)(2,1)S(1)} %slice.26), channel_id=1, source_target_pairs={{0,16},{4,20},{8,24},{12,28},{16,0},{20,4},{24,8},{28,12},{1,17},{... | collective-permute-start | bytes 393224 | tf_op jit(solution)/shard_map/ppermute | solution.py:287
  49.9 0.8 %collective-permute-start.20 = (bf16[8,32,256]{2,1,0:T(8,128)(2,1)S(1)}, bf16[8,32,256]{2,1,0:T(8,128)(2,1)S(1)}, u32[]{:S(2)}, u32[]{:S(2)}) collective-permute-start(bf16[8,32,256]{2,1,0:T(8,128)(2,1)S(1)} %slice.29), channel_id=1, source_target_pairs={{0,8},{4,12},{8,0},{12,4},{16,24},{20,28},{24,16},{28,20},{1,9},{5... | collective-permute-start | bytes 393224 | tf_op jit(solution)/shard_map/ppermute | solution.py:287
  50.6 0.6 collective-permute-start.17
  51.2 0.6 pick.4
  51.9 0.6 pick.5
  52.6 0.6 collective-permute-start.11
  53.1 1.8 %collective-permute-done.20.refs_7_.refs_18_ = bf16[8,32,256]{2,1,0:T(8,128)(2,1)S(1)} collective-permute-done((bf16[8,32,256]{2,1,0:T(8,128)(2,1)S(1)}, bf16[8,32,256]{2,1,0:T(8,128)(2,1)S(1)}, u32[]{:S(2)}, u32[]{:S(2)}) %collective-permute-start.20) | collective-permute-done | bytes 131104 | tf_op jit(solution)/shard_map/ppermute | solution.py:287
  54.9 0.6 pick.7
  55.7 0.6 pick.6
  56.8 1.0 %left_side.1.left_ref = bf16[8,512,256]{2,1,0:T(8,128)(2,1)S(1)} custom-call(bf16[16,32,256]{2,1,0:T(8,128)(2,1)S(1)} %get-tuple-element.13.refs_0_, bf16[16,32,256]{2,1,0:T(8,128)(2,1)S(1)} %collective-permute-done.refs_1_.refs_0_, bf16[16,32,256]{2,1,0:T(8,128)(2,1)S(1)} %collective-permute-done.1.refs_2_.refs_0_, ...), custom_call_target="tpu_custom_call" | custom-call | tf_op jit(solution)/shard_map/left_side/pallas_call | solution.py:190
  57.8 0.5 collective-permute-done.18.refs_2_
  58.3 4.4 %cross_spectra.1 = f32[2,8,2,256,256]{4,3,2,1,0:T(8,128)} custom-call(s32[2]{0:T(128)S(1)} %broadcast_xor_fusion.1.far_ref, bf16[8,512,256]{2,1,0:T(8,128)(2,1)S(1)} %left_side.1.left_ref, bf16[2,16,32,256]{3,2,1,0:T(8,128)(2,1)S(1)} %collective-permute-done.6.refs_0_, bf16[2,16,32,256]{3,2,1,0:T(8,128)(2,1)S(1)} %collective-permute-done.11.refs_1_, ...), custom_call_target="tpu_custom_call" | custom-call | flops 1073741824 | bytes 8388608 | tf_op jit(solution)/shard_map/cross_spectra/pallas_call | solution.py:261
  (37 shorter events, 2.5 us)
Async XLA Ops:
  0.0 33.4 %copy-start.1 = (s32[8]{0:T(128)S(1)}, s32[8]{0:T(128)}, u32[]{:S(2)}) copy-start(s32[8]{0:T(128)} %param.5) | copy-start | bytes 100
  0.0 33.6 %copy-start = (s32[2,8]{1,0:T(2,128)S(1)}, s32[2,8]{1,0:T(2,128)}, u32[]{:S(2)}) copy-start(s32[2,8]{1,0:T(2,128)} %param.4) | copy-start | bytes 196
  8.2 11.6 %collective-permute-start = (bf16[16,32,256]{2,1,0:T(8,128)(2,1)S(1)}, bf16[16,32,256]{2,1,0:T(8,128)(2,1)S(1)}, u32[]{:S(2)}, u32[]{:S(2)}) collective-permute-start(bf16[16,32,256]{2,1,0:T(8,128)(2,1)S(1)} %get-tuple-element.14), channel_id=1, source_target_pairs={{0,1},{1,0},{2,3},{3,2},{4,5},{5,4},{6,7},{7,6},{8,9},{9,8},{10,11... | collective-permute-start | bytes 786440 | tf_op jit(solution)/shard_map/ppermute | solution.py:287
  11.3 8.5 %collective-permute-start.4 = (bf16[16,32,256]{2,1,0:T(8,128)(2,1)S(1)}, bf16[16,32,256]{2,1,0:T(8,128)(2,1)S(1)}, u32[]{:S(2)}, u32[]{:S(2)}) collective-permute-start(bf16[16,32,256]{2,1,0:T(8,128)(2,1)S(1)} %get-tuple-element.13.refs_0_), channel_id=1, source_target_pairs={{0,16},{4,20},{8,24},{12,28},{16,0},{20,4},{24,8},{28,12},{1,17},{... | collective-permute-start | bytes 786440 | tf_op jit(solution)/shard_map/ppermute | solution.py:287
  12.8 9.2 %collective-permute-start.3 = (bf16[16,32,256]{2,1,0:T(8,128)(2,1)S(1)}, bf16[16,32,256]{2,1,0:T(8,128)(2,1)S(1)}, u32[]{:S(2)}, u32[]{:S(2)}) collective-permute-start(bf16[16,32,256]{2,1,0:T(8,128)(2,1)S(1)} %get-tuple-element.13.refs_0_), channel_id=1, source_target_pairs={{0,8},{4,12},{8,0},{12,4},{16,24},{20,28},{24,16},{28,20},{1,9},{5... | collective-permute-start | bytes 786440 | tf_op jit(solution)/shard_map/ppermute | solution.py:287
  14.3 17.6 %collective-permute-start.5 = (bf16[16,32,256]{2,1,0:T(8,128)(2,1)S(1)}, bf16[16,32,256]{2,1,0:T(8,128)(2,1)S(1)}, u32[]{:S(2)}, u32[]{:S(2)}) collective-permute-start(bf16[16,32,256]{2,1,0:T(8,128)(2,1)S(1)} %get-tuple-element.13.refs_0_), channel_id=1, source_target_pairs={{0,24},{4,28},{8,16},{12,20},{16,8},{20,12},{24,0},{28,4},{1,25},{... | collective-permute-start | bytes 786440 | tf_op jit(solution)/shard_map/ppermute | solution.py:287
  14.8 13.5 %collective-permute-start.1 = (bf16[16,32,256]{2,1,0:T(8,128)(2,1)S(1)}, bf16[16,32,256]{2,1,0:T(8,128)(2,1)S(1)}, u32[]{:S(2)}, u32[]{:S(2)}) collective-permute-start(bf16[16,32,256]{2,1,0:T(8,128)(2,1)S(1)} %get-tuple-element.15), channel_id=1, source_target_pairs={{0,2},{1,3},{2,0},{3,1},{4,6},{5,7},{6,4},{7,5},{8,10},{9,11},{10,... | collective-permute-start | bytes 786440 | tf_op jit(solution)/shard_map/ppermute | solution.py:287
  22.0 9.8 %collective-permute-start.8 = (bf16[16,32,256]{2,1,0:T(8,128)(2,1)S(1)}, bf16[16,32,256]{2,1,0:T(8,128)(2,1)S(1)}, u32[]{:S(2)}, u32[]{:S(2)}) collective-permute-start(bf16[16,32,256]{2,1,0:T(8,128)(2,1)S(1)} %collective-permute-done.refs_1_.refs_0_), channel_id=1, source_target_pairs={{0,16},{4,20},{8,24},{12,28},{16,0},{20,4},{24,8},{28,12},{1,17},{... | collective-permute-start | bytes 786440 | tf_op jit(solution)/shard_map/ppermute | solution.py:287
  22.5 9.3 %collective-permute-start.7 = (bf16[16,32,256]{2,1,0:T(8,128)(2,1)S(1)}, bf16[16,32,256]{2,1,0:T(8,128)(2,1)S(1)}, u32[]{:S(2)}, u32[]{:S(2)}) collective-permute-start(bf16[16,32,256]{2,1,0:T(8,128)(2,1)S(1)} %collective-permute-done.refs_1_.refs_0_), channel_id=1, source_target_pairs={{0,8},{4,12},{8,0},{12,4},{16,24},{20,28},{24,16},{28,20},{1,9},{5... | collective-permute-start | bytes 786440 | tf_op jit(solution)/shard_map/ppermute | solution.py:287
  28.2 8.3 %collective-permute-start.2 = (bf16[16,32,256]{2,1,0:T(8,128)(2,1)S(1)}, bf16[16,32,256]{2,1,0:T(8,128)(2,1)S(1)}, u32[]{:S(2)}, u32[]{:S(2)}) collective-permute-start(bf16[16,32,256]{2,1,0:T(8,128)(2,1)S(1)} %get-tuple-element.17), channel_id=1, source_target_pairs={{0,3},{1,2},{2,1},{3,0},{4,7},{5,6},{6,5},{7,4},{8,11},{9,10},{10,... | collective-permute-start | bytes 786440 | tf_op jit(solution)/shard_map/ppermute | solution.py:287
  31.8 6.4 %collective-permute-start.12 = (bf16[16,32,256]{2,1,0:T(8,128)(2,1)S(1)}, bf16[16,32,256]{2,1,0:T(8,128)(2,1)S(1)}, u32[]{:S(2)}, u32[]{:S(2)}) collective-permute-start(bf16[16,32,256]{2,1,0:T(8,128)(2,1)S(1)} %collective-permute-done.1.refs_2_.refs_0_), channel_id=1, source_target_pairs={{0,8},{4,12},{8,0},{12,4},{16,24},{20,28},{24,16},{28,20},{1,9},{5... | collective-permute-start | bytes 786440 | tf_op jit(solution)/shard_map/ppermute | solution.py:287
  33.7 9.1 %collective-permute-start.13 = (bf16[16,32,256]{2,1,0:T(8,128)(2,1)S(1)}, bf16[16,32,256]{2,1,0:T(8,128)(2,1)S(1)}, u32[]{:S(2)}, u32[]{:S(2)}) collective-permute-start(bf16[16,32,256]{2,1,0:T(8,128)(2,1)S(1)} %collective-permute-done.1.refs_2_.refs_0_), channel_id=1, source_target_pairs={{0,16},{4,20},{8,24},{12,28},{16,0},{20,4},{24,8},{28,12},{1,17},{... | collective-permute-start | bytes 786440 | tf_op jit(solution)/shard_map/ppermute | solution.py:287
  38.3 9.6 %collective-permute-start.16 = (bf16[16,32,256]{2,1,0:T(8,128)(2,1)S(1)}, bf16[16,32,256]{2,1,0:T(8,128)(2,1)S(1)}, u32[]{:S(2)}, u32[]{:S(2)}) collective-permute-start(bf16[16,32,256]{2,1,0:T(8,128)(2,1)S(1)} %collective-permute-done.2.refs_3_.refs_4_), channel_id=1, source_target_pairs={{0,16},{4,20},{8,24},{12,28},{16,0},{20,4},{24,8},{28,12},{1,17},{... | collective-permute-start | bytes 786440 | tf_op jit(solution)/shard_map/ppermute | solution.py:287
  39.8 10.1 %collective-permute-start.15 = (bf16[16,32,256]{2,1,0:T(8,128)(2,1)S(1)}, bf16[16,32,256]{2,1,0:T(8,128)(2,1)S(1)}, u32[]{:S(2)}, u32[]{:S(2)}) collective-permute-start(bf16[16,32,256]{2,1,0:T(8,128)(2,1)S(1)} %collective-permute-done.2.refs_3_.refs_4_), channel_id=1, source_target_pairs={{0,8},{4,12},{8,0},{12,4},{16,24},{20,28},{24,16},{28,20},{1,9},{5... | collective-permute-start | bytes 786440 | tf_op jit(solution)/shard_map/ppermute | solution.py:287
  41.5 9.1 %collective-permute-start.10 = (bf16[8,32,256]{2,1,0:T(8,128)(2,1)S(1)}, bf16[8,32,256]{2,1,0:T(8,128)(2,1)S(1)}, u32[]{:S(2)}, u32[]{:S(2)}) collective-permute-start(bf16[8,32,256]{2,1,0:T(8,128)(2,1)S(1)} %slice.25), channel_id=1, source_target_pairs={{0,8},{4,12},{8,0},{12,4},{16,24},{20,28},{24,16},{28,20},{1,9},{5... | collective-permute-start | bytes 393224 | tf_op jit(solution)/shard_map/ppermute | solution.py:287
  42.3 9.6 %collective-permute-start.9 = (bf16[8,32,256]{2,1,0:T(8,128)(2,1)S(1)}, bf16[8,32,256]{2,1,0:T(8,128)(2,1)S(1)}, u32[]{:S(2)}, u32[]{:S(2)}) collective-permute-start(bf16[8,32,256]{2,1,0:T(8,128)(2,1)S(1)} %slice.24), channel_id=1, source_target_pairs={{0,16},{4,20},{8,24},{12,28},{16,0},{20,4},{24,8},{28,12},{1,17},{... | collective-permute-start | bytes 393224 | tf_op jit(solution)/shard_map/ppermute | solution.py:287
  42.9 9.7 %collective-permute-start.19 = (bf16[8,32,256]{2,1,0:T(8,128)(2,1)S(1)}, bf16[8,32,256]{2,1,0:T(8,128)(2,1)S(1)}, u32[]{:S(2)}, u32[]{:S(2)}) collective-permute-start(bf16[8,32,256]{2,1,0:T(8,128)(2,1)S(1)} %slice.28), channel_id=1, source_target_pairs={{0,8},{4,12},{8,0},{12,4},{16,24},{20,28},{24,16},{28,20},{1,9},{5... | collective-permute-start | bytes 393224 | tf_op jit(solution)/shard_map/ppermute | solution.py:287
  47.9 7.7 %collective-permute-start.14 = (bf16[8,32,256]{2,1,0:T(8,128)(2,1)S(1)}, bf16[8,32,256]{2,1,0:T(8,128)(2,1)S(1)}, u32[]{:S(2)}, u32[]{:S(2)}) collective-permute-start(bf16[8,32,256]{2,1,0:T(8,128)(2,1)S(1)} %slice.26), channel_id=1, source_target_pairs={{0,16},{4,20},{8,24},{12,28},{16,0},{20,4},{24,8},{28,12},{1,17},{... | collective-permute-start | bytes 393224 | tf_op jit(solution)/shard_map/ppermute | solution.py:287
  49.9 5.0 %collective-permute-start.20 = (bf16[8,32,256]{2,1,0:T(8,128)(2,1)S(1)}, bf16[8,32,256]{2,1,0:T(8,128)(2,1)S(1)}, u32[]{:S(2)}, u32[]{:S(2)}) collective-permute-start(bf16[8,32,256]{2,1,0:T(8,128)(2,1)S(1)} %slice.29), channel_id=1, source_target_pairs={{0,8},{4,12},{8,0},{12,4},{16,24},{20,28},{24,16},{28,20},{1,9},{5... | collective-permute-start | bytes 393224 | tf_op jit(solution)/shard_map/ppermute | solution.py:287
  50.6 5.0 %collective-permute-start.17 = (bf16[8,32,256]{2,1,0:T(8,128)(2,1)S(1)}, bf16[8,32,256]{2,1,0:T(8,128)(2,1)S(1)}, u32[]{:S(2)}, u32[]{:S(2)}) collective-permute-start(bf16[8,32,256]{2,1,0:T(8,128)(2,1)S(1)} %slice.27), channel_id=1, source_target_pairs={{0,16},{4,20},{8,24},{12,28},{16,0},{20,4},{24,8},{28,12},{1,17},{... | collective-permute-start | bytes 393224 | tf_op jit(solution)/shard_map/ppermute | solution.py:287
  51.9 5.9 %collective-permute-start.6 = (bf16[2,16,32,256]{3,2,1,0:T(8,128)(2,1)S(1)}, bf16[2,16,32,256]{3,2,1,0:T(8,128)(2,1)S(1)}, u32[]{:S(2)}, u32[]{:S(2)}) collective-permute-start(bf16[2,16,32,256]{3,2,1,0:T(8,128)(2,1)S(1)} %pick.4), channel_id=1, source_target_pairs={{0,4},{4,0},{8,12},{12,8},{16,20},{20,16},{24,28},{28,24},{1,5},{5... | collective-permute-start | bytes 1572872 | tf_op jit(solution)/shard_map/ppermute | solution.py:287
  52.6 5.2 %collective-permute-start.11 = (bf16[2,16,32,256]{3,2,1,0:T(8,128)(2,1)S(1)}, bf16[2,16,32,256]{3,2,1,0:T(8,128)(2,1)S(1)}, u32[]{:S(2)}, u32[]{:S(2)}) collective-permute-start(bf16[2,16,32,256]{3,2,1,0:T(8,128)(2,1)S(1)} %pick.5), channel_id=1, source_target_pairs={{0,4},{4,0},{8,12},{12,8},{16,20},{20,16},{24,28},{28,24},{1,5},{5... | collective-permute-start | bytes 1572872 | tf_op jit(solution)/shard_map/ppermute | solution.py:287
  55.5 2.3 %collective-permute-start.21 = (bf16[2,16,32,256]{3,2,1,0:T(8,128)(2,1)S(1)}, bf16[2,16,32,256]{3,2,1,0:T(8,128)(2,1)S(1)}, u32[]{:S(2)}, u32[]{:S(2)}) collective-permute-start(bf16[2,16,32,256]{3,2,1,0:T(8,128)(2,1)S(1)} %pick.7), channel_id=1, source_target_pairs={{0,4},{4,0},{8,12},{12,8},{16,20},{20,16},{24,28},{28,24},{1,5},{5... | collective-permute-start | bytes 1572872 | tf_op jit(solution)/shard_map/ppermute | solution.py:287
  56.3 2.0 %collective-permute-start.18 = (bf16[2,16,32,256]{3,2,1,0:T(8,128)(2,1)S(1)}, bf16[2,16,32,256]{3,2,1,0:T(8,128)(2,1)S(1)}, u32[]{:S(2)}, u32[]{:S(2)}) collective-permute-start(bf16[2,16,32,256]{3,2,1,0:T(8,128)(2,1)S(1)} %pick.6), channel_id=1, source_target_pairs={{0,4},{4,0},{8,12},{12,8},{16,20},{20,16},{24,28},{28,24},{1,5},{5... | collective-permute-start | bytes 1572872 | tf_op jit(solution)/shard_map/ppermute | solution.py:287
